TPU v7x, 32 devices: a whole 2x2x4 slice. The times are simulated.
32 devices in a mesh: row: 4 (over z), col: 8 (over y, x, core).
Axes of the slice: x: 2, y: 2, z: 4, core: 2. Of those that a mesh axis runs over, the one named last changes fastest.
Arguments:
- start_basis: float32 [4096, 128], P(('row', 'col'))
- tile_values: bfloat16 [4, 8, 16, 128, 128], P('row', 'col')
- tile_coords: int32 [4, 8, 2, 16], P('row', 'col'), may hold values from 0 to 7, as said below
- tile_count: int32 [4, 8], P('row', 'col'), may hold values from 1 to 16, as said below
Outputs:
- basis: float32 [4096, 128], P(('row', 'col'))
- residual: float32 [4096, 128], P(('row', 'col'))
Inputs may be any that keep to these rules, and one draw needn't show every extreme that they name: `tile_coords`: on grid position (r, c), slot s < tile_count[r, c] is a tile; local block rows run below 4 and local block columns below 8; slot 0 holds the diagonal tile, local block row r and local block column c; places may repeat, and slots past the count hold arbitrary places. `tile_count`: some device holds 16 tiles and some only its 1 diagonal ones.
All inputs are finite; a program needn't handle non-finite values.
Results may differ from a plain program's by a relative error of at most 0.0021.
The roundings to bfloat16 on the way count: a program that leaves them out, or rounds other values in their place, can miss the bound.
Values may be sent and summed in bfloat16 or wider, within the bound.
No kernel may reach another device: no remote copies, remote signals or barrier semaphores. Data moves between devices by JAX's collectives and lax.ppermute only.
A program may use at most 64 MiB of HBM per device.

v0:
```python
import jax
import jax.numpy as jnp
from jax import lax
from jax.sharding import PartitionSpec as P

ITERS = 3


EPSILON = 1e-06
STEP_SIZE = 0.5
MOMENTUM = 0.5


def local_moments(left_side, right_side, items_total):
    return (
        jnp.dot(
            left_side.T,
            right_side,
            preferred_element_type=jnp.float32,
            precision=lax.Precision.HIGHEST,
        )
        / items_total
    )


def inverse_root(gram_matrix):
    factor = jnp.linalg.cholesky(gram_matrix)
    identity = jnp.eye(gram_matrix.shape[0], dtype=jnp.float32)
    inverse = lax.linalg.triangular_solve(factor, identity, left_side=True, lower=True)
    return inverse.T


def update_block(current, applied, previous, rayleigh, coupling):
    residual = applied - jnp.dot(current, rayleigh, precision=lax.Precision.HIGHEST)
    direction = residual + MOMENTUM * (
        previous - jnp.dot(current, coupling, precision=lax.Precision.HIGHEST)
    )
    moved = current + STEP_SIZE * direction
    return (residual, direction, moved)


def per_device(start_basis, tile_values, tile_coords, tile_count):
    highest = lax.Precision.HIGHEST
    rows_here, columns = start_basis.shape
    tile_blocks = tile_values[0, 0]
    slot_count, tile_edge = (tile_blocks.shape[0], tile_blocks.shape[1])
    tile_rows = tile_coords[0, 0, 0]
    tile_cols = tile_coords[0, 0, 1]
    tile_total = tile_count[0, 0]
    row_blocks = lax.axis_size("row") * (rows_here // tile_edge)
    col_blocks = lax.axis_size("col") * (rows_here // tile_edge)
    items_total = float(rows_here * lax.axis_size("row") * lax.axis_size("col"))
    live_slots = (jnp.arange(slot_count, dtype=jnp.int32) < tile_total).astype(jnp.float32)
    row_pick = (tile_rows[None, :] == jnp.arange(row_blocks, dtype=jnp.int32)[:, None]).astype(
        jnp.float32
    ) * live_slots[None, :]
    col_pick = (tile_cols[None, :] == jnp.arange(col_blocks, dtype=jnp.int32)[:, None]).astype(
        jnp.float32
    ) * live_slots[None, :]
    row_terms = jnp.einsum(
        "sab,sab->sa", tile_blocks, tile_blocks, preferred_element_type=jnp.float32
    )
    col_terms = jnp.einsum(
        "sab,sab->sb", tile_blocks, tile_blocks, preferred_element_type=jnp.float32
    )
    row_energy = lax.psum_scatter(
        jnp.dot(row_pick, row_terms, precision=highest).reshape(-1),
        "row",
        scatter_dimension=0,
        tiled=True,
    )
    col_energy = lax.psum_scatter(
        jnp.dot(col_pick, col_terms, precision=highest).reshape(-1),
        "col",
        scatter_dimension=0,
        tiled=True,
    )
    row_scale = (row_energy + EPSILON) ** (-0.25)
    col_scale = (col_energy + EPSILON) ** (-0.25)
    start_gram = lax.psum(local_moments(start_basis, start_basis, items_total), ("row", "col"))
    current = jnp.dot(start_basis, inverse_root(start_gram), precision=highest)
    previous = jnp.zeros_like(start_basis)
    residual = previous
    for iteration in range(ITERS):
        scaled = (col_scale[:, None] * current).astype(jnp.bfloat16)
        panels = lax.all_gather(scaled, "col", axis=0, tiled=True).reshape(
            col_blocks, tile_edge, columns
        )
        products = jnp.einsum(
            "sab,sbk->sak", tile_blocks, panels[tile_cols], preferred_element_type=jnp.float32
        )
        partial_value = jnp.dot(row_pick, products.reshape(slot_count, -1), precision=highest)
        summed = lax.psum_scatter(
            partial_value.reshape(row_blocks * tile_edge, columns),
            "row",
            scatter_dimension=0,
            tiled=True,
        )
        applied = row_scale[:, None] * summed
        rayleigh, coupling = lax.psum(
            (
                local_moments(current, applied, items_total),
                local_moments(current, previous, items_total),
            ),
            ("row", "col"),
        )
        residual, direction, moved = update_block(current, applied, previous, rayleigh, coupling)
        gram_matrix = lax.psum(local_moments(moved, moved, items_total), ("row", "col"))
        current = jnp.dot(moved, inverse_root(gram_matrix), precision=highest)
        previous = direction
    return (current, residual)


def solution(mesh):
    return jax.shard_map(
        per_device,
        mesh=mesh,
        in_specs=(
            P(("row", "col"), None),
            P("row", "col", None, None, None),
            P("row", "col", None, None),
            P("row", "col"),
        ),
        out_specs=(P(("row", "col"), None), P(("row", "col"), None)),
        check_vma=False,
    )
```

profile of v0, /device:TPU:0, one launch (start us, length us, event | category | flops | bytes accessed | tf_op | source)
XLA Modules:
  0.0 1093.1 jit_solution(6166007009720697651)
XLA Ops:
  11.7 15.1 %all-reduce.1 = f32[1024]{0:T(1024)S(1)} all-reduce(f32[1024]{0:T(1024)S(1)} %convolution_bitcast_fusion.3), channel_id=3, replica_groups=mesh['row'=4,'col'=8] {'col'}, use_global_device_ids=true, to_apply=%region_4.7.clone | all-reduce | flops 1024 | bytes 8192
  28.8 105.7 %all-reduce.13.cloned.1.call-done = f32[128,128]{0,1:T(8,128)} async-done(((f32[128,128]{0,1:T(8,128)}), f32[128,128]{0,1:T(8,128)}) %all-reduce.13.cloned.1.call-update) | async-done | bytes 65552 | tf_op jit(solution)/shard_map/psum | solution.py:80
  135.5 11.7 %cholesky.74 = f32[128,128]{1,0:T(8,128)S(1)} custom-call(f32[128,128]{1,0:T(8,128)S(1)} %fusion.42), custom_call_target="Cholesky" | custom-call | tf_op jit(solution)/shard_map/jit(cholesky)/cholesky | solution.py:27
  148.5 9.8 custom-call.8
  158.9 9.6 all_gather.9
  174.8 11.1 %all-reduce = f32[512]{0:T(512)S(1)} all-reduce(f32[512]{0:T(512)S(1)} %convolution_bitcast_fusion.4), channel_id=2, replica_groups=mesh['row'=4,'col'=8] {'row'}, use_global_device_ids=true, to_apply=%region_3.6.clone | all-reduce | flops 512 | bytes 4096
  186.9 5.2 reduce-scatter.4.cloned.1.call-done
  192.1 1.7 convolution_multiply_fusion.8
  193.9 126.5 %all-reduce.25.cloned.1.call-done = (f32[128,128]{0,1:T(8,128)}, f32[128,128]{0,1:T(8,128)}) async-done(((f32[128,128]{0,1:T(8,128)}, f32[128,128]{0,1:T(8,128)}), (f32[128,128]{0,1:T(8,128)}, f32[128,128]{0,1:T(8,128)})) %all-reduce.25.cloned.1.call-update) | async-done | bytes 131088 | tf_op jit(solution)/shard_map/psum | solution.py:100
  322.9 121.0 %all-reduce.15.cloned.1.call-done = f32[128,128]{0,1:T(8,128)} async-done(((f32[128,128]{0,1:T(8,128)}), f32[128,128]{0,1:T(8,128)}) %all-reduce.15.cloned.1.call-update) | async-done | bytes 65552 | tf_op jit(solution)/shard_map/psum | solution.py:108
  444.9 11.7 %cholesky.85 = f32[128,128]{1,0:T(8,128)S(1)} custom-call(f32[128,128]{1,0:T(8,128)S(1)} %fusion.39), custom_call_target="Cholesky" | custom-call | tf_op jit(solution)/shard_map/jit(cholesky)/cholesky | solution.py:27
  458.0 9.8 custom-call.9
  468.5 9.6 all_gather.10
  482.9 18.3 %reduce-scatter.6.cloned.1.call-done = f32[128,128]{0,1:T(8,128)} async-done(((f32[512,128]{0,1:T(8,128)}), f32[128,128]{0,1:T(8,128)}) %reduce-scatter.6.cloned.1.call-update) | async-done | bytes 65552 | tf_op jit(solution)/shard_map/reduce_scatter | solution.py:93
  503.0 125.6 %all-reduce.23.cloned.1.call-done = (f32[128,128]{0,1:T(8,128)}, f32[128,128]{0,1:T(8,128)}) async-done(((f32[128,128]{0,1:T(8,128)}, f32[128,128]{0,1:T(8,128)}), (f32[128,128]{0,1:T(8,128)}, f32[128,128]{0,1:T(8,128)})) %all-reduce.23.cloned.1.call-update) | async-done | bytes 131088 | tf_op jit(solution)/shard_map/psum | solution.py:100
  631.2 120.2 %all-reduce.17.cloned.1.call-done = f32[128,128]{0,1:T(8,128)} async-done(((f32[128,128]{0,1:T(8,128)}), f32[128,128]{0,1:T(8,128)}) %all-reduce.17.cloned.1.call-update) | async-done | bytes 65552 | tf_op jit(solution)/shard_map/psum | solution.py:108
  752.4 11.7 %cholesky.96 = f32[128,128]{1,0:T(8,128)S(1)} custom-call(f32[128,128]{1,0:T(8,128)S(1)} %fusion.37), custom_call_target="Cholesky" | custom-call | tf_op jit(solution)/shard_map/jit(cholesky)/cholesky | solution.py:27
  765.5 9.8 custom-call.10
  776.0 9.6 all_gather.11
  790.4 18.4 %reduce-scatter.8.cloned.1.call-done = f32[128,128]{0,1:T(8,128)} async-done(((f32[512,128]{0,1:T(8,128)}), f32[128,128]{0,1:T(8,128)}) %reduce-scatter.8.cloned.1.call-update) | async-done | bytes 65552 | tf_op jit(solution)/shard_map/reduce_scatter | solution.py:93
  810.8 126.4 %all-reduce.21.cloned.1.call-done = (f32[128,128]{0,1:T(8,128)}, f32[128,128]{0,1:T(8,128)}) async-done(((f32[128,128]{0,1:T(8,128)}, f32[128,128]{0,1:T(8,128)}), (f32[128,128]{0,1:T(8,128)}, f32[128,128]{0,1:T(8,128)})) %all-reduce.21.cloned.1.call-update) | async-done | bytes 131088 | tf_op jit(solution)/shard_map/psum | solution.py:100
  940.3 120.5 %all-reduce.19.cloned.1.call-done = f32[128,128]{0,1:T(8,128)} async-done(((f32[128,128]{0,1:T(8,128)}), f32[128,128]{0,1:T(8,128)}) %all-reduce.19.cloned.1.call-update) | async-done | bytes 65552 | tf_op jit(solution)/shard_map/psum | solution.py:108
  1061.8 11.7 %cholesky.107 = f32[128,128]{1,0:T(8,128)S(1)} custom-call(f32[128,128]{1,0:T(8,128)S(1)} %fusion.35), custom_call_target="Cholesky" | custom-call | tf_op jit(solution)/shard_map/jit(cholesky)/cholesky | solution.py:27
  1074.8 9.8 custom-call.11
  (131 shorter events, 45.5 us)
Async XLA Ops:
  7.2 0.8 copy-start
  7.2 127.3 %all-reduce.13.cloned.1.call-start = ((), (), s32[]{:S(2)}) async-start(), calls=%async_computation.3 | async-start | bytes 131072 | tf_op jit(solution)/shard_map/psum | solution.py:80
  9.0 183.2 %reduce-scatter.4.cloned.1.call-start = ((), (), s32[]{:S(2)}) async-start(), calls=%async_computation.4 | async-start | bytes 327680 | tf_op jit(solution)/shard_map/reduce_scatter | solution.py:93
  9.0 0.7 copy-start.12
  26.8 0.7 copy-start.14
  134.4 1.0 copy-start.2
  168.7 1.0 copy-start.1
  172.8 147.6 %all-reduce.25.cloned.1.call-start = ((), (), s32[]{:S(2)}) async-start(), calls=%async_computation.12 | async-start | bytes 262144 | tf_op jit(solution)/shard_map/psum | solution.py:100
  193.9 126.5 %copy-start.6 = (f32[128,128]{0,1:T(8,128)S(1)}, f32[128,128]{0,1:T(8,128)}, u32[]{:S(2)}) copy-start(f32[128,128]{0,1:T(8,128)} %reduce-scatter.4.cloned.1.call-done) | copy-start | bytes 196612
  193.9 250.0 %all-reduce.15.cloned.1.call-start = ((), (), s32[]{:S(2)}) async-start(), calls=%async_computation.5 | async-start | bytes 131072 | tf_op jit(solution)/shard_map/psum | solution.py:108
  320.4 1.1 copy-start.11
  322.6 178.6 %reduce-scatter.6.cloned.1.call-start = ((), (), s32[]{:S(2)}) async-start(), calls=%async_computation.6 | async-start | bytes 327680 | tf_op jit(solution)/shard_map/reduce_scatter | solution.py:93
  443.9 1.0 copy-start.3
  482.1 146.6 %all-reduce.23.cloned.1.call-start = ((), (), s32[]{:S(2)}) async-start(), calls=%async_computation.11 | async-start | bytes 262144 | tf_op jit(solution)/shard_map/psum | solution.py:100
  502.9 125.7 %copy-start.8 = (f32[128,128]{0,1:T(8,128)S(1)}, f32[128,128]{0,1:T(8,128)}, u32[]{:S(2)}) copy-start(f32[128,128]{0,1:T(8,128)} %reduce-scatter.6.cloned.1.call-done) | copy-start | bytes 196612
  503.0 248.4 %all-reduce.17.cloned.1.call-start = ((), (), s32[]{:S(2)}) async-start(), calls=%async_computation.7 | async-start | bytes 131072 | tf_op jit(solution)/shard_map/psum | solution.py:108
  628.6 1.1 copy-start.9
  631.0 177.9 %reduce-scatter.8.cloned.1.call-start = ((), (), s32[]{:S(2)}) async-start(), calls=%async_computation.8 | async-start | bytes 327680 | tf_op jit(solution)/shard_map/reduce_scatter | solution.py:93
  751.4 1.0 copy-start.4
  789.5 147.7 %all-reduce.21.cloned.1.call-start = ((), (), s32[]{:S(2)}) async-start(), calls=%async_computation.10 | async-start | bytes 262144 | tf_op jit(solution)/shard_map/psum | solution.py:100
  810.5 126.7 %copy-start.7 = (f32[128,128]{0,1:T(8,128)S(1)}, f32[128,128]{0,1:T(8,128)}, u32[]{:S(2)}) copy-start(f32[128,128]{0,1:T(8,128)} %reduce-scatter.8.cloned.1.call-done) | copy-start | bytes 196612
  810.5 250.2 %all-reduce.19.cloned.1.call-start = ((), (), s32[]{:S(2)}) async-start(), calls=%async_computation.9 | async-start | bytes 131072 | tf_op jit(solution)/shard_map/psum | solution.py:108
  937.2 1.1 copy-start.10
  1060.7 1.0 copy-start.5
  (1 other events, 0.7 us)
Sparse Core Ops, SparseCore 0:
  14.2 120.2 all-reduce.12
  172.9 19.1 reduce-scatter.3
  199.4 120.9 all-reduce.24
  327.3 116.5 all-reduce.14
  482.2 19.0 reduce-scatter.5
  507.4 121.1 all-reduce.22
  634.8 116.5 all-reduce.16
  789.6 19.1 reduce-scatter.7
  816.1 121.0 all-reduce.20
  944.1 116.5 all-reduce.18
where the time goes:
time: 1100 us; the launch traced here: 1090 us
  waiting for transfers between devices  888 us (81%)
  other arithmetic  93.2 us (8%)
  blocking collectives  55.1 us (5%)
  matrix products  23.6 us (2%)
  between operations  17 us (2%)
  local copies, waits for them, and re-layouts  15.3 us (1%)
    psum x3, waiting for transfers between devices, per_device(): lax.psum((local_moments(current, applied, items_total), local_moments(cur...  378 us
    psum x3, waiting for transfers between devices, per_device(): lax.psum(local_moments(moved, moved, items_total), ('row', 'col'))  362 us
    psum x1, waiting for transfers between devices, per_device(): lax.psum(local_moments(start_basis, start_basis, items_total), ('row', 'c...  106 us
    another operation x12, other arithmetic, inverse_root(): factor = jnp.linalg.cholesky(gram_matrix)  49.6 us
    reduce_scatter x3, waiting for transfers between devices, per_device(): lax.psum_scatter(partial_value.reshape(row_blocks * tile_edge, columns),...  41.9 us
    another operation x8, other arithmetic, inverse_root(): lax.linalg.triangular_solve(factor, identity, left_side=True, lower=True)  41.9 us
    all_gather x3, blocking collectives, per_device(): lax.all_gather(scaled, 'col', axis=0, tiled=True)  28.9 us
    unnamed x2, blocking collectives  26.2 us
  transfers between devices with their start and end apart: 10, of which 10 were waited for; matrix products, arithmetic and copies ran while one was open for 1% of the time, Pallas kernels for 0%

commit v1 on v0

v1 whole, which is shorter than its diff:
```python
import functools

import jax
import jax.numpy as jnp
from jax import lax
from jax.experimental import pallas as pl
from jax.experimental.pallas import tpu as pltpu
from jax.sharding import PartitionSpec as P

ITERS = 3
EPSILON = 1e-06
STEP_SIZE = 0.5
MOMENTUM = 0.5

SUB = 8
F32 = jnp.float32
BF16 = jnp.bfloat16
HIGHEST = lax.Precision.HIGHEST
VMEM = pl.BlockSpec(memory_space=pltpu.VMEM)
SMEM = pl.BlockSpec(memory_space=pltpu.SMEM)
PARAMS = pltpu.CompilerParams(vmem_limit_bytes=40 * 2**20)


def call(body, outputs, scratch=(), smem=1, inputs=0):
    return pl.pallas_call(
        body,
        out_shape=[jax.ShapeDtypeStruct(shape, dtype) for shape, dtype in outputs],
        in_specs=[SMEM] * smem + [VMEM] * (inputs - smem),
        out_specs=[VMEM] * len(outputs),
        scratch_shapes=list(scratch),
        compiler_params=PARAMS,
    )


def dot(left, right, contract=((1,), (0,)), precision=HIGHEST):
    return lax.dot_general(
        left, right, (contract, ((), ())), precision=precision, preferred_element_type=F32
    )


def swap(value, axis, distance):
    size = lax.axis_size(axis)
    return lax.ppermute(value, axis, [(i, i ^ distance) for i in range(size)])


def gather_pieces(value):
    size = lax.axis_size("col")
    even = [value] + [swap(value, "col", k) for k in range(2, size, 2)]
    odd = [swap(piece, "col", 1) for piece in even]
    return [piece for pair in zip(even, odd) for piece in pair]


def plane_sum(keep, send):
    half = keep + swap(send, "col", 1)
    total = half
    for k in range(2, lax.axis_size("col"), 2):
        total = total + swap(half, "col", k)
    return total, swap(total, "col", 1)


def sub(x, k):
    return jnp.broadcast_to(x[k : k + 1, :], x.shape)


def lane(x, j):
    return jnp.broadcast_to(x[:, j : j + 1], x.shape)


def factor(matrix):
    edge = matrix.shape[0]
    blocks = edge // SUB
    shape = (SUB, edge)
    rows = [matrix[SUB * b : SUB * b + SUB, :] for b in range(blocks)]
    sublane = lax.broadcasted_iota(jnp.int32, shape, 0)
    column = lax.broadcasted_iota(jnp.int32, shape, 1)
    inverse = [jnp.where(column == sublane + SUB * b, 1.0, 0.0).astype(F32) for b in range(blocks)]
    upper_out, inverse_out = [], []
    for b in range(blocks):
        cols = [lane(rows[b], SUB * b + k) for k in range(SUB)]
        factors, pivots, pivot_inv, upper = [], [], [], {}
        for k in range(SUB):
            pivot = sub(cols[k], k)
            pivots.append(pivot)
            pivot_inv.append(1.0 / pivot)
            factors.append(jnp.where(sublane > k, cols[k] * pivot_inv[k], 0.0))
            for j in range(k + 1, SUB):
                upper[k, j] = sub(cols[j], k)
                cols[j] = cols[j] - factors[k] * upper[k, j]
        here, inv_here = rows[b], inverse[b]
        row_bcast, inv_bcast = [], []
        for k in range(SUB):
            row_bcast.append(sub(here, k))
            inv_bcast.append(sub(inv_here, k))
            if k < SUB - 1:
                here = here - factors[k] * row_bcast[k]
                inv_here = inv_here - factors[k] * inv_bcast[k]
        pivot = pivots[SUB - 1]
        for k in range(SUB - 1):
            pivot = jnp.where(sublane == k, pivots[k], pivot)
        root_inv = 1.0 / jnp.sqrt(pivot)
        upper_out.append(jnp.where(column >= sublane + SUB * b, here * root_inv, 0.0))
        inverse_out.append(inv_here * root_inv)
        for p in range(b + 1, blocks):
            terms = [lane(rows[p], SUB * b + k) for k in range(SUB)]
            row_p, inv_p = rows[p], inverse[p]
            for k in range(SUB):
                scale = terms[k] * pivot_inv[k]
                for j in range(k + 1, SUB):
                    terms[j] = terms[j] - scale * upper[k, j]
                row_p = row_p - scale * row_bcast[k]
                inv_p = inv_p - scale * inv_bcast[k]
            rows[p], inverse[p] = row_p, inv_p
    return jnp.concatenate(upper_out, axis=0), jnp.concatenate(inverse_out, axis=0)


def energy_kernel(sizes, places, tiles, start, codes, message, row_sums, col_sums):
    edge, slots, n_row, n_col, row_pad = sizes
    row_sums[...] = jnp.zeros_like(row_sums)
    col_sums[...] = jnp.zeros_like(col_sums)
    ones = jnp.ones((SUB, edge), BF16)

    def visit(s, carry):
        wide = tiles[s].astype(F32)
        square = wide * wide
        high = square.astype(BF16)
        low = (square - high.astype(F32)).astype(BF16)
        by_row = ((1,), (1,))
        by_col = ((1,), (0,))
        fast = lax.Precision.DEFAULT
        u = jnp.minimum(places[s], n_row - 1)
        v = jnp.minimum(places[slots + s], n_col - 1)
        row_sums[u] += dot(ones, high, by_row, fast) + dot(ones, low, by_row, fast)
        col_sums[v] += dot(ones, high, by_col, fast) + dot(ones, low, by_col, fast)
        return carry

    lax.fori_loop(0, places[2 * slots], visit, 0)
    message[0:edge, :] = start[...]
    for v in range(n_col):
        message[edge + v : edge + v + 1, :] = col_sums[v, 0:1, :]
    base = edge + n_col
    for u in range(n_row):
        message[base + u : base + u + 1, :] = row_sums[u, 0:1, :]
    for u in range(n_row, row_pad):
        message[base + u : base + u + 1, :] = row_sums[0, 0:1, :]
    message[base + row_pad :, :] = codes[...]


def start_kernel(sizes, here, *refs):
    edge, n_row, n_col, row_pad = sizes
    pieces, (basis, keep, send, row_scale, half) = refs[:n_row], refs[n_row:]
    rank, core = here[0], here[1] % 2
    gram = jnp.zeros((edge, edge), F32)
    row_energy = jnp.zeros((row_pad, edge), F32)
    part = n_row * n_col // 2
    for k in range(n_row):
        group = rank ^ k
        rows = pieces[k][0:edge, :]
        basis[pl.ds(pl.multiple_of(group * edge, edge), edge), :] = rows
        gram += dot(rows, rows, ((0,), (0,)))
        row_energy += pieces[k][edge + n_col : edge + n_col + row_pad, :]
        half[pl.ds(pl.multiple_of(edge + group * n_col, n_col), n_col), :] = pieces[k][
            edge : edge + n_col, :
        ]
    half[0:edge, :] = gram
    low = jnp.concatenate([half[0 : edge // 2, :], half[edge : edge + part, :]], axis=0)
    high = jnp.concatenate([half[edge // 2 : edge, :], half[edge + part :, :]], axis=0)
    keep[...] = jnp.where(core == 0, low, high)
    send[...] = jnp.where(core == 0, high, low)
    scale = inverse_fourth_root(row_energy)
    for u in range(n_row):
        row_scale[u * edge : (u + 1) * edge, :] = down_rows(scale[u : u + 1, :], edge)


def inverse_fourth_root(energy):
    return 1.0 / jnp.sqrt(jnp.sqrt(energy + EPSILON))


def down_rows(row, edge):
    return jnp.transpose(jnp.broadcast_to(row, (edge, edge)))


def halves(here, mine, other):
    core = here[1] % 2
    own, sibling = mine[...], other[...]
    return jnp.where(core == 0, own, sibling), jnp.where(core == 0, sibling, own)


def first_kernel(sizes, here, mine, other, basis, current, scaled, col_scale, energy):
    edge, n_row, n_col, items = sizes
    low, high = halves(here, mine, other)
    gram = jnp.concatenate([low[: edge // 2], high[: edge // 2]], axis=0) / items
    energy[...] = jnp.concatenate([low[edge // 2 :], high[edge // 2 :]], axis=0)
    for u in range(n_row):
        row = energy[pl.ds(u * n_col + here[1], 1), :]
        col_scale[u * edge : (u + 1) * edge, :] = down_rows(inverse_fourth_root(row), edge)
    _, inverse = factor(gram)
    value = dot(basis[...], inverse, ((1,), (1,)))
    current[...] = value
    scaled[...] = (col_scale[...] * value).astype(BF16)


def apply_kernel(sizes, first, meta, here, tiles, row_scale, current, previous, *refs):
    edge, slots, n_row, n_col, unroll = sizes
    pieces, (value, keep, send, panels, total) = refs[:n_col], refs[n_col:]
    rank, place = here[0], here[1]
    for k in range(n_col):
        panels[place ^ k] = pieces[k][...].reshape(n_row, edge, edge)
    total[...] = jnp.zeros_like(total)
    width = slots + 1
    for k in range(n_row):
        group = rank ^ k
        count = meta[k * width + slots]

        def visit(q, carry, k=k, group=group, count=count):
            for j in range(unroll):
                s = q * unroll + j
                code = meta[k * width + s]
                u = jnp.minimum(code // n_col, n_row - 1)
                v = code % n_col
                product = dot(
                    tiles[group * slots + s],
                    panels[v, group],
                    precision=lax.Precision.DEFAULT,
                )
                total[u] += jnp.where(s < count, product, 0.0)
            return carry

        lax.fori_loop(0, (count + unroll - 1) // unroll, visit, 0)
    applied = row_scale[...] * total[...].reshape(n_row * edge, edge)
    moved = applied if first else applied + MOMENTUM * previous[...]
    value[...] = moved
    cross = dot(current[...], moved, ((0,), (0,)))
    square = dot(moved, moved, ((0,), (0,)))
    core = place % 2
    keep[...] = jnp.where(core == 0, cross, square)
    send[...] = jnp.where(core == 0, square, cross)


def moved_gram(cross, square):
    edge = cross.shape[0]
    shape = (edge, edge)
    row = lax.broadcasted_iota(jnp.int32, shape, 0)
    column = lax.broadcasted_iota(jnp.int32, shape, 1)
    identity = jnp.where(row == column, 1.0, 0.0).astype(F32)
    change = square - dot(cross, cross, ((0,), (0,)))
    return identity + STEP_SIZE * STEP_SIZE * change


def update_kernel(
    items, here, mine, other, current, value, col_scale, new, scaled, direction, coupling
):
    cross, square = halves(here, mine, other)
    cross, square = cross / items, square / items
    step = value[...] - dot(current[...], cross)
    direction[...] = step
    upper, inverse = factor(moved_gram(cross, square))
    coupling[...] = (upper - inverse) / STEP_SIZE
    result = dot(current[...] + STEP_SIZE * step, inverse, ((1,), (1,)))
    new[...] = result
    scaled[...] = (col_scale[...] * result).astype(BF16)


def last_kernel(
    sizes, here, mine, other, current, value, previous, coupling, basis, residual
):
    edge, items = sizes
    cross, square = halves(here, mine, other)
    cross, square = cross / items, square / items
    rows = pl.ds(pl.multiple_of(here[0] * edge, edge), edge)
    old, moved = current[rows, :], value[rows, :]
    rayleigh = cross - MOMENTUM * coupling[...]
    residual[...] = moved - MOMENTUM * previous[rows, :] - dot(old, rayleigh)
    step = moved - dot(old, cross)
    _, inverse = factor(moved_gram(cross, square))
    basis[...] = dot(old + STEP_SIZE * step, inverse, ((1,), (1,)))


def per_device(start_basis, tile_values, tile_coords, tile_count):
    edge, columns = start_basis.shape
    tiles = tile_values[0, 0]
    slots = tiles.shape[0]
    n_row, n_col = lax.axis_size("row"), lax.axis_size("col")
    items = float(edge * n_row * n_col)
    rows = n_row * edge
    row_pad = -(-n_row // SUB) * SUB
    here = jnp.stack([lax.axis_index("row"), lax.axis_index("col")]).astype(jnp.int32)
    block = ((rows, columns), F32)
    square = ((columns, columns), F32)

    all_tiles = lax.all_gather(tiles, "row", axis=0, tiled=True)

    places = jnp.concatenate([tile_coords[0, 0].reshape(-1), tile_count[0]])
    codes = jnp.concatenate([tile_coords[0, 0, 0] * n_col + tile_coords[0, 0, 1], tile_count[0]])
    codes = jnp.pad(codes.astype(F32)[None, :], ((0, SUB - 1), (0, columns - slots - 1)))
    length = edge + n_col + row_pad + SUB
    (message,) = call(
        functools.partial(energy_kernel, (edge, slots, n_row, n_col, row_pad)),
        [((length, columns), F32)],
        [pltpu.VMEM((n_row, SUB, columns), F32), pltpu.VMEM((n_col, SUB, columns), F32)],
        inputs=4,
    )(places, tiles, start_basis, codes)
    messages = [message] + [swap(message, "row", k) for k in range(1, n_row)]
    meta = jnp.concatenate([m[length - SUB, : slots + 1] for m in messages]).astype(jnp.int32)

    part = (edge + n_row * n_col) // 2
    basis, keep, send, row_scale = call(
        functools.partial(start_kernel, (edge, n_row, n_col, row_pad)),
        [block, ((part, columns), F32), ((part, columns), F32), block],
        [pltpu.VMEM((2 * part, columns), F32)],
        inputs=1 + n_row,
    )(here, *messages)
    mine, other = plane_sum(keep, send)
    current, scaled, col_scale = call(
        functools.partial(first_kernel, (edge, n_row, n_col, items)),
        [block, ((rows, columns), BF16), block],
        [pltpu.VMEM((n_row * n_col, columns), F32)],
        inputs=4,
    )(here, mine, other, basis)

    previous, coupling = current, None
    for iteration in range(ITERS):
        pieces = gather_pieces(scaled)
        value, keep, send = call(
            functools.partial(apply_kernel, (edge, slots, n_row, n_col, 4), iteration == 0),
            [block, square, square],
            [
                pltpu.VMEM((n_col, n_row, edge, columns), BF16),
                pltpu.VMEM((n_row, edge, columns), F32),
            ],
            smem=2,
            inputs=6 + n_col,
        )(meta, here, all_tiles, row_scale, current, previous, *pieces)
        mine, other = plane_sum(keep, send)
        if iteration == ITERS - 1:
            break
        current, scaled, previous, coupling = call(
            functools.partial(update_kernel, items),
            [block, ((rows, columns), BF16), block, square],
            inputs=6,
        )(here, mine, other, current, value, col_scale)
    basis, residual = call(
        functools.partial(last_kernel, (edge, items)),
        [((edge, columns), F32), ((edge, columns), F32)],
        inputs=7,
    )(here, mine, other, current, value, previous, coupling)
    return (basis, residual)


def solution(mesh):
    return jax.shard_map(
        per_device,
        mesh=mesh,
        in_specs=(
            P(("row", "col"), None),
            P("row", "col", None, None, None),
            P("row", "col", None, None),
            P("row", "col"),
        ),
        out_specs=(P(("row", "col"), None), P(("row", "col"), None)),
        check_vma=False,
    )
```

time: 1100 us -> 147 us (0.13)
  waiting for transfers between devices: 888 us -> 58.7 us
  other arithmetic: 93.2 us -> 1.16 us
  blocking collectives: 55.1 us -> 0 us
  Pallas kernels: 0 us -> 33.3 us
  starting transfers between devices: 1.05 us -> 33.2 us
  matrix products: 23.6 us -> 0 us
  local copies, waits for them, and re-layouts: 15.3 us -> 4.25 us
    psum x7 -> x0, waiting for transfers between devices: 846 us -> none  [the longest x3 378 us: per_device(): lax.psum((local_moments(current, applied, items_total), local_moments(cur...]
    another operation x20 -> x1, other arithmetic: 91.4 us -> 0.07 us  [per_device(): jnp.stack([lax.axis_index('row'), lax.axis_index('col')]).astype(jnp.int32)]
    ppermute x0 -> x44, waiting for transfers between devices: none -> 55.7 us  [swap(): return lax.ppermute(value, axis, [(i, i ^ distance) for i in range(size)])]
    reduce_scatter x3 -> x0, waiting for transfers between devices: 41.9 us -> none  [per_device(): lax.psum_scatter(partial_value.reshape(row_blocks * tile_edge, columns),...]
    pallas_call x0 -> x9, Pallas kernels: none -> 33.3 us  [the longest x2 11.2 us: per_device(): call(functools.partial(update_kernel, items), [block, ((rows, columns), B...]
    ppermute x0 -> x44, starting transfers between devices: none -> 33.2 us  [swap(): return lax.ppermute(value, axis, [(i, i ^ distance) for i in range(size)])]
    all_gather x3 -> x0, blocking collectives: 28.9 us -> none  [per_device(): lax.all_gather(scaled, 'col', axis=0, tiled=True)]
    unnamed x2 -> x0, blocking collectives: 26.2 us -> none
  transfers between devices with their start and end apart: 10 -> 45, of which waited for: 10 -> 34; matrix products, arithmetic and copies ran while one was open for 1% -> 1% of each run, Pallas kernels for 0% -> 6%
where the time goes in v1:
time: 147 us; the launch traced here: 145 us
  waiting for transfers between devices  58.7 us (40%)
  Pallas kernels  33.3 us (23%)
  starting transfers between devices  33.2 us (23%)
  between operations  14.8 us (10%)
  local copies, waits for them, and re-layouts  4.25 us (3%)
    ppermute x44, waiting for transfers between devices, swap(): return lax.ppermute(value, axis, [(i, i ^ distance) for i in range(size)])  55.7 us
    ppermute x44, starting transfers between devices, swap(): return lax.ppermute(value, axis, [(i, i ^ distance) for i in range(size)])  33.2 us
    pallas_call x2, Pallas kernels, per_device(): call(functools.partial(update_kernel, items), [block, ((rows, columns), B...  11.2 us
    pallas_call x3, Pallas kernels, per_device(): call(functools.partial(apply_kernel, (edge, slots, n_row, n_col, 4), iter...  8.1 us
    pallas_call x1, Pallas kernels, per_device(): call(functools.partial(last_kernel, (edge, items)), [((edge, columns), F3...  5.91 us
    pallas_call x1, Pallas kernels, per_device(): call(functools.partial(first_kernel, (edge, n_row, n_col, items)), [block...  5.06 us
    unnamed x8, local copies, waits for them, and re-layouts  3.47 us
  transfers between devices with their start and end apart: 45, of which 34 were waited for; matrix products, arithmetic and copies ran while one was open for 1% of the time, Pallas kernels for 6%

profile of v1, /device:TPU:0, one launch (start us, length us, event | category | flops | bytes accessed | tf_op | source)
XLA Modules:
  0.0 145.5 jit_solution(5808156786045648198)
XLA Ops:
  12.1 2.1 %shard_map.59.refs_0_ = f32[152,128]{1,0:T(8,128)S(1)} custom-call(s32[33]{0:T(128)S(1)} %pad_add_fusion.1.places, bf16[16,128,128]{2,1,0:T(8,128)(2,1)S(1)} %bitcast.21, f32[128,128]{1,0:T(8,128)S(1)} %copy-done.3, f32[8,128]{1,0:T(8,128)S(1)} %pad.4.codes), custom_call_target="tpu_custom_call" | custom-call | tf_op jit(solution)/shard_map/pallas_call | solution.py:296
  14.2 3.7 %collective-permute-start.2 = (f32[152,128]{1,0:T(8,128)S(1)}, f32[152,128]{1,0:T(8,128)S(1)}, u32[]{:S(2)}, u32[]{:S(2)}) collective-permute-start(f32[152,128]{1,0:T(8,128)S(1)} %shard_map.59.refs_0_), channel_id=1, source_target_pairs={{0,24},{8,16},{16,8},{24,0},{1,25},{9,17},{17,9},{25,1},{2,26},{10... | collective-permute-start | bytes 233480 | tf_op jit(solution)/shard_map/ppermute | solution.py:43
  18.8 2.4 %collective-permute-done.2.refs_3_ = f32[152,128]{1,0:T(8,128)S(1)} collective-permute-done((f32[152,128]{1,0:T(8,128)S(1)}, f32[152,128]{1,0:T(8,128)S(1)}, u32[]{:S(2)}, u32[]{:S(2)}) %collective-permute-start.2) | collective-permute-done | bytes 77856 | tf_op jit(solution)/shard_map/ppermute | solution.py:43
  21.1 11.0 %collective-permute-done.1.refs_2_ = f32[152,128]{1,0:T(8,128)S(1)} collective-permute-done((f32[152,128]{1,0:T(8,128)S(1)}, f32[152,128]{1,0:T(8,128)S(1)}, u32[]{:S(2)}, u32[]{:S(2)}) %collective-permute-start.1) | collective-permute-done | bytes 77856 | tf_op jit(solution)/shard_map/ppermute | solution.py:43
  41.8 5.1 %shard_map.61 = (f32[512,128]{1,0:T(8,128)S(1)}, bf16[512,128]{1,0:T(8,128)(2,1)S(1)}, f32[512,128]{1,0:T(8,128)S(1)}) custom-call(s32[2]{0:T(128)S(1)} %pad_add_fusion.here, f32[80,128]{1,0:T(8,128)S(1)} %add_add_fusion.3.mine, f32[80,128]{1,0:T(8,128)S(1)} %collective-permute-done.7.other, f32[512,128]{1,0:T(8,128)S(1)} %get-tuple-element.28.basis), custom_call_target="tpu_custom_call" | custom-call | tf_op jit(solution)/shard_map/pallas_call | solution.py:313
  46.9 2.9 %collective-permute-start.13 = (bf16[512,128]{1,0:T(8,128)(2,1)S(1)}, bf16[512,128]{1,0:T(8,128)(2,1)S(1)}, u32[]{:S(2)}, u32[]{:S(2)}) collective-permute-start(bf16[512,128]{1,0:T(8,128)(2,1)S(1)} %get-tuple-element.30.refs_0_), channel_id=1, source_target_pairs={{0,6},{1,7},{2,4},{3,5},{4,2},{5,3},{6,0},{7,1},{8,14},{9,15},{10,... | collective-permute-start | bytes 393224 | tf_op jit(solution)/shard_map/ppermute | solution.py:43
  50.4 3.3 %collective-permute-done.13.refs_6_ = bf16[512,128]{1,0:T(8,128)(2,1)S(1)} collective-permute-done((bf16[512,128]{1,0:T(8,128)(2,1)S(1)}, bf16[512,128]{1,0:T(8,128)(2,1)S(1)}, u32[]{:S(2)}, u32[]{:S(2)}) %collective-permute-start.13) | collective-permute-done | bytes 131104 | tf_op jit(solution)/shard_map/ppermute | solution.py:43
  53.7 2.7 %collective-permute-done.11.refs_4_ = bf16[512,128]{1,0:T(8,128)(2,1)S(1)} collective-permute-done((bf16[512,128]{1,0:T(8,128)(2,1)S(1)}, bf16[512,128]{1,0:T(8,128)(2,1)S(1)}, u32[]{:S(2)}, u32[]{:S(2)}) %collective-permute-start.11) | collective-permute-done | bytes 131104 | tf_op jit(solution)/shard_map/ppermute | solution.py:43
  58.0 2.3 %all-gather.3.cloned.1.call-done = bf16[1,1,64,128,128]{4,3,1,0,2:T(8,128)(2,1)} async-done(((bf16[1,1,16,128,128]{4,3,1,0,2:T(8,128)(2,1)}), bf16[1,1,64,128,128]{4,3,1,0,2:T(8,128)(2,1)}) %all-gather.3.cloned.1.call-update) | async-done | bytes 2097168 | tf_op jit(solution)/shard_map/all_gather | solution.py:290
  61.8 2.6 %shard_map.62 = (f32[512,128]{1,0:T(8,128)S(1)}, f32[128,128]{1,0:T(8,128)S(1)}, f32[128,128]{1,0:T(8,128)S(1)}) custom-call(s32[68]{0:T(128)S(1)} %maximum_convert_fusion.meta, s32[2]{0:T(128)S(1)} %pad_add_fusion.here, bf16[64,128,128]{2,1,0:T(8,128)(2,1)S(1)} %bitcast.17, f32[512,128]{1,0:T(8,128)S(1)} %get-tuple-element.25.row_scale, ...), custom_call_target="tpu_custom_call" | custom-call | tf_op jit(solution)/shard_map/pallas_call | solution.py:323
  66.1 2.6 %collective-permute-start.18 = (f32[128,128]{1,0:T(8,128)S(1)}, f32[128,128]{1,0:T(8,128)S(1)}, u32[]{:S(2)}, u32[]{:S(2)}) collective-permute-start(f32[128,128]{1,0:T(8,128)S(1)} %add.65), channel_id=1, source_target_pairs={{0,6},{1,7},{2,4},{3,5},{4,2},{5,3},{6,0},{7,1},{8,14},{9,15},{10,... | collective-permute-start | bytes 196616 | tf_op jit(solution)/shard_map/ppermute | solution.py:43
  69.6 1.8 %collective-permute-done.18 = f32[128,128]{1,0:T(8,128)S(1)} collective-permute-done((f32[128,128]{1,0:T(8,128)S(1)}, f32[128,128]{1,0:T(8,128)S(1)}, u32[]{:S(2)}, u32[]{:S(2)}) %collective-permute-start.18) | collective-permute-done | bytes 65568 | tf_op jit(solution)/shard_map/ppermute | solution.py:43
  74.4 5.7 %shard_map.63 = (f32[512,128]{1,0:T(8,128)S(1)}, bf16[512,128]{1,0:T(8,128)(2,1)S(1)}, f32[512,128]{1,0:T(8,128)S(1)}, f32[128,128]{1,0:T(8,128)}) custom-call(s32[2]{0:T(128)S(1)} %pad_add_fusion.here, f32[128,128]{1,0:T(8,128)S(1)} %add_add_fusion.2.mine, f32[128,128]{1,0:T(8,128)S(1)} %collective-permute-done.19.other, ...), custom_call_target="tpu_custom_call" | custom-call | tf_op jit(solution)/shard_map/pallas_call | solution.py:336
  83.5 3.8 %collective-permute-done.25.refs_6_ = bf16[512,128]{1,0:T(8,128)(2,1)S(1)} collective-permute-done((bf16[512,128]{1,0:T(8,128)(2,1)S(1)}, bf16[512,128]{1,0:T(8,128)(2,1)S(1)}, u32[]{:S(2)}, u32[]{:S(2)}) %collective-permute-start.25) | collective-permute-done | bytes 131104 | tf_op jit(solution)/shard_map/ppermute | solution.py:43
  87.3 2.0 %collective-permute-done.23.refs_4_ = bf16[512,128]{1,0:T(8,128)(2,1)S(1)} collective-permute-done((bf16[512,128]{1,0:T(8,128)(2,1)S(1)}, bf16[512,128]{1,0:T(8,128)(2,1)S(1)}, u32[]{:S(2)}, u32[]{:S(2)}) %collective-permute-start.23) | collective-permute-done | bytes 131104 | tf_op jit(solution)/shard_map/ppermute | solution.py:43
  91.1 2.8 %shard_map.64 = (f32[512,128]{1,0:T(8,128)S(1)}, f32[128,128]{1,0:T(8,128)S(1)}, f32[128,128]{1,0:T(8,128)S(1)}) custom-call(s32[68]{0:T(128)S(1)} %maximum_convert_fusion.meta, s32[2]{0:T(128)S(1)} %pad_add_fusion.here, bf16[64,128,128]{2,1,0:T(8,128)(2,1)S(1)} %bitcast.18, f32[512,128]{1,0:T(8,128)S(1)} %get-tuple-element.25.row_scale, ...), custom_call_target="tpu_custom_call" | custom-call | tf_op jit(solution)/shard_map/pallas_call | solution.py:323
  99.2 1.9 %collective-permute-done.30 = f32[128,128]{1,0:T(8,128)S(1)} collective-permute-done((f32[128,128]{1,0:T(8,128)S(1)}, f32[128,128]{1,0:T(8,128)S(1)}, u32[]{:S(2)}, u32[]{:S(2)}) %collective-permute-start.30) | collective-permute-done | bytes 65568 | tf_op jit(solution)/shard_map/ppermute | solution.py:43
  103.7 5.5 %shard_map.65 = (f32[512,128]{1,0:T(8,128)S(1)}, bf16[512,128]{1,0:T(8,128)(2,1)S(1)}, f32[512,128]{1,0:T(8,128)S(1)}, f32[128,128]{1,0:T(8,128)S(1)}) custom-call(s32[2]{0:T(128)S(1)} %pad_add_fusion.here, f32[128,128]{1,0:T(8,128)S(1)} %add_add_fusion.1.mine, f32[128,128]{1,0:T(8,128)S(1)} %collective-permute-done.31.other, ...), custom_call_target="tpu_custom_call" | custom-call | tf_op jit(solution)/shard_map/pallas_call | solution.py:336
  112.8 3.8 %collective-permute-done.37.refs_6_ = bf16[512,128]{1,0:T(8,128)(2,1)S(1)} collective-permute-done((bf16[512,128]{1,0:T(8,128)(2,1)S(1)}, bf16[512,128]{1,0:T(8,128)(2,1)S(1)}, u32[]{:S(2)}, u32[]{:S(2)}) %collective-permute-start.37) | collective-permute-done | bytes 131104 | tf_op jit(solution)/shard_map/ppermute | solution.py:43
  116.5 2.0 %collective-permute-done.35.refs_4_ = bf16[512,128]{1,0:T(8,128)(2,1)S(1)} collective-permute-done((bf16[512,128]{1,0:T(8,128)(2,1)S(1)}, bf16[512,128]{1,0:T(8,128)(2,1)S(1)}, u32[]{:S(2)}, u32[]{:S(2)}) %collective-permute-start.35) | collective-permute-done | bytes 131104 | tf_op jit(solution)/shard_map/ppermute | solution.py:43
  120.1 2.6 %shard_map.66 = (f32[512,128]{1,0:T(8,128)S(1)}, f32[128,128]{1,0:T(8,128)S(1)}, f32[128,128]{1,0:T(8,128)S(1)}) custom-call(s32[68]{0:T(128)S(1)} %maximum_convert_fusion.meta, s32[2]{0:T(128)S(1)} %pad_add_fusion.here, bf16[64,128,128]{2,1,0:T(8,128)(2,1)S(1)} %bitcast.19, f32[512,128]{1,0:T(8,128)S(1)} %get-tuple-element.25.row_scale, ...), custom_call_target="tpu_custom_call" | custom-call | tf_op jit(solution)/shard_map/pallas_call | solution.py:323
  124.6 1.8 %collective-permute-start.42 = (f32[128,128]{1,0:T(8,128)S(1)}, f32[128,128]{1,0:T(8,128)S(1)}, u32[]{:S(2)}, u32[]{:S(2)}) collective-permute-start(f32[128,128]{1,0:T(8,128)S(1)} %add.73), channel_id=1, source_target_pairs={{0,6},{1,7},{2,4},{3,5},{4,2},{5,3},{6,0},{7,1},{8,14},{9,15},{10,... | collective-permute-start | bytes 196616 | tf_op jit(solution)/shard_map/ppermute | solution.py:43
  128.2 1.9 %collective-permute-done.42 = f32[128,128]{1,0:T(8,128)S(1)} collective-permute-done((f32[128,128]{1,0:T(8,128)S(1)}, f32[128,128]{1,0:T(8,128)S(1)}, u32[]{:S(2)}, u32[]{:S(2)}) %collective-permute-start.42) | collective-permute-done | bytes 65568 | tf_op jit(solution)/shard_map/ppermute | solution.py:43
  132.7 5.9 %shard_map.67 = (f32[128,128]{1,0:T(8,128)}, f32[128,128]{1,0:T(8,128)}) custom-call(s32[2]{0:T(128)S(1)} %pad_add_fusion.here, f32[128,128]{1,0:T(8,128)S(1)} %add_add_fusion.mine, f32[128,128]{1,0:T(8,128)S(1)} %collective-permute-done.43.other, f32[512,128]{1,0:T(8,128)S(1)} %get-tuple-element.41.current, f32[512,128]{1,0:T(8,128)S(1)} %get-tuple-element.46.value, ...), custom_call_target="tpu_custom_call" | custom-call | tf_op jit(solution)/shard_map/pallas_call | solution.py:341
  (103 shorter events, 48.7 us)
Async XLA Ops:
  7.2 53.1 %all-gather.3.cloned.1.call-start = ((), (), s32[]{:S(2)}) async-start(), calls=%async_computation | async-start | bytes 2621440 | tf_op jit(solution)/shard_map/all_gather | solution.py:290
  14.2 6.9 %collective-permute-start.2 = (f32[152,128]{1,0:T(8,128)S(1)}, f32[152,128]{1,0:T(8,128)S(1)}, u32[]{:S(2)}, u32[]{:S(2)}) collective-permute-start(f32[152,128]{1,0:T(8,128)S(1)} %shard_map.59.refs_0_), channel_id=1, source_target_pairs={{0,24},{8,16},{16,8},{24,0},{1,25},{9,17},{17,9},{25,1},{2,26},{10... | collective-permute-start | bytes 233480 | tf_op jit(solution)/shard_map/ppermute | solution.py:43
  18.0 14.2 %collective-permute-start.1 = (f32[152,128]{1,0:T(8,128)S(1)}, f32[152,128]{1,0:T(8,128)S(1)}, u32[]{:S(2)}, u32[]{:S(2)}) collective-permute-start(f32[152,128]{1,0:T(8,128)S(1)} %shard_map.59.refs_0_), channel_id=1, source_target_pairs={{0,16},{8,24},{16,0},{24,8},{1,17},{9,25},{17,1},{25,9},{2,18},{10... | collective-permute-start | bytes 233480 | tf_op jit(solution)/shard_map/ppermute | solution.py:43
  18.4 13.7 %collective-permute-start = (f32[152,128]{1,0:T(8,128)S(1)}, f32[152,128]{1,0:T(8,128)S(1)}, u32[]{:S(2)}, u32[]{:S(2)}) collective-permute-start(f32[152,128]{1,0:T(8,128)S(1)} %shard_map.59.refs_0_), channel_id=1, source_target_pairs={{0,8},{8,0},{16,24},{24,16},{1,9},{9,1},{17,25},{25,17},{2,10},{10... | collective-permute-start | bytes 233480 | tf_op jit(solution)/shard_map/ppermute | solution.py:43
  34.4 4.9 %collective-permute-start.6 = (f32[80,128]{1,0:T(8,128)S(1)}, f32[80,128]{1,0:T(8,128)S(1)}, u32[]{:S(2)}, u32[]{:S(2)}) collective-permute-start(f32[80,128]{1,0:T(8,128)S(1)} %add.61), channel_id=1, source_target_pairs={{0,6},{1,7},{2,4},{3,5},{4,2},{5,3},{6,0},{7,1},{8,14},{9,15},{10,... | collective-permute-start | bytes 122888 | tf_op jit(solution)/shard_map/ppermute | solution.py:43
  35.3 4.4 %collective-permute-start.5 = (f32[80,128]{1,0:T(8,128)S(1)}, f32[80,128]{1,0:T(8,128)S(1)}, u32[]{:S(2)}, u32[]{:S(2)}) collective-permute-start(f32[80,128]{1,0:T(8,128)S(1)} %add.61), channel_id=1, source_target_pairs={{0,4},{1,5},{2,6},{3,7},{4,0},{5,1},{6,2},{7,3},{8,12},{9,13},{10,... | collective-permute-start | bytes 122888 | tf_op jit(solution)/shard_map/ppermute | solution.py:43
  46.9 6.8 %collective-permute-start.13 = (bf16[512,128]{1,0:T(8,128)(2,1)S(1)}, bf16[512,128]{1,0:T(8,128)(2,1)S(1)}, u32[]{:S(2)}, u32[]{:S(2)}) collective-permute-start(bf16[512,128]{1,0:T(8,128)(2,1)S(1)} %get-tuple-element.30.refs_0_), channel_id=1, source_target_pairs={{0,6},{1,7},{2,4},{3,5},{4,2},{5,3},{6,0},{7,1},{8,14},{9,15},{10,... | collective-permute-start | bytes 393224 | tf_op jit(solution)/shard_map/ppermute | solution.py:43
  49.8 6.6 %collective-permute-start.11 = (bf16[512,128]{1,0:T(8,128)(2,1)S(1)}, bf16[512,128]{1,0:T(8,128)(2,1)S(1)}, u32[]{:S(2)}, u32[]{:S(2)}) collective-permute-start(bf16[512,128]{1,0:T(8,128)(2,1)S(1)} %get-tuple-element.30.refs_0_), channel_id=1, source_target_pairs={{0,4},{1,5},{2,6},{3,7},{4,0},{5,1},{6,2},{7,3},{8,12},{9,13},{10,... | collective-permute-start | bytes 393224 | tf_op jit(solution)/shard_map/ppermute | solution.py:43
  49.8 6.8 %collective-permute-start.9 = (bf16[512,128]{1,0:T(8,128)(2,1)S(1)}, bf16[512,128]{1,0:T(8,128)(2,1)S(1)}, u32[]{:S(2)}, u32[]{:S(2)}) collective-permute-start(bf16[512,128]{1,0:T(8,128)(2,1)S(1)} %get-tuple-element.30.refs_0_), channel_id=1, source_target_pairs={{0,2},{1,3},{2,0},{3,1},{4,6},{5,7},{6,4},{7,5},{8,10},{9,11},{10,... | collective-permute-start | bytes 393224 | tf_op jit(solution)/shard_map/ppermute | solution.py:43
  50.4 6.6 %collective-permute-start.8 = (bf16[512,128]{1,0:T(8,128)(2,1)S(1)}, bf16[512,128]{1,0:T(8,128)(2,1)S(1)}, u32[]{:S(2)}, u32[]{:S(2)}) collective-permute-start(bf16[512,128]{1,0:T(8,128)(2,1)S(1)} %get-tuple-element.30.refs_0_), channel_id=1, source_target_pairs={{0,1},{1,0},{2,3},{3,2},{4,5},{5,4},{6,7},{7,6},{8,9},{9,8},{10,11... | collective-permute-start | bytes 393224 | tf_op jit(solution)/shard_map/ppermute | solution.py:43
  66.1 5.3 %collective-permute-start.18 = (f32[128,128]{1,0:T(8,128)S(1)}, f32[128,128]{1,0:T(8,128)S(1)}, u32[]{:S(2)}, u32[]{:S(2)}) collective-permute-start(f32[128,128]{1,0:T(8,128)S(1)} %add.65), channel_id=1, source_target_pairs={{0,6},{1,7},{2,4},{3,5},{4,2},{5,3},{6,0},{7,1},{8,14},{9,15},{10,... | collective-permute-start | bytes 196616 | tf_op jit(solution)/shard_map/ppermute | solution.py:43
  80.0 7.2 %collective-permute-start.25 = (bf16[512,128]{1,0:T(8,128)(2,1)S(1)}, bf16[512,128]{1,0:T(8,128)(2,1)S(1)}, u32[]{:S(2)}, u32[]{:S(2)}) collective-permute-start(bf16[512,128]{1,0:T(8,128)(2,1)S(1)} %get-tuple-element.37.refs_0_), channel_id=1, source_target_pairs={{0,6},{1,7},{2,4},{3,5},{4,2},{5,3},{6,0},{7,1},{8,14},{9,15},{10,... | collective-permute-start | bytes 393224 | tf_op jit(solution)/shard_map/ppermute | solution.py:43
  81.7 7.6 %collective-permute-start.23 = (bf16[512,128]{1,0:T(8,128)(2,1)S(1)}, bf16[512,128]{1,0:T(8,128)(2,1)S(1)}, u32[]{:S(2)}, u32[]{:S(2)}) collective-permute-start(bf16[512,128]{1,0:T(8,128)(2,1)S(1)} %get-tuple-element.37.refs_0_), channel_id=1, source_target_pairs={{0,4},{1,5},{2,6},{3,7},{4,0},{5,1},{6,2},{7,3},{8,12},{9,13},{10,... | collective-permute-start | bytes 393224 | tf_op jit(solution)/shard_map/ppermute | solution.py:43
  82.8 6.9 %collective-permute-start.21 = (bf16[512,128]{1,0:T(8,128)(2,1)S(1)}, bf16[512,128]{1,0:T(8,128)(2,1)S(1)}, u32[]{:S(2)}, u32[]{:S(2)}) collective-permute-start(bf16[512,128]{1,0:T(8,128)(2,1)S(1)} %get-tuple-element.37.refs_0_), channel_id=1, source_target_pairs={{0,2},{1,3},{2,0},{3,1},{4,6},{5,7},{6,4},{7,5},{8,10},{9,11},{10,... | collective-permute-start | bytes 393224 | tf_op jit(solution)/shard_map/ppermute | solution.py:43
  83.5 6.3 %collective-permute-start.20 = (bf16[512,128]{1,0:T(8,128)(2,1)S(1)}, bf16[512,128]{1,0:T(8,128)(2,1)S(1)}, u32[]{:S(2)}, u32[]{:S(2)}) collective-permute-start(bf16[512,128]{1,0:T(8,128)(2,1)S(1)} %get-tuple-element.37.refs_0_), channel_id=1, source_target_pairs={{0,1},{1,0},{2,3},{3,2},{4,5},{5,4},{6,7},{7,6},{8,9},{9,8},{10,11... | collective-permute-start | bytes 393224 | tf_op jit(solution)/shard_map/ppermute | solution.py:43
  95.7 5.4 %collective-permute-start.30 = (f32[128,128]{1,0:T(8,128)S(1)}, f32[128,128]{1,0:T(8,128)S(1)}, u32[]{:S(2)}, u32[]{:S(2)}) collective-permute-start(f32[128,128]{1,0:T(8,128)S(1)} %add.69), channel_id=1, source_target_pairs={{0,6},{1,7},{2,4},{3,5},{4,2},{5,3},{6,0},{7,1},{8,14},{9,15},{10,... | collective-permute-start | bytes 196616 | tf_op jit(solution)/shard_map/ppermute | solution.py:43
  97.3 5.0 %collective-permute-start.29 = (f32[128,128]{1,0:T(8,128)S(1)}, f32[128,128]{1,0:T(8,128)S(1)}, u32[]{:S(2)}, u32[]{:S(2)}) collective-permute-start(f32[128,128]{1,0:T(8,128)S(1)} %add.69), channel_id=1, source_target_pairs={{0,4},{1,5},{2,6},{3,7},{4,0},{5,1},{6,2},{7,3},{8,12},{9,13},{10,... | collective-permute-start | bytes 196616 | tf_op jit(solution)/shard_map/ppermute | solution.py:43
  109.2 7.3 %collective-permute-start.37 = (bf16[512,128]{1,0:T(8,128)(2,1)S(1)}, bf16[512,128]{1,0:T(8,128)(2,1)S(1)}, u32[]{:S(2)}, u32[]{:S(2)}) collective-permute-start(bf16[512,128]{1,0:T(8,128)(2,1)S(1)} %get-tuple-element.43.refs_0_), channel_id=1, source_target_pairs={{0,6},{1,7},{2,4},{3,5},{4,2},{5,3},{6,0},{7,1},{8,14},{9,15},{10,... | collective-permute-start | bytes 393224 | tf_op jit(solution)/shard_map/ppermute | solution.py:43
  111.0 7.6 %collective-permute-start.35 = (bf16[512,128]{1,0:T(8,128)(2,1)S(1)}, bf16[512,128]{1,0:T(8,128)(2,1)S(1)}, u32[]{:S(2)}, u32[]{:S(2)}) collective-permute-start(bf16[512,128]{1,0:T(8,128)(2,1)S(1)} %get-tuple-element.43.refs_0_), channel_id=1, source_target_pairs={{0,4},{1,5},{2,6},{3,7},{4,0},{5,1},{6,2},{7,3},{8,12},{9,13},{10,... | collective-permute-start | bytes 393224 | tf_op jit(solution)/shard_map/ppermute | solution.py:43
  111.9 6.7 %collective-permute-start.33 = (bf16[512,128]{1,0:T(8,128)(2,1)S(1)}, bf16[512,128]{1,0:T(8,128)(2,1)S(1)}, u32[]{:S(2)}, u32[]{:S(2)}) collective-permute-start(bf16[512,128]{1,0:T(8,128)(2,1)S(1)} %get-tuple-element.43.refs_0_), channel_id=1, source_target_pairs={{0,2},{1,3},{2,0},{3,1},{4,6},{5,7},{6,4},{7,5},{8,10},{9,11},{10,... | collective-permute-start | bytes 393224 | tf_op jit(solution)/shard_map/ppermute | solution.py:43
  112.8 6.3 %collective-permute-start.32 = (bf16[512,128]{1,0:T(8,128)(2,1)S(1)}, bf16[512,128]{1,0:T(8,128)(2,1)S(1)}, u32[]{:S(2)}, u32[]{:S(2)}) collective-permute-start(bf16[512,128]{1,0:T(8,128)(2,1)S(1)} %get-tuple-element.43.refs_0_), channel_id=1, source_target_pairs={{0,1},{1,0},{2,3},{3,2},{4,5},{5,4},{6,7},{7,6},{8,9},{9,8},{10,11... | collective-permute-start | bytes 393224 | tf_op jit(solution)/shard_map/ppermute | solution.py:43
  124.6 5.4 %collective-permute-start.42 = (f32[128,128]{1,0:T(8,128)S(1)}, f32[128,128]{1,0:T(8,128)S(1)}, u32[]{:S(2)}, u32[]{:S(2)}) collective-permute-start(f32[128,128]{1,0:T(8,128)S(1)} %add.73), channel_id=1, source_target_pairs={{0,6},{1,7},{2,4},{3,5},{4,2},{5,3},{6,0},{7,1},{8,14},{9,15},{10,... | collective-permute-start | bytes 196616 | tf_op jit(solution)/shard_map/ppermute | solution.py:43
  126.4 5.0 %collective-permute-start.41 = (f32[128,128]{1,0:T(8,128)S(1)}, f32[128,128]{1,0:T(8,128)S(1)}, u32[]{:S(2)}, u32[]{:S(2)}) collective-permute-start(f32[128,128]{1,0:T(8,128)S(1)} %add.73), channel_id=1, source_target_pairs={{0,4},{1,5},{2,6},{3,7},{4,0},{5,1},{6,2},{7,3},{8,12},{9,13},{10,... | collective-permute-start | bytes 196616 | tf_op jit(solution)/shard_map/ppermute | solution.py:43
  126.9 4.5 %collective-permute-start.40 = (f32[128,128]{1,0:T(8,128)S(1)}, f32[128,128]{1,0:T(8,128)S(1)}, u32[]{:S(2)}, u32[]{:S(2)}) collective-permute-start(f32[128,128]{1,0:T(8,128)S(1)} %add.73), channel_id=1, source_target_pairs={{0,2},{1,3},{2,0},{3,1},{4,6},{5,7},{6,4},{7,5},{8,10},{9,11},{10,... | collective-permute-start | bytes 196616 | tf_op jit(solution)/shard_map/ppermute | solution.py:43
  (25 other events, 78.1 us)
Sparse Core Ops, SparseCore 0:
  9.6 50.6 all-gather.2

commit v2 on v1

--- a/solution.py
+++ b/solution.py
@@ -113,27 +113,30 @@
     return jnp.concatenate(upper_out, axis=0), jnp.concatenate(inverse_out, axis=0)
 
 
-def energy_kernel(sizes, places, tiles, start, codes, message, row_sums, col_sums):
-    edge, slots, n_row, n_col, row_pad = sizes
+def energy_kernel(sizes, places, counts, tiles, start, message, row_sums, col_sums):
+    edge, slots, n_row, n_col, row_pad, unroll = sizes
+    count = counts[0, 0]
     row_sums[...] = jnp.zeros_like(row_sums)
     col_sums[...] = jnp.zeros_like(col_sums)
     ones = jnp.ones((SUB, edge), BF16)
 
-    def visit(s, carry):
-        wide = tiles[s].astype(F32)
-        square = wide * wide
-        high = square.astype(BF16)
-        low = (square - high.astype(F32)).astype(BF16)
-        by_row = ((1,), (1,))
-        by_col = ((1,), (0,))
-        fast = lax.Precision.DEFAULT
-        u = jnp.minimum(places[s], n_row - 1)
-        v = jnp.minimum(places[slots + s], n_col - 1)
-        row_sums[u] += dot(ones, high, by_row, fast) + dot(ones, low, by_row, fast)
-        col_sums[v] += dot(ones, high, by_col, fast) + dot(ones, low, by_col, fast)
+    def visit(q, carry):
+        for j in range(unroll):
+            s = q * unroll + j
+            wide = tiles[0, 0, s].astype(F32)
+            square = jnp.where(s < count, wide * wide, 0.0)
+            high = square.astype(BF16)
+            low = (square - high.astype(F32)).astype(BF16)
+            by_row = ((1,), (1,))
+            by_col = ((1,), (0,))
+            fast = lax.Precision.DEFAULT
+            u = jnp.minimum(places[0, 0, 0, s], n_row - 1)
+            v = jnp.minimum(places[0, 0, 1, s], n_col - 1)
+            row_sums[u] += dot(ones, high, by_row, fast) + dot(ones, low, by_row, fast)
+            col_sums[v] += dot(ones, high, by_col, fast) + dot(ones, low, by_col, fast)
         return carry
 
-    lax.fori_loop(0, places[2 * slots], visit, 0)
+    lax.fori_loop(0, (count + unroll - 1) // unroll, visit, 0)
     message[0:edge, :] = start[...]
     for v in range(n_col):
         message[edge + v : edge + v + 1, :] = col_sums[v, 0:1, :]
@@ -142,7 +145,12 @@
         message[base + u : base + u + 1, :] = row_sums[u, 0:1, :]
     for u in range(n_row, row_pad):
         message[base + u : base + u + 1, :] = row_sums[0, 0:1, :]
-    message[base + row_pad :, :] = codes[...]
+    column = lax.broadcasted_iota(jnp.int32, (SUB, edge), 1)
+    codes = jnp.where(column == slots, count, 0)
+    for s in range(slots):
+        code = places[0, 0, 0, s] * n_col + places[0, 0, 1, s]
+        codes = jnp.where(column == s, code, codes)
+    message[base + row_pad :, :] = codes.astype(F32)
 
 
 def start_kernel(sizes, here, *refs):
@@ -199,9 +207,10 @@
     scaled[...] = (col_scale[...] * value).astype(BF16)
 
 
-def apply_kernel(sizes, first, meta, here, tiles, row_scale, current, previous, *refs):
+def apply_kernel(sizes, first, meta, here, row_scale, current, previous, *refs):
     edge, slots, n_row, n_col, unroll = sizes
-    pieces, (value, keep, send, panels, total) = refs[:n_col], refs[n_col:]
+    tiles, pieces = refs[: 2 * n_row], refs[2 * n_row : 2 * n_row + n_col]
+    value, keep, send, panels, total = refs[2 * n_row + n_col :]
     rank, place = here[0], here[1]
     for k in range(n_col):
         panels[place ^ k] = pieces[k][...].reshape(n_row, edge, edge)
@@ -209,23 +218,25 @@
     width = slots + 1
     for k in range(n_row):
         group = rank ^ k
-        count = meta[k * width + slots]
-
-        def visit(q, carry, k=k, group=group, count=count):
-            for j in range(unroll):
-                s = q * unroll + j
-                code = meta[k * width + s]
-                u = jnp.minimum(code // n_col, n_row - 1)
-                v = code % n_col
-                product = dot(
-                    tiles[group * slots + s],
-                    panels[v, group],
-                    precision=lax.Precision.DEFAULT,
-                )
-                total[u] += jnp.where(s < count, product, 0.0)
-            return carry
-
-        lax.fori_loop(0, (count + unroll - 1) // unroll, visit, 0)
+        for part in range(2):
+            begin = part * tiles[0].shape[2]
+            live = jnp.clip(meta[k * width + slots] - begin, 0, tiles[part].shape[2])
+
+            def visit(q, carry, k=k, group=group, part=part, begin=begin, live=live):
+                for j in range(unroll):
+                    s = q * unroll + j
+                    code = meta[k * width + begin + s]
+                    u = jnp.minimum(code // n_col, n_row - 1)
+                    v = code % n_col
+                    product = dot(
+                        tiles[2 * k + part][0, 0, s],
+                        panels[v, group],
+                        precision=lax.Precision.DEFAULT,
+                    )
+                    total[u] += jnp.where(s < live, product, 0.0)
+                return carry
+
+            lax.fori_loop(0, (live + unroll - 1) // unroll, visit, 0)
     applied = row_scale[...] * total[...].reshape(n_row * edge, edge)
     moved = applied if first else applied + MOMENTUM * previous[...]
     value[...] = moved
@@ -277,8 +288,7 @@
 
 def per_device(start_basis, tile_values, tile_coords, tile_count):
     edge, columns = start_basis.shape
-    tiles = tile_values[0, 0]
-    slots = tiles.shape[0]
+    slots = tile_values.shape[2]
     n_row, n_col = lax.axis_size("row"), lax.axis_size("col")
     items = float(edge * n_row * n_col)
     rows = n_row * edge
@@ -287,19 +297,28 @@
     block = ((rows, columns), F32)
     square = ((columns, columns), F32)
 
-    all_tiles = lax.all_gather(tiles, "row", axis=0, tiled=True)
-
-    places = jnp.concatenate([tile_coords[0, 0].reshape(-1), tile_count[0]])
-    codes = jnp.concatenate([tile_coords[0, 0, 0] * n_col + tile_coords[0, 0, 1], tile_count[0]])
-    codes = jnp.pad(codes.astype(F32)[None, :], ((0, SUB - 1), (0, columns - slots - 1)))
+    first = slots * 4 // 16
+    halves_here = (tile_values[:, :, :first], tile_values[:, :, first:])
+    early, late = ([half] + [None] * (n_row - 1) for half in halves_here)
+    direct = [k for k in range(1, n_row) if k & (k - 1) == 0]
+    relayed = [k for k in range(1, n_row) if k & (k - 1) != 0]
+    for k in direct:
+        early[k] = swap(early[0], "row", k)
+
     length = edge + n_col + row_pad + SUB
     (message,) = call(
-        functools.partial(energy_kernel, (edge, slots, n_row, n_col, row_pad)),
+        functools.partial(energy_kernel, (edge, slots, n_row, n_col, row_pad, 4)),
         [((length, columns), F32)],
         [pltpu.VMEM((n_row, SUB, columns), F32), pltpu.VMEM((n_col, SUB, columns), F32)],
+        smem=2,
         inputs=4,
-    )(places, tiles, start_basis, codes)
+    )(tile_coords, tile_count, tile_values, start_basis)
     messages = [message] + [swap(message, "row", k) for k in range(1, n_row)]
+    messages, early, late[0] = lax.optimization_barrier((messages, early, late[0]))
+    for k in relayed:
+        early[k] = swap(early[k & (k - 1)], "row", k & -k)
+    for k in direct:
+        late[k] = swap(late[0], "row", k)
     meta = jnp.concatenate([m[length - SUB, : slots + 1] for m in messages]).astype(jnp.int32)
 
     part = (edge + n_row * n_col) // 2
@@ -317,6 +336,11 @@
         inputs=4,
     )(here, mine, other, basis)
 
+    scaled, early, late = lax.optimization_barrier((scaled, early, late))
+    for k in relayed:
+        late[k] = swap(late[k & (k - 1)], "row", k & -k)
+    tiles = [half for pair in zip(early, late) for half in pair]
+
     previous, coupling = current, None
     for iteration in range(ITERS):
         pieces = gather_pieces(scaled)
@@ -328,8 +352,8 @@
                 pltpu.VMEM((n_row, edge, columns), F32),
             ],
             smem=2,
-            inputs=6 + n_col,
-        )(meta, here, all_tiles, row_scale, current, previous, *pieces)
+            inputs=5 + 2 * n_row + n_col,
+        )(meta, here, row_scale, current, previous, *tiles, *pieces)
         mine, other = plane_sum(keep, send)
         if iteration == ITERS - 1:
             break

time: 147 us -> 132 us (0.90); the launches traced: 145 us -> 132 us
  between operations: 14.8 us -> 1.52 us
  starting transfers between devices: 33.2 us -> 40.6 us
  waiting for transfers between devices: 58.7 us -> 55.6 us
  local copies, waits for them, and re-layouts: 4.25 us -> 2.03 us
    ppermute x44 -> x50, starting transfers between devices: 33.2 us -> 40.6 us  [swap(): return lax.ppermute(value, axis, [(i, i ^ distance) for i in range(size)])]
    unnamed x8 -> x6, local copies, waits for them, and re-layouts: 3.47 us -> 1.05 us
    all_gather x1 -> x0, waiting for transfers between devices: 2.26 us -> none  [per_device(): all_tiles = lax.all_gather(tiles, 'row', axis=0, tiled=True)]
    ppermute x44 -> x50, waiting for transfers between devices: 55.7 us -> 55.6 us  [swap(): return lax.ppermute(value, axis, [(i, i ^ distance) for i in range(size)])]
  transfers between devices with their start and end apart: 45 -> 50, of which waited for: 34 -> 35; matrix products, arithmetic and copies ran while one was open for 1% -> 0% of each run, Pallas kernels for 6% -> 5%
where the time goes in v2:
time: 132 us
  waiting for transfers between devices  55.6 us (42%)
  starting transfers between devices  40.6 us (31%)
  Pallas kernels  32 us (24%)
  local copies, waits for them, and re-layouts  2.03 us (2%)
  between operations  1.52 us (1%)
    ppermute x50, waiting for transfers between devices, swap(): return lax.ppermute(value, axis, [(i, i ^ distance) for i in range(size)])  55.6 us
    ppermute x50, starting transfers between devices, swap(): return lax.ppermute(value, axis, [(i, i ^ distance) for i in range(size)])  40.6 us
    pallas_call x2, Pallas kernels, per_device(): call(functools.partial(update_kernel, items), [block, ((rows, columns), B...  11.2 us
    pallas_call x3, Pallas kernels, per_device(): call(functools.partial(apply_kernel, (edge, slots, n_row, n_col, 4), iter...  7.96 us
    pallas_call x1, Pallas kernels, per_device(): call(functools.partial(last_kernel, (edge, items)), [((edge, columns), F3...  5.91 us
    pallas_call x1, Pallas kernels, per_device(): call(functools.partial(first_kernel, (edge, n_row, n_col, items)), [block...  5.06 us
  transfers between devices with their start and end apart: 50, of which 35 were waited for; matrix products, arithmetic and copies ran while one was open for 0% of the time, Pallas kernels for 5%

profile of v2, /device:TPU:0, one launch (start us, length us, event | category | flops | bytes accessed | tf_op | source)
XLA Modules:
  0.0 132.0 jit_solution(10647118126846810757)
XLA Ops:
  1.6 4.1 %collective-permute-start.4 = (bf16[1,1,4,128,128]{4,3,2,1,0:T(8,128)(2,1)S(1)}, bf16[1,1,4,128,128]{4,3,2,1,0:T(8,128)(2,1)S(1)}, u32[]{:S(2)}, u32[]{:S(2)}) collective-permute-start(bf16[1,1,4,128,128]{4,3,2,1,0:T(8,128)(2,1)S(1)} %slice.18.refs_0_), channel_id=1, source_target_pairs={{0,16},{8,24},{16,0},{24,8},{1,17},{9,25},{17,1},{25,9},{2,18},{10... | collective-permute-start | bytes 393224 | tf_op jit(solution)/shard_map/ppermute | solution.py:43
  10.0 2.6 %collective-permute-start.1 = (f32[152,128]{1,0:T(8,128)S(1)}, f32[152,128]{1,0:T(8,128)S(1)}, u32[]{:S(2)}, u32[]{:S(2)}) collective-permute-start(f32[152,128]{1,0:T(8,128)S(1)} %shard_map.59.refs_0_), channel_id=1, source_target_pairs={{0,16},{8,24},{16,0},{24,8},{1,17},{9,25},{17,1},{25,9},{2,18},{10... | collective-permute-start | bytes 233480 | tf_op jit(solution)/shard_map/ppermute | solution.py:43
  14.4 2.6 %collective-permute-done.2.refs_3_ = f32[152,128]{1,0:T(8,128)S(1)} collective-permute-done((f32[152,128]{1,0:T(8,128)S(1)}, f32[152,128]{1,0:T(8,128)S(1)}, u32[]{:S(2)}, u32[]{:S(2)}) %collective-permute-start.2) | collective-permute-done | bytes 77856 | tf_op jit(solution)/shard_map/ppermute | solution.py:43
  17.0 2.4 %collective-permute-done.1.refs_2_ = f32[152,128]{1,0:T(8,128)S(1)} collective-permute-done((f32[152,128]{1,0:T(8,128)S(1)}, f32[152,128]{1,0:T(8,128)S(1)}, u32[]{:S(2)}, u32[]{:S(2)}) %collective-permute-start.1) | collective-permute-done | bytes 77856 | tf_op jit(solution)/shard_map/ppermute | solution.py:43
  19.8 3.0 %collective-permute-start.11 = (bf16[1,1,12,128,128]{4,3,2,1,0:T(8,128)(2,1)S(1)}, bf16[1,1,12,128,128]{4,3,2,1,0:T(8,128)(2,1)S(1)}, u32[]{:S(2)}, u32[]{:S(2)}) collective-permute-start(bf16[1,1,12,128,128]{4,3,2,1,0:T(8,128)(2,1)S(1)} %slice.19.refs_1_), channel_id=1, source_target_pairs={{0,8},{8,0},{16,24},{24,16},{1,9},{9,1},{17,25},{25,17},{2,10},{10... | collective-permute-start | bytes 1179656 | tf_op jit(solution)/shard_map/ppermute | solution.py:43
  25.2 2.4 %collective-permute-start.8 = (f32[80,128]{1,0:T(8,128)S(1)}, f32[80,128]{1,0:T(8,128)S(1)}, u32[]{:S(2)}, u32[]{:S(2)}) collective-permute-start(f32[80,128]{1,0:T(8,128)S(1)} %add.48), channel_id=1, source_target_pairs={{0,6},{1,7},{2,4},{3,5},{4,2},{5,3},{6,0},{7,1},{8,14},{9,15},{10,... | collective-permute-start | bytes 122888 | tf_op jit(solution)/shard_map/ppermute | solution.py:43
  33.5 5.1 %shard_map.61 = (f32[512,128]{1,0:T(8,128)S(1)}, bf16[512,128]{1,0:T(8,128)(2,1)S(1)}, f32[512,128]{1,0:T(8,128)S(1)}) custom-call(s32[2]{0:T(128)S(1)} %pad_add_fusion.here, f32[80,128]{1,0:T(8,128)S(1)} %add_add_fusion.3.mine, f32[80,128]{1,0:T(8,128)S(1)} %collective-permute-done.9.other, f32[512,128]{1,0:T(8,128)S(1)} %get-tuple-element.48.basis), custom_call_target="tpu_custom_call" | custom-call | tf_op jit(solution)/shard_map/pallas_call | solution.py:332
  38.5 3.1 %collective-permute-done.10.refs_6_ = bf16[1,1,4,128,128]{4,3,2,1,0:T(8,128)(2,1)S(1)} collective-permute-done((bf16[1,1,4,128,128]{4,3,2,1,0:T(8,128)(2,1)S(1)}, bf16[1,1,4,128,128]{4,3,2,1,0:T(8,128)(2,1)S(1)}, u32[]{:S(2)}, u32[]{:S(2)}) %collective-permute-start.10) | collective-permute-done | bytes 131104 | tf_op jit(solution)/shard_map/ppermute | solution.py:43
  45.6 3.3 %collective-permute-done.19.refs_14_ = bf16[512,128]{1,0:T(8,128)(2,1)S(1)} collective-permute-done((bf16[512,128]{1,0:T(8,128)(2,1)S(1)}, bf16[512,128]{1,0:T(8,128)(2,1)S(1)}, u32[]{:S(2)}, u32[]{:S(2)}) %collective-permute-start.19) | collective-permute-done | bytes 131104 | tf_op jit(solution)/shard_map/ppermute | solution.py:43
  52.0 3.0 %collective-permute-done.13.refs_7_ = bf16[1,1,12,128,128]{4,3,2,1,0:T(8,128)(2,1)S(1)} collective-permute-done((bf16[1,1,12,128,128]{4,3,2,1,0:T(8,128)(2,1)S(1)}, bf16[1,1,12,128,128]{4,3,2,1,0:T(8,128)(2,1)S(1)}, u32[]{:S(2)}, u32[]{:S(2)}) %collective-permute-start.13) | collective-permute-done | bytes 393248 | tf_op jit(solution)/shard_map/ppermute | solution.py:43
  55.0 2.7 %shard_map.62 = (f32[512,128]{1,0:T(8,128)S(1)}, f32[128,128]{1,0:T(8,128)S(1)}, f32[128,128]{1,0:T(8,128)S(1)}) custom-call(s32[68]{0:T(128)S(1)} %maximum_convert_fusion.meta, s32[2]{0:T(128)S(1)} %pad_add_fusion.here, f32[512,128]{1,0:T(8,128)S(1)} %get-tuple-element.45.row_scale, f32[512,128]{1,0:T(8,128)S(1)} %get-tuple-element.49.current.previous, ...), custom_call_target="tpu_custom_call" | custom-call | tf_op jit(solution)/shard_map/pallas_call | solution.py:347
  59.0 2.9 %collective-permute-start.24 = (f32[128,128]{1,0:T(8,128)S(1)}, f32[128,128]{1,0:T(8,128)S(1)}, u32[]{:S(2)}, u32[]{:S(2)}) collective-permute-start(f32[128,128]{1,0:T(8,128)S(1)} %add.52), channel_id=1, source_target_pairs={{0,6},{1,7},{2,4},{3,5},{4,2},{5,3},{6,0},{7,1},{8,14},{9,15},{10,... | collective-permute-start | bytes 196616 | tf_op jit(solution)/shard_map/ppermute | solution.py:43
  67.5 5.7 %shard_map.63 = (f32[512,128]{1,0:T(8,128)S(1)}, bf16[512,128]{1,0:T(8,128)(2,1)S(1)}, f32[512,128]{1,0:T(8,128)S(1)}, f32[128,128]{1,0:T(8,128)}) custom-call(s32[2]{0:T(128)S(1)} %pad_add_fusion.here, f32[128,128]{1,0:T(8,128)S(1)} %add_add_fusion.2.mine, f32[128,128]{1,0:T(8,128)S(1)} %collective-permute-done.25.other, ...), custom_call_target="tpu_custom_call" | custom-call | tf_op jit(solution)/shard_map/pallas_call | solution.py:360
  76.7 3.8 %collective-permute-done.31.refs_14_ = bf16[512,128]{1,0:T(8,128)(2,1)S(1)} collective-permute-done((bf16[512,128]{1,0:T(8,128)(2,1)S(1)}, bf16[512,128]{1,0:T(8,128)(2,1)S(1)}, u32[]{:S(2)}, u32[]{:S(2)}) %collective-permute-start.31) | collective-permute-done | bytes 131104 | tf_op jit(solution)/shard_map/ppermute | solution.py:43
  80.5 2.0 %collective-permute-done.29.refs_12_ = bf16[512,128]{1,0:T(8,128)(2,1)S(1)} collective-permute-done((bf16[512,128]{1,0:T(8,128)(2,1)S(1)}, bf16[512,128]{1,0:T(8,128)(2,1)S(1)}, u32[]{:S(2)}, u32[]{:S(2)}) %collective-permute-start.29) | collective-permute-done | bytes 131104 | tf_op jit(solution)/shard_map/ppermute | solution.py:43
  84.4 2.7 %shard_map.64 = (f32[512,128]{1,0:T(8,128)S(1)}, f32[128,128]{1,0:T(8,128)S(1)}, f32[128,128]{1,0:T(8,128)S(1)}) custom-call(s32[68]{0:T(128)S(1)} %maximum_convert_fusion.meta, s32[2]{0:T(128)S(1)} %pad_add_fusion.here, f32[512,128]{1,0:T(8,128)S(1)} %get-tuple-element.45.row_scale, f32[512,128]{1,0:T(8,128)S(1)} %get-tuple-element.67.current, ...), custom_call_target="tpu_custom_call" | custom-call | tf_op jit(solution)/shard_map/pallas_call | solution.py:347
  88.5 2.7 %collective-permute-start.36 = (f32[128,128]{1,0:T(8,128)S(1)}, f32[128,128]{1,0:T(8,128)S(1)}, u32[]{:S(2)}, u32[]{:S(2)}) collective-permute-start(f32[128,128]{1,0:T(8,128)S(1)} %add.56), channel_id=1, source_target_pairs={{0,6},{1,7},{2,4},{3,5},{4,2},{5,3},{6,0},{7,1},{8,14},{9,15},{10,... | collective-permute-start | bytes 196616 | tf_op jit(solution)/shard_map/ppermute | solution.py:43
  96.8 5.5 %shard_map.65 = (f32[512,128]{1,0:T(8,128)S(1)}, bf16[512,128]{1,0:T(8,128)(2,1)S(1)}, f32[512,128]{1,0:T(8,128)S(1)}, f32[128,128]{1,0:T(8,128)S(1)}) custom-call(s32[2]{0:T(128)S(1)} %pad_add_fusion.here, f32[128,128]{1,0:T(8,128)S(1)} %add_add_fusion.1.mine, f32[128,128]{1,0:T(8,128)S(1)} %collective-permute-done.37.other, ...), custom_call_target="tpu_custom_call" | custom-call | tf_op jit(solution)/shard_map/pallas_call | solution.py:360
  102.3 1.9 %collective-permute-start.43 = (bf16[512,128]{1,0:T(8,128)(2,1)S(1)}, bf16[512,128]{1,0:T(8,128)(2,1)S(1)}, u32[]{:S(2)}, u32[]{:S(2)}) collective-permute-start(bf16[512,128]{1,0:T(8,128)(2,1)S(1)} %get-tuple-element.75.refs_8_), channel_id=1, source_target_pairs={{0,6},{1,7},{2,4},{3,5},{4,2},{5,3},{6,0},{7,1},{8,14},{9,15},{10,... | collective-permute-start | bytes 393224 | tf_op jit(solution)/shard_map/ppermute | solution.py:43
  105.9 3.7 %collective-permute-done.43.refs_14_ = bf16[512,128]{1,0:T(8,128)(2,1)S(1)} collective-permute-done((bf16[512,128]{1,0:T(8,128)(2,1)S(1)}, bf16[512,128]{1,0:T(8,128)(2,1)S(1)}, u32[]{:S(2)}, u32[]{:S(2)}) %collective-permute-start.43) | collective-permute-done | bytes 131104 | tf_op jit(solution)/shard_map/ppermute | solution.py:43
  109.6 2.0 %collective-permute-done.41.refs_12_ = bf16[512,128]{1,0:T(8,128)(2,1)S(1)} collective-permute-done((bf16[512,128]{1,0:T(8,128)(2,1)S(1)}, bf16[512,128]{1,0:T(8,128)(2,1)S(1)}, u32[]{:S(2)}, u32[]{:S(2)}) %collective-permute-start.41) | collective-permute-done | bytes 131104 | tf_op jit(solution)/shard_map/ppermute | solution.py:43
  113.6 2.5 %shard_map.66 = (f32[512,128]{1,0:T(8,128)S(1)}, f32[128,128]{1,0:T(8,128)S(1)}, f32[128,128]{1,0:T(8,128)S(1)}) custom-call(s32[68]{0:T(128)S(1)} %maximum_convert_fusion.meta, s32[2]{0:T(128)S(1)} %pad_add_fusion.here, f32[512,128]{1,0:T(8,128)S(1)} %get-tuple-element.45.row_scale, f32[512,128]{1,0:T(8,128)S(1)} %get-tuple-element.73.current, ...), custom_call_target="tpu_custom_call" | custom-call | tf_op jit(solution)/shard_map/pallas_call | solution.py:347
  117.4 3.0 %collective-permute-start.48 = (f32[128,128]{1,0:T(8,128)S(1)}, f32[128,128]{1,0:T(8,128)S(1)}, u32[]{:S(2)}, u32[]{:S(2)}) collective-permute-start(f32[128,128]{1,0:T(8,128)S(1)} %add.60), channel_id=1, source_target_pairs={{0,6},{1,7},{2,4},{3,5},{4,2},{5,3},{6,0},{7,1},{8,14},{9,15},{10,... | collective-permute-start | bytes 196616 | tf_op jit(solution)/shard_map/ppermute | solution.py:43
  126.1 5.9 %shard_map.67 = (f32[128,128]{1,0:T(8,128)}, f32[128,128]{1,0:T(8,128)}) custom-call(s32[2]{0:T(128)S(1)} %pad_add_fusion.here, f32[128,128]{1,0:T(8,128)S(1)} %add_add_fusion.mine, f32[128,128]{1,0:T(8,128)S(1)} %collective-permute-done.49.other, f32[512,128]{1,0:T(8,128)S(1)} %get-tuple-element.73.current, f32[512,128]{1,0:T(8,128)S(1)} %get-tuple-element.78.value, ...), custom_call_target="tpu_custom_call" | custom-call | tf_op jit(solution)/shard_map/pallas_call | solution.py:365
  (105 shorter events, 51.8 us)
Async XLA Ops:
  1.6 17.8 %collective-permute-start.4 = (bf16[1,1,4,128,128]{4,3,2,1,0:T(8,128)(2,1)S(1)}, bf16[1,1,4,128,128]{4,3,2,1,0:T(8,128)(2,1)S(1)}, u32[]{:S(2)}, u32[]{:S(2)}) collective-permute-start(bf16[1,1,4,128,128]{4,3,2,1,0:T(8,128)(2,1)S(1)} %slice.18.refs_0_), channel_id=1, source_target_pairs={{0,16},{8,24},{16,0},{24,8},{1,17},{9,25},{17,1},{25,9},{2,18},{10... | collective-permute-start | bytes 393224 | tf_op jit(solution)/shard_map/ppermute | solution.py:43
  5.7 13.7 %collective-permute-start.3 = (bf16[1,1,4,128,128]{4,3,2,1,0:T(8,128)(2,1)S(1)}, bf16[1,1,4,128,128]{4,3,2,1,0:T(8,128)(2,1)S(1)}, u32[]{:S(2)}, u32[]{:S(2)}) collective-permute-start(bf16[1,1,4,128,128]{4,3,2,1,0:T(8,128)(2,1)S(1)} %slice.18.refs_0_), channel_id=1, source_target_pairs={{0,8},{8,0},{16,24},{24,16},{1,9},{9,1},{17,25},{25,17},{2,10},{10... | collective-permute-start | bytes 393224 | tf_op jit(solution)/shard_map/ppermute | solution.py:43
  9.9 7.1 %collective-permute-start.2 = (f32[152,128]{1,0:T(8,128)S(1)}, f32[152,128]{1,0:T(8,128)S(1)}, u32[]{:S(2)}, u32[]{:S(2)}) collective-permute-start(f32[152,128]{1,0:T(8,128)S(1)} %shard_map.59.refs_0_), channel_id=1, source_target_pairs={{0,24},{8,16},{16,8},{24,0},{1,25},{9,17},{17,9},{25,1},{2,26},{10... | collective-permute-start | bytes 233480 | tf_op jit(solution)/shard_map/ppermute | solution.py:43
  10.0 9.4 %collective-permute-start.1 = (f32[152,128]{1,0:T(8,128)S(1)}, f32[152,128]{1,0:T(8,128)S(1)}, u32[]{:S(2)}, u32[]{:S(2)}) collective-permute-start(f32[152,128]{1,0:T(8,128)S(1)} %shard_map.59.refs_0_), channel_id=1, source_target_pairs={{0,16},{8,24},{16,0},{24,8},{1,17},{9,25},{17,1},{25,9},{2,18},{10... | collective-permute-start | bytes 233480 | tf_op jit(solution)/shard_map/ppermute | solution.py:43
  12.6 6.8 %collective-permute-start = (f32[152,128]{1,0:T(8,128)S(1)}, f32[152,128]{1,0:T(8,128)S(1)}, u32[]{:S(2)}, u32[]{:S(2)}) collective-permute-start(f32[152,128]{1,0:T(8,128)S(1)} %shard_map.59.refs_0_), channel_id=1, source_target_pairs={{0,8},{8,0},{16,24},{24,16},{1,9},{9,1},{17,25},{25,17},{2,10},{10... | collective-permute-start | bytes 233480 | tf_op jit(solution)/shard_map/ppermute | solution.py:43
  19.4 22.2 %collective-permute-start.12 = (bf16[1,1,12,128,128]{4,3,2,1,0:T(8,128)(2,1)S(1)}, bf16[1,1,12,128,128]{4,3,2,1,0:T(8,128)(2,1)S(1)}, u32[]{:S(2)}, u32[]{:S(2)}) collective-permute-start(bf16[1,1,12,128,128]{4,3,2,1,0:T(8,128)(2,1)S(1)} %slice.19.refs_1_), channel_id=1, source_target_pairs={{0,16},{8,24},{16,0},{24,8},{1,17},{9,25},{17,1},{25,9},{2,18},{10... | collective-permute-start | bytes 1179656 | tf_op jit(solution)/shard_map/ppermute | solution.py:43
  19.8 21.8 %collective-permute-start.11 = (bf16[1,1,12,128,128]{4,3,2,1,0:T(8,128)(2,1)S(1)}, bf16[1,1,12,128,128]{4,3,2,1,0:T(8,128)(2,1)S(1)}, u32[]{:S(2)}, u32[]{:S(2)}) collective-permute-start(bf16[1,1,12,128,128]{4,3,2,1,0:T(8,128)(2,1)S(1)} %slice.19.refs_1_), channel_id=1, source_target_pairs={{0,8},{8,0},{16,24},{24,16},{1,9},{9,1},{17,25},{25,17},{2,10},{10... | collective-permute-start | bytes 1179656 | tf_op jit(solution)/shard_map/ppermute | solution.py:43
  30.1 11.5 %collective-permute-start.10 = (bf16[1,1,4,128,128]{4,3,2,1,0:T(8,128)(2,1)S(1)}, bf16[1,1,4,128,128]{4,3,2,1,0:T(8,128)(2,1)S(1)}, u32[]{:S(2)}, u32[]{:S(2)}) collective-permute-start(bf16[1,1,4,128,128]{4,3,2,1,0:T(8,128)(2,1)S(1)} %collective-permute-done.4.refs_4_), channel_id=1, source_target_pairs={{0,8},{8,0},{16,24},{24,16},{1,9},{9,1},{17,25},{25,17},{2,10},{10... | collective-permute-start | bytes 393224 | tf_op jit(solution)/shard_map/ppermute | solution.py:43
  41.6 7.3 %collective-permute-start.19 = (bf16[512,128]{1,0:T(8,128)(2,1)S(1)}, bf16[512,128]{1,0:T(8,128)(2,1)S(1)}, u32[]{:S(2)}, u32[]{:S(2)}) collective-permute-start(bf16[512,128]{1,0:T(8,128)(2,1)S(1)} %get-tuple-element.62.refs_8_), channel_id=1, source_target_pairs={{0,6},{1,7},{2,4},{3,5},{4,2},{5,3},{6,0},{7,1},{8,14},{9,15},{10,... | collective-permute-start | bytes 393224 | tf_op jit(solution)/shard_map/ppermute | solution.py:43
  42.9 7.5 %collective-permute-start.17 = (bf16[512,128]{1,0:T(8,128)(2,1)S(1)}, bf16[512,128]{1,0:T(8,128)(2,1)S(1)}, u32[]{:S(2)}, u32[]{:S(2)}) collective-permute-start(bf16[512,128]{1,0:T(8,128)(2,1)S(1)} %get-tuple-element.62.refs_8_), channel_id=1, source_target_pairs={{0,4},{1,5},{2,6},{3,7},{4,0},{5,1},{6,2},{7,3},{8,12},{9,13},{10,... | collective-permute-start | bytes 393224 | tf_op jit(solution)/shard_map/ppermute | solution.py:43
  43.4 7.0 %collective-permute-start.15 = (bf16[512,128]{1,0:T(8,128)(2,1)S(1)}, bf16[512,128]{1,0:T(8,128)(2,1)S(1)}, u32[]{:S(2)}, u32[]{:S(2)}) collective-permute-start(bf16[512,128]{1,0:T(8,128)(2,1)S(1)} %get-tuple-element.62.refs_8_), channel_id=1, source_target_pairs={{0,2},{1,3},{2,0},{3,1},{4,6},{5,7},{6,4},{7,5},{8,10},{9,11},{10,... | collective-permute-start | bytes 393224 | tf_op jit(solution)/shard_map/ppermute | solution.py:43
  45.1 9.9 %collective-permute-start.13 = (bf16[1,1,12,128,128]{4,3,2,1,0:T(8,128)(2,1)S(1)}, bf16[1,1,12,128,128]{4,3,2,1,0:T(8,128)(2,1)S(1)}, u32[]{:S(2)}, u32[]{:S(2)}) collective-permute-start(bf16[1,1,12,128,128]{4,3,2,1,0:T(8,128)(2,1)S(1)} %collective-permute-done.12.refs_5_), channel_id=1, source_target_pairs={{0,8},{8,0},{16,24},{24,16},{1,9},{9,1},{17,25},{25,17},{2,10},{10... | collective-permute-start | bytes 1179656 | tf_op jit(solution)/shard_map/ppermute | solution.py:43
  45.6 5.5 %collective-permute-start.14 = (bf16[512,128]{1,0:T(8,128)(2,1)S(1)}, bf16[512,128]{1,0:T(8,128)(2,1)S(1)}, u32[]{:S(2)}, u32[]{:S(2)}) collective-permute-start(bf16[512,128]{1,0:T(8,128)(2,1)S(1)} %get-tuple-element.62.refs_8_), channel_id=1, source_target_pairs={{0,1},{1,0},{2,3},{3,2},{4,5},{5,4},{6,7},{7,6},{8,9},{9,8},{10,11... | collective-permute-start | bytes 393224 | tf_op jit(solution)/shard_map/ppermute | solution.py:43
  59.0 5.3 %collective-permute-start.24 = (f32[128,128]{1,0:T(8,128)S(1)}, f32[128,128]{1,0:T(8,128)S(1)}, u32[]{:S(2)}, u32[]{:S(2)}) collective-permute-start(f32[128,128]{1,0:T(8,128)S(1)} %add.52), channel_id=1, source_target_pairs={{0,6},{1,7},{2,4},{3,5},{4,2},{5,3},{6,0},{7,1},{8,14},{9,15},{10,... | collective-permute-start | bytes 196616 | tf_op jit(solution)/shard_map/ppermute | solution.py:43
  73.2 7.3 %collective-permute-start.31 = (bf16[512,128]{1,0:T(8,128)(2,1)S(1)}, bf16[512,128]{1,0:T(8,128)(2,1)S(1)}, u32[]{:S(2)}, u32[]{:S(2)}) collective-permute-start(bf16[512,128]{1,0:T(8,128)(2,1)S(1)} %get-tuple-element.69.refs_8_), channel_id=1, source_target_pairs={{0,6},{1,7},{2,4},{3,5},{4,2},{5,3},{6,0},{7,1},{8,14},{9,15},{10,... | collective-permute-start | bytes 393224 | tf_op jit(solution)/shard_map/ppermute | solution.py:43
  74.7 7.8 %collective-permute-start.29 = (bf16[512,128]{1,0:T(8,128)(2,1)S(1)}, bf16[512,128]{1,0:T(8,128)(2,1)S(1)}, u32[]{:S(2)}, u32[]{:S(2)}) collective-permute-start(bf16[512,128]{1,0:T(8,128)(2,1)S(1)} %get-tuple-element.69.refs_8_), channel_id=1, source_target_pairs={{0,4},{1,5},{2,6},{3,7},{4,0},{5,1},{6,2},{7,3},{8,12},{9,13},{10,... | collective-permute-start | bytes 393224 | tf_op jit(solution)/shard_map/ppermute | solution.py:43
  76.0 7.1 %collective-permute-start.27 = (bf16[512,128]{1,0:T(8,128)(2,1)S(1)}, bf16[512,128]{1,0:T(8,128)(2,1)S(1)}, u32[]{:S(2)}, u32[]{:S(2)}) collective-permute-start(bf16[512,128]{1,0:T(8,128)(2,1)S(1)} %get-tuple-element.69.refs_8_), channel_id=1, source_target_pairs={{0,2},{1,3},{2,0},{3,1},{4,6},{5,7},{6,4},{7,5},{8,10},{9,11},{10,... | collective-permute-start | bytes 393224 | tf_op jit(solution)/shard_map/ppermute | solution.py:43
  76.7 6.4 %collective-permute-start.26 = (bf16[512,128]{1,0:T(8,128)(2,1)S(1)}, bf16[512,128]{1,0:T(8,128)(2,1)S(1)}, u32[]{:S(2)}, u32[]{:S(2)}) collective-permute-start(bf16[512,128]{1,0:T(8,128)(2,1)S(1)} %get-tuple-element.69.refs_8_), channel_id=1, source_target_pairs={{0,1},{1,0},{2,3},{3,2},{4,5},{5,4},{6,7},{7,6},{8,9},{9,8},{10,11... | collective-permute-start | bytes 393224 | tf_op jit(solution)/shard_map/ppermute | solution.py:43
  88.5 5.3 %collective-permute-start.36 = (f32[128,128]{1,0:T(8,128)S(1)}, f32[128,128]{1,0:T(8,128)S(1)}, u32[]{:S(2)}, u32[]{:S(2)}) collective-permute-start(f32[128,128]{1,0:T(8,128)S(1)} %add.56), channel_id=1, source_target_pairs={{0,6},{1,7},{2,4},{3,5},{4,2},{5,3},{6,0},{7,1},{8,14},{9,15},{10,... | collective-permute-start | bytes 196616 | tf_op jit(solution)/shard_map/ppermute | solution.py:43
  102.3 7.3 %collective-permute-start.43 = (bf16[512,128]{1,0:T(8,128)(2,1)S(1)}, bf16[512,128]{1,0:T(8,128)(2,1)S(1)}, u32[]{:S(2)}, u32[]{:S(2)}) collective-permute-start(bf16[512,128]{1,0:T(8,128)(2,1)S(1)} %get-tuple-element.75.refs_8_), channel_id=1, source_target_pairs={{0,6},{1,7},{2,4},{3,5},{4,2},{5,3},{6,0},{7,1},{8,14},{9,15},{10,... | collective-permute-start | bytes 393224 | tf_op jit(solution)/shard_map/ppermute | solution.py:43
  104.2 7.4 %collective-permute-start.41 = (bf16[512,128]{1,0:T(8,128)(2,1)S(1)}, bf16[512,128]{1,0:T(8,128)(2,1)S(1)}, u32[]{:S(2)}, u32[]{:S(2)}) collective-permute-start(bf16[512,128]{1,0:T(8,128)(2,1)S(1)} %get-tuple-element.75.refs_8_), channel_id=1, source_target_pairs={{0,4},{1,5},{2,6},{3,7},{4,0},{5,1},{6,2},{7,3},{8,12},{9,13},{10,... | collective-permute-start | bytes 393224 | tf_op jit(solution)/shard_map/ppermute | solution.py:43
  105.1 7.1 %collective-permute-start.39 = (bf16[512,128]{1,0:T(8,128)(2,1)S(1)}, bf16[512,128]{1,0:T(8,128)(2,1)S(1)}, u32[]{:S(2)}, u32[]{:S(2)}) collective-permute-start(bf16[512,128]{1,0:T(8,128)(2,1)S(1)} %get-tuple-element.75.refs_8_), channel_id=1, source_target_pairs={{0,2},{1,3},{2,0},{3,1},{4,6},{5,7},{6,4},{7,5},{8,10},{9,11},{10,... | collective-permute-start | bytes 393224 | tf_op jit(solution)/shard_map/ppermute | solution.py:43
  105.9 6.4 %collective-permute-start.38 = (bf16[512,128]{1,0:T(8,128)(2,1)S(1)}, bf16[512,128]{1,0:T(8,128)(2,1)S(1)}, u32[]{:S(2)}, u32[]{:S(2)}) collective-permute-start(bf16[512,128]{1,0:T(8,128)(2,1)S(1)} %get-tuple-element.75.refs_8_), channel_id=1, source_target_pairs={{0,1},{1,0},{2,3},{3,2},{4,5},{5,4},{6,7},{7,6},{8,9},{9,8},{10,11... | collective-permute-start | bytes 393224 | tf_op jit(solution)/shard_map/ppermute | solution.py:43
  117.4 5.4 %collective-permute-start.48 = (f32[128,128]{1,0:T(8,128)S(1)}, f32[128,128]{1,0:T(8,128)S(1)}, u32[]{:S(2)}, u32[]{:S(2)}) collective-permute-start(f32[128,128]{1,0:T(8,128)S(1)} %add.60), channel_id=1, source_target_pairs={{0,6},{1,7},{2,4},{3,5},{4,2},{5,3},{6,0},{7,1},{8,14},{9,15},{10,... | collective-permute-start | bytes 196616 | tf_op jit(solution)/shard_map/ppermute | solution.py:43
  (29 other events, 79.3 us)

commit v3 on v2

--- a/solution.py
+++ b/solution.py
@@ -1,4 +1,5 @@
 import functools
+import math
 
 import jax
 import jax.numpy as jnp
@@ -18,18 +19,28 @@
 HIGHEST = lax.Precision.HIGHEST
 VMEM = pl.BlockSpec(memory_space=pltpu.VMEM)
 SMEM = pl.BlockSpec(memory_space=pltpu.SMEM)
-PARAMS = pltpu.CompilerParams(vmem_limit_bytes=40 * 2**20)
+SPARE_BYTES = 6 * 2**20
+
+
+def nbytes(shape, dtype):
+    return math.prod(shape) * jnp.dtype(dtype).itemsize
 
 
 def call(body, outputs, scratch=(), smem=1, inputs=0):
-    return pl.pallas_call(
-        body,
-        out_shape=[jax.ShapeDtypeStruct(shape, dtype) for shape, dtype in outputs],
-        in_specs=[SMEM] * smem + [VMEM] * (inputs - smem),
-        out_specs=[VMEM] * len(outputs),
-        scratch_shapes=list(scratch),
-        compiler_params=PARAMS,
-    )
+    def run(*operands):
+        held = sum(nbytes(x.shape, x.dtype) for x in operands)
+        held += sum(nbytes(*output) for output in outputs)
+        held += sum(nbytes(x.shape, x.dtype) for x in scratch)
+        return pl.pallas_call(
+            body,
+            out_shape=[jax.ShapeDtypeStruct(shape, dtype) for shape, dtype in outputs],
+            in_specs=[SMEM] * smem + [VMEM] * (inputs - smem),
+            out_specs=[VMEM] * len(outputs),
+            scratch_shapes=list(scratch),
+            compiler_params=pltpu.CompilerParams(vmem_limit_bytes=held + SPARE_BYTES),
+        )(*operands)
+
+    return run
 
 
 def dot(left, right, contract=((1,), (0,)), precision=HIGHEST):
@@ -43,19 +54,17 @@
     return lax.ppermute(value, axis, [(i, i ^ distance) for i in range(size)])
 
 
-def gather_pieces(value):
-    size = lax.axis_size("col")
-    even = [value] + [swap(value, "col", k) for k in range(2, size, 2)]
-    odd = [swap(piece, "col", 1) for piece in even]
-    return [piece for pair in zip(even, odd) for piece in pair]
-
-
-def plane_sum(keep, send):
+def spread(value):
+    return [value] + [swap(value, "col", k) for k in range(2, lax.axis_size("col"), 2)]
+
+
+def plane_sum(keep, send, rider=None):
     half = keep + swap(send, "col", 1)
-    total = half
-    for k in range(2, lax.axis_size("col"), 2):
-        total = total + swap(half, "col", k)
-    return total, swap(total, "col", 1)
+    if rider is not None:
+        half, rider = lax.optimization_barrier((half, rider))
+    total = functools.reduce(jnp.add, spread(half))
+    pieces = None if rider is None else spread(rider)
+    return total, swap(total, "col", 1), pieces
 
 
 def sub(x, k):
@@ -66,51 +75,69 @@
     return jnp.broadcast_to(x[:, j : j + 1], x.shape)
 
 
-def factor(matrix):
+def factor(matrix, want_upper=False):
     edge = matrix.shape[0]
     blocks = edge // SUB
     shape = (SUB, edge)
     rows = [matrix[SUB * b : SUB * b + SUB, :] for b in range(blocks)]
     sublane = lax.broadcasted_iota(jnp.int32, shape, 0)
     column = lax.broadcasted_iota(jnp.int32, shape, 1)
-    inverse = [jnp.where(column == sublane + SUB * b, 1.0, 0.0).astype(F32) for b in range(blocks)]
+    at = [sublane == k for k in range(SUB)]
+    below = [sublane > k for k in range(SUB)]
     upper_out, inverse_out = [], []
+    cols = [lane(rows[0], k) for k in range(SUB)]
     for b in range(blocks):
-        cols = [lane(rows[b], SUB * b + k) for k in range(SUB)]
-        factors, pivots, pivot_inv, upper = [], [], [], {}
+        here, base = rows[b], SUB * b
+        block = (column >= base) & (column < base + SUB)
+        more = b + 1 < blocks
+        if more:
+            first = [lane(rows[b + 1], base + k) for k in range(SUB)]
+            ahead = [lane(rows[b + 1], base + SUB + k) for k in range(SUB)]
+            terms = list(first)
+        unit = jnp.where(column == sublane + base, 1.0, 0.0).astype(F32)
+        both = jnp.where(block, unit, here)
+        forward, upper = both, here
+        pivot = pivot_inv = jnp.ones(shape, F32)
         for k in range(SUB):
-            pivot = sub(cols[k], k)
-            pivots.append(pivot)
-            pivot_inv.append(1.0 / pivot)
-            factors.append(jnp.where(sublane > k, cols[k] * pivot_inv[k], 0.0))
+            spread = sub(cols[k], k)
+            inv = 1.0 / spread
+            pivot = jnp.where(at[k], spread, pivot)
+            pivot_inv = jnp.where(at[k], inv, pivot_inv)
+            others = jnp.where(at[k], 0.0, cols[k])
+            heads = {j: sub(cols[j], k) for j in range(k + 1, SUB)}
             for j in range(k + 1, SUB):
-                upper[k, j] = sub(cols[j], k)
-                cols[j] = cols[j] - factors[k] * upper[k, j]
-        here, inv_here = rows[b], inverse[b]
-        row_bcast, inv_bcast = [], []
-        for k in range(SUB):
-            row_bcast.append(sub(here, k))
-            inv_bcast.append(sub(inv_here, k))
+                cols[j] = cols[j] - (others * heads[j]) * inv
+            if more:
+                scale = terms[k] * inv
+                for j in range(k + 1, SUB):
+                    terms[j] = terms[j] - scale * heads[j]
+                for j in range(SUB):
+                    ahead[j] = ahead[j] - scale * sub(terms[k], j)
+            factors = others * inv
+            row = sub(forward, k)
+            both = both - factors * row
             if k < SUB - 1:
-                here = here - factors[k] * row_bcast[k]
-                inv_here = inv_here - factors[k] * inv_bcast[k]
-        pivot = pivots[SUB - 1]
-        for k in range(SUB - 1):
-            pivot = jnp.where(sublane == k, pivots[k], pivot)
-        root_inv = 1.0 / jnp.sqrt(pivot)
-        upper_out.append(jnp.where(column >= sublane + SUB * b, here * root_inv, 0.0))
-        inverse_out.append(inv_here * root_inv)
+                low = jnp.where(below[k], factors, 0.0)
+                if want_upper:
+                    upper = upper - low * sub(upper, k)
+                forward = forward - low * row
+        root = 1.0 / jnp.sqrt(pivot)
+        inverse_out.append(jnp.where(column <= sublane + base, forward * root, 0.0))
+        if want_upper:
+            upper_out.append(jnp.where(column >= sublane + base, upper * root, 0.0))
+        if not more:
+            break
+        solved = both * pivot_inv
+        spreads = [sub(solved, k) for k in range(SUB)]
         for p in range(b + 1, blocks):
-            terms = [lane(rows[p], SUB * b + k) for k in range(SUB)]
-            row_p, inv_p = rows[p], inverse[p]
-            for k in range(SUB):
-                scale = terms[k] * pivot_inv[k]
-                for j in range(k + 1, SUB):
-                    terms[j] = terms[j] - scale * upper[k, j]
-                row_p = row_p - scale * row_bcast[k]
-                inv_p = inv_p - scale * inv_bcast[k]
-            rows[p], inverse[p] = row_p, inv_p
-    return jnp.concatenate(upper_out, axis=0), jnp.concatenate(inverse_out, axis=0)
+            weights = first if p == b + 1 else [lane(rows[p], base + k) for k in range(SUB)]
+            products = [weights[k] * spreads[k] for k in range(SUB)]
+            while len(products) > 1:
+                products = [sum(products[i : i + 2]) for i in range(0, len(products), 2)]
+            rows[p] = jnp.where(block, 0.0, rows[p]) - products[0]
+        cols = ahead
+    inverse = jnp.concatenate(inverse_out, axis=0)
+    return (jnp.concatenate(upper_out, axis=0) if want_upper else None), inverse
 
 
 def energy_kernel(sizes, places, counts, tiles, start, message, row_sums, col_sums):
@@ -193,27 +220,32 @@
     return jnp.where(core == 0, own, sibling), jnp.where(core == 0, sibling, own)
 
 
-def first_kernel(sizes, here, mine, other, basis, current, scaled, col_scale, energy):
-    edge, n_row, n_col, items = sizes
+def first_factor_kernel(sizes, here, mine, other, inverse, energy):
+    edge, items = sizes
     low, high = halves(here, mine, other)
-    gram = jnp.concatenate([low[: edge // 2], high[: edge // 2]], axis=0) / items
-    energy[...] = jnp.concatenate([low[edge // 2 :], high[edge // 2 :]], axis=0)
+    half = edge // 2
+    energy[...] = jnp.concatenate([low[half:], high[half:]], axis=0)
+    gram = jnp.concatenate([low[:half], high[:half]], axis=0) / items
+    inverse[...] = factor(gram)[1]
+
+
+def first_update_kernel(sizes, distance, here, inverse, energy, piece, new, scaled, col_scale):
+    edge, n_row, n_col = sizes
     for u in range(n_row):
-        row = energy[pl.ds(u * n_col + here[1], 1), :]
+        row = energy[pl.ds(u * n_col + (here[1] ^ distance), 1), :]
         col_scale[u * edge : (u + 1) * edge, :] = down_rows(inverse_fourth_root(row), edge)
-    _, inverse = factor(gram)
-    value = dot(basis[...], inverse, ((1,), (1,)))
-    current[...] = value
+    value = dot(piece[...], inverse[...], ((1,), (1,)))
+    new[...] = value
     scaled[...] = (col_scale[...] * value).astype(BF16)
 
 
 def apply_kernel(sizes, first, meta, here, row_scale, current, previous, *refs):
     edge, slots, n_row, n_col, unroll = sizes
-    tiles, pieces = refs[: 2 * n_row], refs[2 * n_row : 2 * n_row + n_col]
+    tiles, scaled = refs[: 2 * n_row], refs[2 * n_row : 2 * n_row + n_col]
     value, keep, send, panels, total = refs[2 * n_row + n_col :]
     rank, place = here[0], here[1]
     for k in range(n_col):
-        panels[place ^ k] = pieces[k][...].reshape(n_row, edge, edge)
+        panels[place ^ k] = scaled[k][...].reshape(n_row, edge, edge)
     total[...] = jnp.zeros_like(total)
     width = slots + 1
     for k in range(n_row):
@@ -257,18 +289,32 @@
     return identity + STEP_SIZE * STEP_SIZE * change
 
 
-def update_kernel(
-    items, here, mine, other, current, value, col_scale, new, scaled, direction, coupling
-):
+def factor_kernel(sizes, here, mine, other, *refs):
+    count, items = sizes
+    currents, inverse_out, bases, coupling = (
+        refs[:count],
+        refs[count],
+        refs[count + 1 : 2 * count + 1],
+        refs[2 * count + 1 :],
+    )
     cross, square = halves(here, mine, other)
     cross, square = cross / items, square / items
-    step = value[...] - dot(current[...], cross)
-    direction[...] = step
-    upper, inverse = factor(moved_gram(cross, square))
-    coupling[...] = (upper - inverse) / STEP_SIZE
-    result = dot(current[...] + STEP_SIZE * step, inverse, ((1,), (1,)))
-    new[...] = result
+    upper, inverse = factor(moved_gram(cross, square), bool(coupling))
+    for current, base in zip(currents, bases):
+        base[...] = current[...] - STEP_SIZE * dot(current[...], cross)
+    inverse_out[...] = inverse
+    if coupling:
+        coupling[0][...] = (upper - inverse) / STEP_SIZE
+
+
+def update_kernel(inverse, base, value, col_scale, current, scaled, *others):
+    moved = base[...] + STEP_SIZE * value[...]
+    result = dot(moved, inverse[...], ((1,), (1,)))
     scaled[...] = (col_scale[...] * result).astype(BF16)
+    if others:
+        others[0][...] = result
+    if len(others) > 1:
+        others[1][...] = (moved - current[...]) / STEP_SIZE
 
 
 def last_kernel(
@@ -328,24 +374,34 @@
         [pltpu.VMEM((2 * part, columns), F32)],
         inputs=1 + n_row,
     )(here, *messages)
-    mine, other = plane_sum(keep, send)
-    current, scaled, col_scale = call(
-        functools.partial(first_kernel, (edge, n_row, n_col, items)),
-        [block, ((rows, columns), BF16), block],
-        [pltpu.VMEM((n_row * n_col, columns), F32)],
-        inputs=4,
-    )(here, mine, other, basis)
-
-    scaled, early, late = lax.optimization_barrier((scaled, early, late))
+    mine, other, pieces = plane_sum(keep, send, basis)
+    mine, late = lax.optimization_barrier((mine, late))
     for k in relayed:
         late[k] = swap(late[k & (k - 1)], "row", k & -k)
     tiles = [half for pair in zip(early, late) for half in pair]
 
-    previous, coupling = current, None
+    count = n_col // 2
+    piece_rows = ((rows, columns), BF16)
+    inverse, energy = call(
+        functools.partial(first_factor_kernel, (edge, items)),
+        [square, ((n_row * n_col, columns), F32)],
+        inputs=3,
+    )(here, mine, other)
+    firsts = [
+        call(
+            functools.partial(first_update_kernel, (edge, n_row, n_col), 2 * i),
+            [block, piece_rows, block],
+            inputs=4,
+        )(here, inverse, energy, piece)
+        for i, piece in enumerate(pieces)
+    ]
+    currents, scaled, col_scales = (list(part) for part in zip(*firsts))
+    previous = basis
     for iteration in range(ITERS):
-        pieces = gather_pieces(scaled)
+        first, final = iteration == 0, iteration == ITERS - 1
+        panels = [part for piece in scaled for part in (piece, swap(piece, "col", 1))]
         value, keep, send = call(
-            functools.partial(apply_kernel, (edge, slots, n_row, n_col, 4), iteration == 0),
+            functools.partial(apply_kernel, (edge, slots, n_row, n_col, 4), first),
             [block, square, square],
             [
                 pltpu.VMEM((n_col, n_row, edge, columns), BF16),
@@ -353,20 +409,31 @@
             ],
             smem=2,
             inputs=5 + 2 * n_row + n_col,
-        )(meta, here, row_scale, current, previous, *tiles, *pieces)
-        mine, other = plane_sum(keep, send)
-        if iteration == ITERS - 1:
+        )(meta, here, row_scale, currents[0], previous, *tiles, *panels)
+        mine, other, values = plane_sum(keep, send, None if final else value)
+        if final:
             break
-        current, scaled, previous, coupling = call(
-            functools.partial(update_kernel, items),
-            [block, ((rows, columns), BF16), block, square],
-            inputs=6,
-        )(here, mine, other, current, value, col_scale)
+        inverse, *rest = call(
+            functools.partial(factor_kernel, (count, items)),
+            [square] + [block] * count + [square] * (iteration == ITERS - 2),
+            inputs=3 + count,
+        )(here, mine, other, *currents)
+        bases, coupling = rest[:count], rest[count:]
+        wanted = [2] + [0 if iteration == ITERS - 2 else 1] * (count - 1)
+        updates = [
+            call(update_kernel, [piece_rows] + [block] * wanted[i], smem=0, inputs=5)(
+                inverse, bases[i], values[i], col_scales[i], currents[i]
+            )
+            for i in range(count)
+        ]
+        scaled = [u[0] for u in updates]
+        previous = updates[0][2]
+        currents = [u[1] for u in updates if len(u) > 1]
     basis, residual = call(
         functools.partial(last_kernel, (edge, items)),
         [((edge, columns), F32), ((edge, columns), F32)],
         inputs=7,
-    )(here, mine, other, current, value, previous, coupling)
+    )(here, mine, other, currents[0], value, previous, *coupling)
     return (basis, residual)
 
 

time: 132 us -> 122 us (0.924)
  waiting for transfers between devices: 55.6 us -> 39.4 us
  starting transfers between devices: 40.6 us -> 46 us
    ppermute x50, waiting for transfers between devices: 55.6 us -> 39.4 us  [swap(): return lax.ppermute(value, axis, [(i, i ^ distance) for i in range(size)])]
    ppermute x50, starting transfers between devices: 40.6 us -> 46 us  [swap(): return lax.ppermute(value, axis, [(i, i ^ distance) for i in range(size)])]
    pallas_call x9 -> x21, Pallas kernels: 32 us -> 33 us  [run(): pl.pallas_call(body, out_shape=[jax.ShapeDtypeStruct(shape, dtype) for sh...]
  transfers between devices with their start and end apart: 50 -> 50, of which waited for: 35 -> 28; matrix products, arithmetic and copies ran while one was open for 0% -> 0% of each run, Pallas kernels for 5% -> 16%
where the time goes in v3:
time: 122 us
  starting transfers between devices  46 us (38%)
  waiting for transfers between devices  39.4 us (32%)
  Pallas kernels  33 us (27%)
  local copies, waits for them, and re-layouts  2.03 us (2%)
  between operations  1.61 us (1%)
    ppermute x50, starting transfers between devices, swap(): return lax.ppermute(value, axis, [(i, i ^ distance) for i in range(size)])  46 us
    ppermute x50, waiting for transfers between devices, swap(): return lax.ppermute(value, axis, [(i, i ^ distance) for i in range(size)])  39.4 us
    pallas_call x21, Pallas kernels, run(): pl.pallas_call(body, out_shape=[jax.ShapeDtypeStruct(shape, dtype) for sh...  33 us
  transfers between devices with their start and end apart: 50, of which 28 were waited for; matrix products, arithmetic and copies ran while one was open for 0% of the time, Pallas kernels for 16%

profile of v3, /device:TPU:0, one launch (start us, length us, event | category | flops | bytes accessed | tf_op | source)
XLA Modules:
  0.0 122.3 jit_solution(17176214010723984988)
XLA Ops:
  1.6 3.1 %collective-permute-start.3 = (bf16[1,1,4,128,128]{4,3,2,1,0:T(8,128)(2,1)S(1)}, bf16[1,1,4,128,128]{4,3,2,1,0:T(8,128)(2,1)S(1)}, u32[]{:S(2)}, u32[]{:S(2)}) collective-permute-start(bf16[1,1,4,128,128]{4,3,2,1,0:T(8,128)(2,1)S(1)} %slice.18.refs_0_), channel_id=1, source_target_pairs={{0,8},{8,0},{16,24},{24,16},{1,9},{9,1},{17,25},{25,17},{2,10},{10... | collective-permute-start | bytes 393224 | tf_op jit(solution)/shard_map/ppermute | solution.py:54
  4.7 2.6 %collective-permute-start.4 = (bf16[1,1,4,128,128]{4,3,2,1,0:T(8,128)(2,1)S(1)}, bf16[1,1,4,128,128]{4,3,2,1,0:T(8,128)(2,1)S(1)}, u32[]{:S(2)}, u32[]{:S(2)}) collective-permute-start(bf16[1,1,4,128,128]{4,3,2,1,0:T(8,128)(2,1)S(1)} %slice.18.refs_0_), channel_id=1, source_target_pairs={{0,16},{8,24},{16,0},{24,8},{1,17},{9,25},{17,1},{25,9},{2,18},{10... | collective-permute-start | bytes 393224 | tf_op jit(solution)/shard_map/ppermute | solution.py:54
  11.5 2.9 %collective-permute-start.2 = (f32[152,128]{1,0:T(8,128)S(1)}, f32[152,128]{1,0:T(8,128)S(1)}, u32[]{:S(2)}, u32[]{:S(2)}) collective-permute-start(f32[152,128]{1,0:T(8,128)S(1)} %shard_map.59.refs_0_), channel_id=1, source_target_pairs={{0,24},{8,16},{16,8},{24,0},{1,25},{9,17},{17,9},{25,1},{2,26},{10... | collective-permute-start | bytes 233480 | tf_op jit(solution)/shard_map/ppermute | solution.py:54
  14.9 4.6 %collective-permute-done.1.refs_2_ = f32[152,128]{1,0:T(8,128)S(1)} collective-permute-done((f32[152,128]{1,0:T(8,128)S(1)}, f32[152,128]{1,0:T(8,128)S(1)}, u32[]{:S(2)}, u32[]{:S(2)}) %collective-permute-start.1) | collective-permute-done | bytes 77856 | tf_op jit(solution)/shard_map/ppermute | solution.py:54
  19.5 2.2 %collective-permute-start.10 = (bf16[1,1,12,128,128]{4,3,2,1,0:T(8,128)(2,1)S(1)}, bf16[1,1,12,128,128]{4,3,2,1,0:T(8,128)(2,1)S(1)}, u32[]{:S(2)}, u32[]{:S(2)}) collective-permute-start(bf16[1,1,12,128,128]{4,3,2,1,0:T(8,128)(2,1)S(1)} %slice.19.refs_1_), channel_id=1, source_target_pairs={{0,16},{8,24},{16,0},{24,8},{1,17},{9,25},{17,1},{25,9},{2,18},{10... | collective-permute-start | bytes 1179656 | tf_op jit(solution)/shard_map/ppermute | solution.py:54
  30.2 2.2 %collective-permute-done.8 = f32[80,128]{1,0:T(8,128)S(1)} collective-permute-done((f32[80,128]{1,0:T(8,128)S(1)}, f32[80,128]{1,0:T(8,128)S(1)}, u32[]{:S(2)}, u32[]{:S(2)}) %collective-permute-start.8) | collective-permute-done | bytes 40992 | tf_op jit(solution)/shard_map/ppermute | solution.py:54
  34.8 3.2 %collective-permute-done.10.refs_5_ = bf16[1,1,12,128,128]{4,3,2,1,0:T(8,128)(2,1)S(1)} collective-permute-done((bf16[1,1,12,128,128]{4,3,2,1,0:T(8,128)(2,1)S(1)}, bf16[1,1,12,128,128]{4,3,2,1,0:T(8,128)(2,1)S(1)}, u32[]{:S(2)}, u32[]{:S(2)}) %collective-permute-start.10) | collective-permute-done | bytes 393248 | tf_op jit(solution)/shard_map/ppermute | solution.py:54
  37.9 1.8 %collective-permute-start.15 = (f32[512,128]{1,0:T(8,128)S(1)}, f32[512,128]{1,0:T(8,128)S(1)}, u32[]{:S(2)}, u32[]{:S(2)}) collective-permute-start(f32[512,128]{1,0:T(8,128)S(1)} %get-tuple-element.83.piece.previous), channel_id=1, source_target_pairs={{0,2},{1,3},{2,0},{3,1},{4,6},{5,7},{6,4},{7,5},{8,10},{9,11},{10,... | collective-permute-start | bytes 786440 | tf_op jit(solution)/shard_map/ppermute | solution.py:54
  39.8 2.0 %collective-permute-start.13 = (bf16[1,1,12,128,128]{4,3,2,1,0:T(8,128)(2,1)S(1)}, bf16[1,1,12,128,128]{4,3,2,1,0:T(8,128)(2,1)S(1)}, u32[]{:S(2)}, u32[]{:S(2)}) collective-permute-start(bf16[1,1,12,128,128]{4,3,2,1,0:T(8,128)(2,1)S(1)} %collective-permute-done.10.refs_5_), channel_id=1, source_target_pairs={{0,8},{8,0},{16,24},{24,16},{1,9},{9,1},{17,25},{25,17},{2,10},{10... | collective-permute-start | bytes 1179656 | tf_op jit(solution)/shard_map/ppermute | solution.py:54
  41.8 3.2 %shard_map.61 = (f32[128,128]{1,0:T(8,128)S(1)}, f32[32,128]{1,0:T(8,128)S(1)}) custom-call(s32[2]{0:T(128)S(1)} %pad_add_fusion.here, f32[80,128]{1,0:T(8,128)S(1)} %add_add_fusion.3.mine, f32[80,128]{1,0:T(8,128)S(1)} %collective-permute-done.11.other), custom_call_target="tpu_custom_call" | custom-call | tf_op jit(solution)/shard_map/pallas_call | solution.py:34
  51.8 2.9 %shard_map.66 = (f32[512,128]{1,0:T(8,128)S(1)}, f32[128,128]{1,0:T(8,128)S(1)}, f32[128,128]{1,0:T(8,128)S(1)}) custom-call(s32[68]{0:T(128)S(1)} %maximum_convert_fusion.meta, s32[2]{0:T(128)S(1)} %pad_add_fusion.here, f32[512,128]{1,0:T(8,128)S(1)} %get-tuple-element.74.row_scale, f32[512,128]{1,0:T(8,128)S(1)} %get-tuple-element.84.current.refs_0_, ...), custom_call_target="tpu_custom_call" | custom-call | tf_op jit(solution)/shard_map/pallas_call | solution.py:34
  57.4 1.8 %collective-permute-start.23 = (f32[128,128]{1,0:T(8,128)S(1)}, f32[128,128]{1,0:T(8,128)S(1)}, u32[]{:S(2)}, u32[]{:S(2)}) collective-permute-start(f32[128,128]{1,0:T(8,128)S(1)} %add.52), channel_id=1, source_target_pairs={{0,4},{1,5},{2,6},{3,7},{4,0},{5,1},{6,2},{7,3},{8,12},{9,13},{10,... | collective-permute-start | bytes 196616 | tf_op jit(solution)/shard_map/ppermute | solution.py:54
  60.3 1.7 %collective-permute-start.31 = (f32[512,128]{1,0:T(8,128)S(1)}, f32[512,128]{1,0:T(8,128)S(1)}, u32[]{:S(2)}, u32[]{:S(2)}) collective-permute-start(f32[512,128]{1,0:T(8,128)S(1)} %get-tuple-element.104.value), channel_id=1, source_target_pairs={{0,6},{1,7},{2,4},{3,5},{4,2},{5,3},{6,0},{7,1},{8,14},{9,15},{10,... | collective-permute-start | bytes 786440 | tf_op jit(solution)/shard_map/ppermute | solution.py:54
  66.4 3.8 %shard_map.67 = (f32[128,128]{1,0:T(8,128)S(1)}, f32[512,128]{1,0:T(8,128)S(1)}, f32[512,128]{1,0:T(8,128)S(1)}, f32[512,128]{1,0:T(8,128)S(1)}, f32[512,128]{1,0:T(8,128)S(1)}) custom-call(s32[2]{0:T(128)S(1)} %pad_add_fusion.here, f32[128,128]{1,0:T(8,128)S(1)} %add_add_fusion.2.mine, f32[128,128]{1,0:T(8,128)S(1)} %collective-permute-done.25.other, ...), custom_call_target="tpu_custom_call" | custom-call | tf_op jit(solution)/shard_map/pallas_call | solution.py:34
  71.6 3.7 %collective-permute-done.29.value = f32[512,128]{1,0:T(8,128)S(1)} collective-permute-done((f32[512,128]{1,0:T(8,128)S(1)}, f32[512,128]{1,0:T(8,128)S(1)}, u32[]{:S(2)}, u32[]{:S(2)}) %collective-permute-start.29) | collective-permute-done | bytes 262176 | tf_op jit(solution)/shard_map/ppermute | solution.py:54
  77.8 2.9 %shard_map.72 = (f32[512,128]{1,0:T(8,128)S(1)}, f32[128,128]{1,0:T(8,128)S(1)}, f32[128,128]{1,0:T(8,128)S(1)}) custom-call(s32[68]{0:T(128)S(1)} %maximum_convert_fusion.meta, s32[2]{0:T(128)S(1)} %pad_add_fusion.here, f32[512,128]{1,0:T(8,128)S(1)} %get-tuple-element.74.row_scale, f32[512,128]{1,0:T(8,128)S(1)} %get-tuple-element.106.current.refs_0_, ...), custom_call_target="tpu_custom_call" | custom-call | tf_op jit(solution)/shard_map/pallas_call | solution.py:34
  82.0 2.1 %collective-permute-start.34 = (f32[128,128]{1,0:T(8,128)S(1)}, f32[128,128]{1,0:T(8,128)S(1)}, u32[]{:S(2)}, u32[]{:S(2)}) collective-permute-start(f32[128,128]{1,0:T(8,128)S(1)} %add.56), channel_id=1, source_target_pairs={{0,2},{1,3},{2,0},{3,1},{4,6},{5,7},{6,4},{7,5},{8,10},{9,11},{10,... | collective-permute-start | bytes 196616 | tf_op jit(solution)/shard_map/ppermute | solution.py:54
  84.1 1.8 %collective-permute-start.35 = (f32[128,128]{1,0:T(8,128)S(1)}, f32[128,128]{1,0:T(8,128)S(1)}, u32[]{:S(2)}, u32[]{:S(2)}) collective-permute-start(f32[128,128]{1,0:T(8,128)S(1)} %add.56), channel_id=1, source_target_pairs={{0,4},{1,5},{2,6},{3,7},{4,0},{5,1},{6,2},{7,3},{8,12},{9,13},{10,... | collective-permute-start | bytes 196616 | tf_op jit(solution)/shard_map/ppermute | solution.py:54
  85.9 2.9 %collective-permute-start.43 = (f32[512,128]{1,0:T(8,128)S(1)}, f32[512,128]{1,0:T(8,128)S(1)}, u32[]{:S(2)}, u32[]{:S(2)}) collective-permute-start(f32[512,128]{1,0:T(8,128)S(1)} %get-tuple-element.127.value), channel_id=1, source_target_pairs={{0,6},{1,7},{2,4},{3,5},{4,2},{5,3},{6,0},{7,1},{8,14},{9,15},{10,... | collective-permute-start | bytes 786440 | tf_op jit(solution)/shard_map/ppermute | solution.py:54
  89.4 4.8 %collective-permute-done.35 = f32[128,128]{1,0:T(8,128)S(1)} collective-permute-done((f32[128,128]{1,0:T(8,128)S(1)}, f32[128,128]{1,0:T(8,128)S(1)}, u32[]{:S(2)}, u32[]{:S(2)}) %collective-permute-start.35) | collective-permute-done | bytes 65568 | tf_op jit(solution)/shard_map/ppermute | solution.py:54
  95.5 3.8 %shard_map.73 = (f32[128,128]{1,0:T(8,128)S(1)}, f32[512,128]{1,0:T(8,128)S(1)}, f32[512,128]{1,0:T(8,128)S(1)}, f32[512,128]{1,0:T(8,128)S(1)}, f32[512,128]{1,0:T(8,128)S(1)}, /*index=5*/f32[128,128]{1,0:T(8,128)S(1)}) custom-call(s32[2]{0:T(128)S(1)} %pad_add_fusion.here, f32[128,128]{1,0:T(8,128)S(1)} %add_add_fusion.1.mine, ...), custom_call_target="tpu_custom_call" | custom-call | tf_op jit(solution)/shard_map/pallas_call | solution.py:34
  104.2 2.7 %shard_map.78 = (f32[512,128]{1,0:T(8,128)S(1)}, f32[128,128]{1,0:T(8,128)S(1)}, f32[128,128]{1,0:T(8,128)S(1)}) custom-call(s32[68]{0:T(128)S(1)} %maximum_convert_fusion.meta, s32[2]{0:T(128)S(1)} %pad_add_fusion.here, f32[512,128]{1,0:T(8,128)S(1)} %get-tuple-element.74.row_scale, f32[512,128]{1,0:T(8,128)S(1)} %get-tuple-element.128.current, ...), custom_call_target="tpu_custom_call" | custom-call | tf_op jit(solution)/shard_map/pallas_call | solution.py:34
  113.9 1.9 %collective-permute-done.48 = f32[128,128]{1,0:T(8,128)S(1)} collective-permute-done((f32[128,128]{1,0:T(8,128)S(1)}, f32[128,128]{1,0:T(8,128)S(1)}, u32[]{:S(2)}, u32[]{:S(2)}) %collective-permute-start.48) | collective-permute-done | bytes 65568 | tf_op jit(solution)/shard_map/ppermute | solution.py:54
  117.2 5.1 %shard_map.79 = (f32[128,128]{1,0:T(8,128)}, f32[128,128]{1,0:T(8,128)}) custom-call(s32[2]{0:T(128)S(1)} %pad_add_fusion.here, f32[128,128]{1,0:T(8,128)S(1)} %add_add_fusion.mine, f32[128,128]{1,0:T(8,128)S(1)} %collective-permute-done.49.other, f32[512,128]{1,0:T(8,128)S(1)} %get-tuple-element.128.current, f32[512,128]{1,0:T(8,128)S(1)} %get-tuple-element.136.value, ...), custom_call_target="tpu_custom_call" | custom-call | tf_op jit(solution)/shard_map/pallas_call | solution.py:34
  (119 shorter events, 51.0 us)
Async XLA Ops:
  1.6 17.9 %collective-permute-start.3 = (bf16[1,1,4,128,128]{4,3,2,1,0:T(8,128)(2,1)S(1)}, bf16[1,1,4,128,128]{4,3,2,1,0:T(8,128)(2,1)S(1)}, u32[]{:S(2)}, u32[]{:S(2)}) collective-permute-start(bf16[1,1,4,128,128]{4,3,2,1,0:T(8,128)(2,1)S(1)} %slice.18.refs_0_), channel_id=1, source_target_pairs={{0,8},{8,0},{16,24},{24,16},{1,9},{9,1},{17,25},{25,17},{2,10},{10... | collective-permute-start | bytes 393224 | tf_op jit(solution)/shard_map/ppermute | solution.py:54
  4.7 14.8 %collective-permute-start.4 = (bf16[1,1,4,128,128]{4,3,2,1,0:T(8,128)(2,1)S(1)}, bf16[1,1,4,128,128]{4,3,2,1,0:T(8,128)(2,1)S(1)}, u32[]{:S(2)}, u32[]{:S(2)}) collective-permute-start(bf16[1,1,4,128,128]{4,3,2,1,0:T(8,128)(2,1)S(1)} %slice.18.refs_0_), channel_id=1, source_target_pairs={{0,16},{8,24},{16,0},{24,8},{1,17},{9,25},{17,1},{25,9},{2,18},{10... | collective-permute-start | bytes 393224 | tf_op jit(solution)/shard_map/ppermute | solution.py:54
  10.4 9.0 %collective-permute-start.1 = (f32[152,128]{1,0:T(8,128)S(1)}, f32[152,128]{1,0:T(8,128)S(1)}, u32[]{:S(2)}, u32[]{:S(2)}) collective-permute-start(f32[152,128]{1,0:T(8,128)S(1)} %shard_map.59.refs_0_), channel_id=1, source_target_pairs={{0,16},{8,24},{16,0},{24,8},{1,17},{9,25},{17,1},{25,9},{2,18},{10... | collective-permute-start | bytes 233480 | tf_op jit(solution)/shard_map/ppermute | solution.py:54
  11.5 8.0 %collective-permute-start.2 = (f32[152,128]{1,0:T(8,128)S(1)}, f32[152,128]{1,0:T(8,128)S(1)}, u32[]{:S(2)}, u32[]{:S(2)}) collective-permute-start(f32[152,128]{1,0:T(8,128)S(1)} %shard_map.59.refs_0_), channel_id=1, source_target_pairs={{0,24},{8,16},{16,8},{24,0},{1,25},{9,17},{17,9},{25,1},{2,26},{10... | collective-permute-start | bytes 233480 | tf_op jit(solution)/shard_map/ppermute | solution.py:54
  19.5 18.5 %collective-permute-start.10 = (bf16[1,1,12,128,128]{4,3,2,1,0:T(8,128)(2,1)S(1)}, bf16[1,1,12,128,128]{4,3,2,1,0:T(8,128)(2,1)S(1)}, u32[]{:S(2)}, u32[]{:S(2)}) collective-permute-start(bf16[1,1,12,128,128]{4,3,2,1,0:T(8,128)(2,1)S(1)} %slice.19.refs_1_), channel_id=1, source_target_pairs={{0,16},{8,24},{16,0},{24,8},{1,17},{9,25},{17,1},{25,9},{2,18},{10... | collective-permute-start | bytes 1179656 | tf_op jit(solution)/shard_map/ppermute | solution.py:54
  21.7 18.1 %collective-permute-start.9 = (bf16[1,1,12,128,128]{4,3,2,1,0:T(8,128)(2,1)S(1)}, bf16[1,1,12,128,128]{4,3,2,1,0:T(8,128)(2,1)S(1)}, u32[]{:S(2)}, u32[]{:S(2)}) collective-permute-start(bf16[1,1,12,128,128]{4,3,2,1,0:T(8,128)(2,1)S(1)} %slice.19.refs_1_), channel_id=1, source_target_pairs={{0,8},{8,0},{16,24},{24,16},{1,9},{9,1},{17,25},{25,17},{2,10},{10... | collective-permute-start | bytes 1179656 | tf_op jit(solution)/shard_map/ppermute | solution.py:54
  32.4 7.4 %collective-permute-start.11 = (f32[80,128]{1,0:T(8,128)S(1)}, f32[80,128]{1,0:T(8,128)S(1)}, u32[]{:S(2)}, u32[]{:S(2)}) collective-permute-start(f32[80,128]{1,0:T(8,128)S(1)} %add_add_fusion.3.mine), channel_id=1, source_target_pairs={{0,1},{1,0},{2,3},{3,2},{4,5},{5,4},{6,7},{7,6},{8,9},{9,8},{10,11... | collective-permute-start | bytes 122888 | tf_op jit(solution)/shard_map/ppermute | solution.py:54
  32.4 13.5 %collective-permute-start.19 = (f32[512,128]{1,0:T(8,128)S(1)}, f32[512,128]{1,0:T(8,128)S(1)}, u32[]{:S(2)}, u32[]{:S(2)}) collective-permute-start(f32[512,128]{1,0:T(8,128)S(1)} %get-tuple-element.83.piece.previous), channel_id=1, source_target_pairs={{0,6},{1,7},{2,4},{3,5},{4,2},{5,3},{6,0},{7,1},{8,14},{9,15},{10,... | collective-permute-start | bytes 786440 | tf_op jit(solution)/shard_map/ppermute | solution.py:54
  33.2 14.0 %collective-permute-start.17 = (f32[512,128]{1,0:T(8,128)S(1)}, f32[512,128]{1,0:T(8,128)S(1)}, u32[]{:S(2)}, u32[]{:S(2)}) collective-permute-start(f32[512,128]{1,0:T(8,128)S(1)} %get-tuple-element.83.piece.previous), channel_id=1, source_target_pairs={{0,4},{1,5},{2,6},{3,7},{4,0},{5,1},{6,2},{7,3},{8,12},{9,13},{10,... | collective-permute-start | bytes 786440 | tf_op jit(solution)/shard_map/ppermute | solution.py:54
  37.9 10.5 %collective-permute-start.15 = (f32[512,128]{1,0:T(8,128)S(1)}, f32[512,128]{1,0:T(8,128)S(1)}, u32[]{:S(2)}, u32[]{:S(2)}) collective-permute-start(f32[512,128]{1,0:T(8,128)S(1)} %get-tuple-element.83.piece.previous), channel_id=1, source_target_pairs={{0,2},{1,3},{2,0},{3,1},{4,6},{5,7},{6,4},{7,5},{8,10},{9,11},{10,... | collective-permute-start | bytes 786440 | tf_op jit(solution)/shard_map/ppermute | solution.py:54
  39.8 10.0 %collective-permute-start.12 = (bf16[1,1,4,128,128]{4,3,2,1,0:T(8,128)(2,1)S(1)}, bf16[1,1,4,128,128]{4,3,2,1,0:T(8,128)(2,1)S(1)}, u32[]{:S(2)}, u32[]{:S(2)}) collective-permute-start(bf16[1,1,4,128,128]{4,3,2,1,0:T(8,128)(2,1)S(1)} %collective-permute-done.4.refs_4_), channel_id=1, source_target_pairs={{0,8},{8,0},{16,24},{24,16},{1,9},{9,1},{17,25},{25,17},{2,10},{10... | collective-permute-start | bytes 393224 | tf_op jit(solution)/shard_map/ppermute | solution.py:54
  39.8 12.1 %collective-permute-start.13 = (bf16[1,1,12,128,128]{4,3,2,1,0:T(8,128)(2,1)S(1)}, bf16[1,1,12,128,128]{4,3,2,1,0:T(8,128)(2,1)S(1)}, u32[]{:S(2)}, u32[]{:S(2)}) collective-permute-start(bf16[1,1,12,128,128]{4,3,2,1,0:T(8,128)(2,1)S(1)} %collective-permute-done.10.refs_5_), channel_id=1, source_target_pairs={{0,8},{8,0},{16,24},{24,16},{1,9},{9,1},{17,25},{25,17},{2,10},{10... | collective-permute-start | bytes 1179656 | tf_op jit(solution)/shard_map/ppermute | solution.py:54
  56.1 6.3 %collective-permute-start.22 = (f32[128,128]{1,0:T(8,128)S(1)}, f32[128,128]{1,0:T(8,128)S(1)}, u32[]{:S(2)}, u32[]{:S(2)}) collective-permute-start(f32[128,128]{1,0:T(8,128)S(1)} %add.52), channel_id=1, source_target_pairs={{0,2},{1,3},{2,0},{3,1},{4,6},{5,7},{6,4},{7,5},{8,10},{9,11},{10,... | collective-permute-start | bytes 196616 | tf_op jit(solution)/shard_map/ppermute | solution.py:54
  57.4 6.4 %collective-permute-start.23 = (f32[128,128]{1,0:T(8,128)S(1)}, f32[128,128]{1,0:T(8,128)S(1)}, u32[]{:S(2)}, u32[]{:S(2)}) collective-permute-start(f32[128,128]{1,0:T(8,128)S(1)} %add.52), channel_id=1, source_target_pairs={{0,4},{1,5},{2,6},{3,7},{4,0},{5,1},{6,2},{7,3},{8,12},{9,13},{10,... | collective-permute-start | bytes 196616 | tf_op jit(solution)/shard_map/ppermute | solution.py:54
  60.3 10.5 %collective-permute-start.31 = (f32[512,128]{1,0:T(8,128)S(1)}, f32[512,128]{1,0:T(8,128)S(1)}, u32[]{:S(2)}, u32[]{:S(2)}) collective-permute-start(f32[512,128]{1,0:T(8,128)S(1)} %get-tuple-element.104.value), channel_id=1, source_target_pairs={{0,6},{1,7},{2,4},{3,5},{4,2},{5,3},{6,0},{7,1},{8,14},{9,15},{10,... | collective-permute-start | bytes 786440 | tf_op jit(solution)/shard_map/ppermute | solution.py:54
  62.1 13.3 %collective-permute-start.29 = (f32[512,128]{1,0:T(8,128)S(1)}, f32[512,128]{1,0:T(8,128)S(1)}, u32[]{:S(2)}, u32[]{:S(2)}) collective-permute-start(f32[512,128]{1,0:T(8,128)S(1)} %get-tuple-element.104.value), channel_id=1, source_target_pairs={{0,4},{1,5},{2,6},{3,7},{4,0},{5,1},{6,2},{7,3},{8,12},{9,13},{10,... | collective-permute-start | bytes 786440 | tf_op jit(solution)/shard_map/ppermute | solution.py:54
  62.4 13.4 %collective-permute-start.27 = (f32[512,128]{1,0:T(8,128)S(1)}, f32[512,128]{1,0:T(8,128)S(1)}, u32[]{:S(2)}, u32[]{:S(2)}) collective-permute-start(f32[512,128]{1,0:T(8,128)S(1)} %get-tuple-element.104.value), channel_id=1, source_target_pairs={{0,2},{1,3},{2,0},{3,1},{4,6},{5,7},{6,4},{7,5},{8,10},{9,11},{10,... | collective-permute-start | bytes 786440 | tf_op jit(solution)/shard_map/ppermute | solution.py:54
  70.6 6.2 %collective-permute-start.26 = (bf16[512,128]{1,0:T(8,128)(2,1)S(1)}, bf16[512,128]{1,0:T(8,128)(2,1)S(1)}, u32[]{:S(2)}, u32[]{:S(2)}) collective-permute-start(bf16[512,128]{1,0:T(8,128)(2,1)S(1)} %get-tuple-element.108.refs_8_), channel_id=1, source_target_pairs={{0,1},{1,0},{2,3},{3,2},{4,5},{5,4},{6,7},{7,6},{8,9},{9,8},{10,11... | collective-permute-start | bytes 393224 | tf_op jit(solution)/shard_map/ppermute | solution.py:54
  82.0 7.0 %collective-permute-start.34 = (f32[128,128]{1,0:T(8,128)S(1)}, f32[128,128]{1,0:T(8,128)S(1)}, u32[]{:S(2)}, u32[]{:S(2)}) collective-permute-start(f32[128,128]{1,0:T(8,128)S(1)} %add.56), channel_id=1, source_target_pairs={{0,2},{1,3},{2,0},{3,1},{4,6},{5,7},{6,4},{7,5},{8,10},{9,11},{10,... | collective-permute-start | bytes 196616 | tf_op jit(solution)/shard_map/ppermute | solution.py:54
  84.1 10.1 %collective-permute-start.35 = (f32[128,128]{1,0:T(8,128)S(1)}, f32[128,128]{1,0:T(8,128)S(1)}, u32[]{:S(2)}, u32[]{:S(2)}) collective-permute-start(f32[128,128]{1,0:T(8,128)S(1)} %add.56), channel_id=1, source_target_pairs={{0,4},{1,5},{2,6},{3,7},{4,0},{5,1},{6,2},{7,3},{8,12},{9,13},{10,... | collective-permute-start | bytes 196616 | tf_op jit(solution)/shard_map/ppermute | solution.py:54
  85.9 8.3 %collective-permute-start.36 = (f32[128,128]{1,0:T(8,128)S(1)}, f32[128,128]{1,0:T(8,128)S(1)}, u32[]{:S(2)}, u32[]{:S(2)}) collective-permute-start(f32[128,128]{1,0:T(8,128)S(1)} %add.56), channel_id=1, source_target_pairs={{0,6},{1,7},{2,4},{3,5},{4,2},{5,3},{6,0},{7,1},{8,14},{9,15},{10,... | collective-permute-start | bytes 196616 | tf_op jit(solution)/shard_map/ppermute | solution.py:54
  85.9 14.1 %collective-permute-start.43 = (f32[512,128]{1,0:T(8,128)S(1)}, f32[512,128]{1,0:T(8,128)S(1)}, u32[]{:S(2)}, u32[]{:S(2)}) collective-permute-start(f32[512,128]{1,0:T(8,128)S(1)} %get-tuple-element.127.value), channel_id=1, source_target_pairs={{0,6},{1,7},{2,4},{3,5},{4,2},{5,3},{6,0},{7,1},{8,14},{9,15},{10,... | collective-permute-start | bytes 786440 | tf_op jit(solution)/shard_map/ppermute | solution.py:54
  88.8 13.0 %collective-permute-start.41 = (f32[512,128]{1,0:T(8,128)S(1)}, f32[512,128]{1,0:T(8,128)S(1)}, u32[]{:S(2)}, u32[]{:S(2)}) collective-permute-start(f32[512,128]{1,0:T(8,128)S(1)} %get-tuple-element.127.value), channel_id=1, source_target_pairs={{0,4},{1,5},{2,6},{3,7},{4,0},{5,1},{6,2},{7,3},{8,12},{9,13},{10,... | collective-permute-start | bytes 786440 | tf_op jit(solution)/shard_map/ppermute | solution.py:54
  89.1 13.2 %collective-permute-start.39 = (f32[512,128]{1,0:T(8,128)S(1)}, f32[512,128]{1,0:T(8,128)S(1)}, u32[]{:S(2)}, u32[]{:S(2)}) collective-permute-start(f32[512,128]{1,0:T(8,128)S(1)} %get-tuple-element.127.value), channel_id=1, source_target_pairs={{0,2},{1,3},{2,0},{3,1},{4,6},{5,7},{6,4},{7,5},{8,10},{9,11},{10,... | collective-permute-start | bytes 786440 | tf_op jit(solution)/shard_map/ppermute | solution.py:54
  (30 other events, 92.6 us)

commit v4 on v3

--- a/solution.py
+++ b/solution.py
@@ -49,22 +49,52 @@
     )
 
 
+def split(value):
+    high = value.astype(BF16)
+    return high, (value - high.astype(F32)).astype(BF16)
+
+
+def products(left, right):
+    left_high, left_low = split(left)
+    high, low = split(right)
+    rows = jnp.concatenate([left_high, high, left_low, low], axis=1)
+    both = jnp.concatenate([high, low], axis=1)
+    result = dot(rows, both, ((0,), (0,)), lax.Precision.DEFAULT)
+    half, edge = rows.shape[1] // 2, high.shape[1]
+    return result[:half, :edge] + (result[half:, :edge] + result[:half, edge:])
+
+
 def swap(value, axis, distance):
     size = lax.axis_size(axis)
     return lax.ppermute(value, axis, [(i, i ^ distance) for i in range(size)])
 
 
-def spread(value):
-    return [value] + [swap(value, "col", k) for k in range(2, lax.axis_size("col"), 2)]
-
-
-def plane_sum(keep, send, rider=None):
+def spread(value, distances):
+    return [swap(value, "col", k) if k else value for k in distances]
+
+
+def parity_distances():
+    return list(range(0, lax.axis_size("col"), 2))
+
+
+def near_distances():
+    return [k for k in parity_distances() if k & (k - 1) == 0]
+
+
+def plane_sum(keep, send, rider=None, distances=()):
     half = keep + swap(send, "col", 1)
     if rider is not None:
         half, rider = lax.optimization_barrier((half, rider))
-    total = functools.reduce(jnp.add, spread(half))
-    pieces = None if rider is None else spread(rider)
+    total = functools.reduce(jnp.add, spread(half, parity_distances()))
+    pieces = None if rider is None else spread(rider, distances)
     return total, swap(total, "col", 1), pieces
+
+
+def plane_panels(scaled):
+    for k in parity_distances():
+        if k not in scaled:
+            scaled = {**scaled, k: swap(scaled[k & (k - 1)], "col", k & -k)}
+    return [part for k in parity_distances() for part in (scaled[k], swap(scaled[k], "col", 1))]
 
 
 def sub(x, k):
@@ -272,8 +302,8 @@
     applied = row_scale[...] * total[...].reshape(n_row * edge, edge)
     moved = applied if first else applied + MOMENTUM * previous[...]
     value[...] = moved
-    cross = dot(current[...], moved, ((0,), (0,)))
-    square = dot(moved, moved, ((0,), (0,)))
+    parts = products(current[...], moved)
+    cross, square = parts[:edge], parts[edge:]
     core = place % 2
     keep[...] = jnp.where(core == 0, cross, square)
     send[...] = jnp.where(core == 0, square, cross)
@@ -326,9 +356,9 @@
     rows = pl.ds(pl.multiple_of(here[0] * edge, edge), edge)
     old, moved = current[rows, :], value[rows, :]
     rayleigh = cross - MOMENTUM * coupling[...]
+    _, inverse = factor(moved_gram(cross, square))
     residual[...] = moved - MOMENTUM * previous[rows, :] - dot(old, rayleigh)
     step = moved - dot(old, cross)
-    _, inverse = factor(moved_gram(cross, square))
     basis[...] = dot(old + STEP_SIZE * step, inverse, ((1,), (1,)))
 
 
@@ -374,13 +404,14 @@
         [pltpu.VMEM((2 * part, columns), F32)],
         inputs=1 + n_row,
     )(here, *messages)
-    mine, other, pieces = plane_sum(keep, send, basis)
+    everywhere, near = parity_distances(), near_distances()
+    mine, other, pieces = plane_sum(keep, send, basis, everywhere)
     mine, late = lax.optimization_barrier((mine, late))
     for k in relayed:
         late[k] = swap(late[k & (k - 1)], "row", k & -k)
     tiles = [half for pair in zip(early, late) for half in pair]
 
-    count = n_col // 2
+    count = len(near)
     piece_rows = ((rows, columns), BF16)
     inverse, energy = call(
         functools.partial(first_factor_kernel, (edge, items)),
@@ -389,17 +420,18 @@
     )(here, mine, other)
     firsts = [
         call(
-            functools.partial(first_update_kernel, (edge, n_row, n_col), 2 * i),
+            functools.partial(first_update_kernel, (edge, n_row, n_col), distance),
             [block, piece_rows, block],
             inputs=4,
         )(here, inverse, energy, piece)
-        for i, piece in enumerate(pieces)
+        for distance, piece in zip(everywhere, pieces)
     ]
-    currents, scaled, col_scales = (list(part) for part in zip(*firsts))
+    scaled = {k: f[1] for k, f in zip(everywhere, firsts)}
+    currents, _, col_scales = zip(*[f for k, f in zip(everywhere, firsts) if k in near])
     previous = basis
     for iteration in range(ITERS):
         first, final = iteration == 0, iteration == ITERS - 1
-        panels = [part for piece in scaled for part in (piece, swap(piece, "col", 1))]
+        panels = plane_panels(scaled)
         value, keep, send = call(
             functools.partial(apply_kernel, (edge, slots, n_row, n_col, 4), first),
             [block, square, square],
@@ -410,7 +442,7 @@
             smem=2,
             inputs=5 + 2 * n_row + n_col,
         )(meta, here, row_scale, currents[0], previous, *tiles, *panels)
-        mine, other, values = plane_sum(keep, send, None if final else value)
+        mine, other, values = plane_sum(keep, send, None if final else value, near)
         if final:
             break
         inverse, *rest = call(
@@ -426,7 +458,7 @@
             )
             for i in range(count)
         ]
-        scaled = [u[0] for u in updates]
+        scaled = {k: u[0] for k, u in zip(near, updates)}
         previous = updates[0][2]
         currents = [u[1] for u in updates if len(u) > 1]
     basis, residual = call(

time: 122 us -> 119 us (0.975)
  starting transfers between devices: 46 us -> 42.9 us
    ppermute x50, starting transfers between devices: 46 us -> 42.9 us  [swap(): return lax.ppermute(value, axis, [(i, i ^ distance) for i in range(size)])]
    pallas_call x21 -> x19, Pallas kernels: 33 us -> 32.5 us  [run(): pl.pallas_call(body, out_shape=[jax.ShapeDtypeStruct(shape, dtype) for sh...]
  transfers between devices with their start and end apart: 50 -> 50, of which waited for: 28 -> 29; matrix products, arithmetic and copies ran while one was open for 0% -> 0% of each run, Pallas kernels for 16% -> 16%
where the time goes in v4:
time: 119 us
  starting transfers between devices  42.9 us (36%)
  waiting for transfers between devices  39.2 us (33%)
  Pallas kernels  32.5 us (27%)
  local copies, waits for them, and re-layouts  2.03 us (2%)
  between operations  1.66 us (1%)
    ppermute x50, starting transfers between devices, swap(): return lax.ppermute(value, axis, [(i, i ^ distance) for i in range(size)])  42.9 us
    ppermute x50, waiting for transfers between devices, swap(): return lax.ppermute(value, axis, [(i, i ^ distance) for i in range(size)])  39.2 us
    pallas_call x19, Pallas kernels, run(): pl.pallas_call(body, out_shape=[jax.ShapeDtypeStruct(shape, dtype) for sh...  32.5 us
  transfers between devices with their start and end apart: 50, of which 29 were waited for; matrix products, arithmetic and copies ran while one was open for 0% of the time, Pallas kernels for 16%

profile of v4, /device:TPU:0, one launch (start us, length us, event | category | flops | bytes accessed | tf_op | source)
XLA Modules:
  0.0 118.6 jit_solution(17978682962596991180)
XLA Ops:
  1.6 4.1 %collective-permute-start.4 = (bf16[1,1,4,128,128]{4,3,2,1,0:T(8,128)(2,1)S(1)}, bf16[1,1,4,128,128]{4,3,2,1,0:T(8,128)(2,1)S(1)}, u32[]{:S(2)}, u32[]{:S(2)}) collective-permute-start(bf16[1,1,4,128,128]{4,3,2,1,0:T(8,128)(2,1)S(1)} %slice.18.refs_0_), channel_id=1, source_target_pairs={{0,16},{8,24},{16,0},{24,8},{1,17},{9,25},{17,1},{25,9},{2,18},{10... | collective-permute-start | bytes 393224 | tf_op jit(solution)/shard_map/ppermute | solution.py:69
  5.7 1.6 %collective-permute-start.3 = (bf16[1,1,4,128,128]{4,3,2,1,0:T(8,128)(2,1)S(1)}, bf16[1,1,4,128,128]{4,3,2,1,0:T(8,128)(2,1)S(1)}, u32[]{:S(2)}, u32[]{:S(2)}) collective-permute-start(bf16[1,1,4,128,128]{4,3,2,1,0:T(8,128)(2,1)S(1)} %slice.18.refs_0_), channel_id=1, source_target_pairs={{0,8},{8,0},{16,24},{24,16},{1,9},{9,1},{17,25},{25,17},{2,10},{10... | collective-permute-start | bytes 393224 | tf_op jit(solution)/shard_map/ppermute | solution.py:69
  10.0 2.2 %collective-permute-start.1 = (f32[152,128]{1,0:T(8,128)S(1)}, f32[152,128]{1,0:T(8,128)S(1)}, u32[]{:S(2)}, u32[]{:S(2)}) collective-permute-start(f32[152,128]{1,0:T(8,128)S(1)} %shard_map.59.refs_0_), channel_id=1, source_target_pairs={{0,16},{8,24},{16,0},{24,8},{1,17},{9,25},{17,1},{25,9},{2,18},{10... | collective-permute-start | bytes 233480 | tf_op jit(solution)/shard_map/ppermute | solution.py:69
  12.2 2.1 %collective-permute-start = (f32[152,128]{1,0:T(8,128)S(1)}, f32[152,128]{1,0:T(8,128)S(1)}, u32[]{:S(2)}, u32[]{:S(2)}) collective-permute-start(f32[152,128]{1,0:T(8,128)S(1)} %shard_map.59.refs_0_), channel_id=1, source_target_pairs={{0,8},{8,0},{16,24},{24,16},{1,9},{9,1},{17,25},{25,17},{2,10},{10... | collective-permute-start | bytes 233480 | tf_op jit(solution)/shard_map/ppermute | solution.py:69
  14.4 2.7 %collective-permute-done.2.refs_3_ = f32[152,128]{1,0:T(8,128)S(1)} collective-permute-done((f32[152,128]{1,0:T(8,128)S(1)}, f32[152,128]{1,0:T(8,128)S(1)}, u32[]{:S(2)}, u32[]{:S(2)}) %collective-permute-start.2) | collective-permute-done | bytes 77856 | tf_op jit(solution)/shard_map/ppermute | solution.py:69
  17.1 1.6 %collective-permute-done.1.refs_2_ = f32[152,128]{1,0:T(8,128)S(1)} collective-permute-done((f32[152,128]{1,0:T(8,128)S(1)}, f32[152,128]{1,0:T(8,128)S(1)}, u32[]{:S(2)}, u32[]{:S(2)}) %collective-permute-start.1) | collective-permute-done | bytes 77856 | tf_op jit(solution)/shard_map/ppermute | solution.py:69
  19.8 3.0 %collective-permute-start.9 = (bf16[1,1,12,128,128]{4,3,2,1,0:T(8,128)(2,1)S(1)}, bf16[1,1,12,128,128]{4,3,2,1,0:T(8,128)(2,1)S(1)}, u32[]{:S(2)}, u32[]{:S(2)}) collective-permute-start(bf16[1,1,12,128,128]{4,3,2,1,0:T(8,128)(2,1)S(1)} %slice.19.refs_1_), channel_id=1, source_target_pairs={{0,8},{8,0},{16,24},{24,16},{1,9},{9,1},{17,25},{25,17},{2,10},{10... | collective-permute-start | bytes 1179656 | tf_op jit(solution)/shard_map/ppermute | solution.py:69
  25.2 2.4 %collective-permute-start.8 = (f32[80,128]{1,0:T(8,128)S(1)}, f32[80,128]{1,0:T(8,128)S(1)}, u32[]{:S(2)}, u32[]{:S(2)}) collective-permute-start(f32[80,128]{1,0:T(8,128)S(1)} %add.48), channel_id=1, source_target_pairs={{0,6},{1,7},{2,4},{3,5},{4,2},{5,3},{6,0},{7,1},{8,14},{9,15},{10,... | collective-permute-start | bytes 122888 | tf_op jit(solution)/shard_map/ppermute | solution.py:69
  32.2 1.6 %collective-permute-start.17 = (f32[512,128]{1,0:T(8,128)S(1)}, f32[512,128]{1,0:T(8,128)S(1)}, u32[]{:S(2)}, u32[]{:S(2)}) collective-permute-start(f32[512,128]{1,0:T(8,128)S(1)} %get-tuple-element.77.piece.previous), channel_id=1, source_target_pairs={{0,4},{1,5},{2,6},{3,7},{4,0},{5,1},{6,2},{7,3},{8,12},{9,13},{10,... | collective-permute-start | bytes 786440 | tf_op jit(solution)/shard_map/ppermute | solution.py:69
  34.4 3.2 %collective-permute-done.10.refs_5_ = bf16[1,1,12,128,128]{4,3,2,1,0:T(8,128)(2,1)S(1)} collective-permute-done((bf16[1,1,12,128,128]{4,3,2,1,0:T(8,128)(2,1)S(1)}, bf16[1,1,12,128,128]{4,3,2,1,0:T(8,128)(2,1)S(1)}, u32[]{:S(2)}, u32[]{:S(2)}) %collective-permute-start.10) | collective-permute-done | bytes 393248 | tf_op jit(solution)/shard_map/ppermute | solution.py:69
  37.6 2.4 %collective-permute-start.19 = (f32[512,128]{1,0:T(8,128)S(1)}, f32[512,128]{1,0:T(8,128)S(1)}, u32[]{:S(2)}, u32[]{:S(2)}) collective-permute-start(f32[512,128]{1,0:T(8,128)S(1)} %get-tuple-element.77.piece.previous), channel_id=1, source_target_pairs={{0,6},{1,7},{2,4},{3,5},{4,2},{5,3},{6,0},{7,1},{8,14},{9,15},{10,... | collective-permute-start | bytes 786440 | tf_op jit(solution)/shard_map/ppermute | solution.py:69
  42.1 3.2 %shard_map.61 = (f32[128,128]{1,0:T(8,128)S(1)}, f32[32,128]{1,0:T(8,128)S(1)}) custom-call(s32[2]{0:T(128)S(1)} %pad_add_fusion.here, f32[80,128]{1,0:T(8,128)S(1)} %add_add_fusion.3.mine, f32[80,128]{1,0:T(8,128)S(1)} %collective-permute-done.11.other), custom_call_target="tpu_custom_call" | custom-call | tf_op jit(solution)/shard_map/pallas_call | solution.py:34
  48.7 1.6 %shard_map.65 = (f32[512,128]{1,0:T(8,128)}, bf16[512,128]{1,0:T(8,128)(2,1)S(1)}, f32[512,128]{1,0:T(8,128)}) custom-call(s32[2]{0:T(128)S(1)} %pad_add_fusion.here, f32[128,128]{1,0:T(8,128)S(1)} %get-tuple-element.75.inverse, f32[32,128]{1,0:T(8,128)S(1)} %get-tuple-element.76.energy, f32[512,128]{1,0:T(8,128)S(1)} %collective-permute-done.19.piece), custom_call_target="tpu_custom_call" | custom-call | tf_op jit(solution)/shard_map/pallas_call | solution.py:34
  52.6 2.8 %shard_map.66 = (f32[512,128]{1,0:T(8,128)S(1)}, f32[128,128]{1,0:T(8,128)S(1)}, f32[128,128]{1,0:T(8,128)S(1)}) custom-call(s32[68]{0:T(128)S(1)} %maximum_convert_fusion.meta, s32[2]{0:T(128)S(1)} %pad_add_fusion.here, f32[512,128]{1,0:T(8,128)S(1)} %get-tuple-element.68.row_scale, f32[512,128]{1,0:T(8,128)S(1)} %get-tuple-element.78.current.refs_0_, ...), custom_call_target="tpu_custom_call" | custom-call | tf_op jit(solution)/shard_map/pallas_call | solution.py:34
  65.6 3.7 %shard_map.67 = (f32[128,128]{1,0:T(8,128)S(1)}, f32[512,128]{1,0:T(8,128)S(1)}, f32[512,128]{1,0:T(8,128)S(1)}, f32[512,128]{1,0:T(8,128)S(1)}) custom-call(s32[2]{0:T(128)S(1)} %pad_add_fusion.here, f32[128,128]{1,0:T(8,128)S(1)} %add_add_fusion.2.mine, f32[128,128]{1,0:T(8,128)S(1)} %collective-permute-done.25.other, ...), custom_call_target="tpu_custom_call" | custom-call | tf_op jit(solution)/shard_map/pallas_call | solution.py:34
  72.3 3.1 %collective-permute-done.31.refs_14_ = bf16[512,128]{1,0:T(8,128)(2,1)S(1)} collective-permute-done((bf16[512,128]{1,0:T(8,128)(2,1)S(1)}, bf16[512,128]{1,0:T(8,128)(2,1)S(1)}, u32[]{:S(2)}, u32[]{:S(2)}) %collective-permute-start.31) | collective-permute-done | bytes 131104 | tf_op jit(solution)/shard_map/ppermute | solution.py:69
  76.7 2.6 %shard_map.71 = (f32[512,128]{1,0:T(8,128)S(1)}, f32[128,128]{1,0:T(8,128)S(1)}, f32[128,128]{1,0:T(8,128)S(1)}) custom-call(s32[68]{0:T(128)S(1)} %maximum_convert_fusion.meta, s32[2]{0:T(128)S(1)} %pad_add_fusion.here, f32[512,128]{1,0:T(8,128)S(1)} %get-tuple-element.68.row_scale, f32[512,128]{1,0:T(8,128)S(1)} %get-tuple-element.99.current.refs_0_, ...), custom_call_target="tpu_custom_call" | custom-call | tf_op jit(solution)/shard_map/pallas_call | solution.py:34
  81.7 2.0 %collective-permute-start.35 = (f32[128,128]{1,0:T(8,128)S(1)}, f32[128,128]{1,0:T(8,128)S(1)}, u32[]{:S(2)}, u32[]{:S(2)}) collective-permute-start(f32[128,128]{1,0:T(8,128)S(1)} %add.56), channel_id=1, source_target_pairs={{0,4},{1,5},{2,6},{3,7},{4,0},{5,1},{6,2},{7,3},{8,12},{9,13},{10,... | collective-permute-start | bytes 196616 | tf_op jit(solution)/shard_map/ppermute | solution.py:69
  90.1 3.7 %shard_map.72 = (f32[128,128]{1,0:T(8,128)S(1)}, f32[512,128]{1,0:T(8,128)S(1)}, f32[512,128]{1,0:T(8,128)S(1)}, f32[512,128]{1,0:T(8,128)S(1)}, f32[128,128]{1,0:T(8,128)S(1)}) custom-call(s32[2]{0:T(128)S(1)} %pad_add_fusion.here, f32[128,128]{1,0:T(8,128)S(1)} %add_add_fusion.1.mine, f32[128,128]{1,0:T(8,128)S(1)} %collective-permute-done.37.other, ...), custom_call_target="tpu_custom_call" | custom-call | tf_op jit(solution)/shard_map/pallas_call | solution.py:34
  96.2 3.6 %collective-permute-done.43.refs_14_ = bf16[512,128]{1,0:T(8,128)(2,1)S(1)} collective-permute-done((bf16[512,128]{1,0:T(8,128)(2,1)S(1)}, bf16[512,128]{1,0:T(8,128)(2,1)S(1)}, u32[]{:S(2)}, u32[]{:S(2)}) %collective-permute-start.43) | collective-permute-done | bytes 131104 | tf_op jit(solution)/shard_map/ppermute | solution.py:69
  101.2 2.8 %shard_map.76 = (f32[512,128]{1,0:T(8,128)S(1)}, f32[128,128]{1,0:T(8,128)S(1)}, f32[128,128]{1,0:T(8,128)S(1)}) custom-call(s32[68]{0:T(128)S(1)} %maximum_convert_fusion.meta, s32[2]{0:T(128)S(1)} %pad_add_fusion.here, f32[512,128]{1,0:T(8,128)S(1)} %get-tuple-element.68.row_scale, f32[512,128]{1,0:T(8,128)S(1)} %get-tuple-element.117.current, ...), custom_call_target="tpu_custom_call" | custom-call | tf_op jit(solution)/shard_map/pallas_call | solution.py:34
  106.0 1.9 %collective-permute-start.47 = (f32[128,128]{1,0:T(8,128)S(1)}, f32[128,128]{1,0:T(8,128)S(1)}, u32[]{:S(2)}, u32[]{:S(2)}) collective-permute-start(f32[128,128]{1,0:T(8,128)S(1)} %add.60), channel_id=1, source_target_pairs={{0,4},{1,5},{2,6},{3,7},{4,0},{5,1},{6,2},{7,3},{8,12},{9,13},{10,... | collective-permute-start | bytes 196616 | tf_op jit(solution)/shard_map/ppermute | solution.py:69
  109.0 2.3 %collective-permute-done.48 = f32[128,128]{1,0:T(8,128)S(1)} collective-permute-done((f32[128,128]{1,0:T(8,128)S(1)}, f32[128,128]{1,0:T(8,128)S(1)}, u32[]{:S(2)}, u32[]{:S(2)}) %collective-permute-start.48) | collective-permute-done | bytes 65568 | tf_op jit(solution)/shard_map/ppermute | solution.py:69
  113.6 5.0 %shard_map.77 = (f32[128,128]{1,0:T(8,128)}, f32[128,128]{1,0:T(8,128)}) custom-call(s32[2]{0:T(128)S(1)} %pad_add_fusion.here, f32[128,128]{1,0:T(8,128)S(1)} %add_add_fusion.mine, f32[128,128]{1,0:T(8,128)S(1)} %collective-permute-done.49.other, f32[512,128]{1,0:T(8,128)S(1)} %get-tuple-element.117.current, f32[512,128]{1,0:T(8,128)S(1)} %get-tuple-element.124.value, ...), custom_call_target="tpu_custom_call" | custom-call | tf_op jit(solution)/shard_map/pallas_call | solution.py:34
  (117 shorter events, 51.3 us)
Async XLA Ops:
  1.6 17.1 %collective-permute-start.4 = (bf16[1,1,4,128,128]{4,3,2,1,0:T(8,128)(2,1)S(1)}, bf16[1,1,4,128,128]{4,3,2,1,0:T(8,128)(2,1)S(1)}, u32[]{:S(2)}, u32[]{:S(2)}) collective-permute-start(bf16[1,1,4,128,128]{4,3,2,1,0:T(8,128)(2,1)S(1)} %slice.18.refs_0_), channel_id=1, source_target_pairs={{0,16},{8,24},{16,0},{24,8},{1,17},{9,25},{17,1},{25,9},{2,18},{10... | collective-permute-start | bytes 393224 | tf_op jit(solution)/shard_map/ppermute | solution.py:69
  5.7 13.0 %collective-permute-start.3 = (bf16[1,1,4,128,128]{4,3,2,1,0:T(8,128)(2,1)S(1)}, bf16[1,1,4,128,128]{4,3,2,1,0:T(8,128)(2,1)S(1)}, u32[]{:S(2)}, u32[]{:S(2)}) collective-permute-start(bf16[1,1,4,128,128]{4,3,2,1,0:T(8,128)(2,1)S(1)} %slice.18.refs_0_), channel_id=1, source_target_pairs={{0,8},{8,0},{16,24},{24,16},{1,9},{9,1},{17,25},{25,17},{2,10},{10... | collective-permute-start | bytes 393224 | tf_op jit(solution)/shard_map/ppermute | solution.py:69
  9.9 7.2 %collective-permute-start.2 = (f32[152,128]{1,0:T(8,128)S(1)}, f32[152,128]{1,0:T(8,128)S(1)}, u32[]{:S(2)}, u32[]{:S(2)}) collective-permute-start(f32[152,128]{1,0:T(8,128)S(1)} %shard_map.59.refs_0_), channel_id=1, source_target_pairs={{0,24},{8,16},{16,8},{24,0},{1,25},{9,17},{17,9},{25,1},{2,26},{10... | collective-permute-start | bytes 233480 | tf_op jit(solution)/shard_map/ppermute | solution.py:69
  10.0 8.7 %collective-permute-start.1 = (f32[152,128]{1,0:T(8,128)S(1)}, f32[152,128]{1,0:T(8,128)S(1)}, u32[]{:S(2)}, u32[]{:S(2)}) collective-permute-start(f32[152,128]{1,0:T(8,128)S(1)} %shard_map.59.refs_0_), channel_id=1, source_target_pairs={{0,16},{8,24},{16,0},{24,8},{1,17},{9,25},{17,1},{25,9},{2,18},{10... | collective-permute-start | bytes 233480 | tf_op jit(solution)/shard_map/ppermute | solution.py:69
  12.2 6.4 %collective-permute-start = (f32[152,128]{1,0:T(8,128)S(1)}, f32[152,128]{1,0:T(8,128)S(1)}, u32[]{:S(2)}, u32[]{:S(2)}) collective-permute-start(f32[152,128]{1,0:T(8,128)S(1)} %shard_map.59.refs_0_), channel_id=1, source_target_pairs={{0,8},{8,0},{16,24},{24,16},{1,9},{9,1},{17,25},{25,17},{2,10},{10... | collective-permute-start | bytes 233480 | tf_op jit(solution)/shard_map/ppermute | solution.py:69
  18.7 18.9 %collective-permute-start.10 = (bf16[1,1,12,128,128]{4,3,2,1,0:T(8,128)(2,1)S(1)}, bf16[1,1,12,128,128]{4,3,2,1,0:T(8,128)(2,1)S(1)}, u32[]{:S(2)}, u32[]{:S(2)}) collective-permute-start(bf16[1,1,12,128,128]{4,3,2,1,0:T(8,128)(2,1)S(1)} %slice.19.refs_1_), channel_id=1, source_target_pairs={{0,16},{8,24},{16,0},{24,8},{1,17},{9,25},{17,1},{25,9},{2,18},{10... | collective-permute-start | bytes 1179656 | tf_op jit(solution)/shard_map/ppermute | solution.py:69
  19.8 20.2 %collective-permute-start.9 = (bf16[1,1,12,128,128]{4,3,2,1,0:T(8,128)(2,1)S(1)}, bf16[1,1,12,128,128]{4,3,2,1,0:T(8,128)(2,1)S(1)}, u32[]{:S(2)}, u32[]{:S(2)}) collective-permute-start(bf16[1,1,12,128,128]{4,3,2,1,0:T(8,128)(2,1)S(1)} %slice.19.refs_1_), channel_id=1, source_target_pairs={{0,8},{8,0},{16,24},{24,16},{1,9},{9,1},{17,25},{25,17},{2,10},{10... | collective-permute-start | bytes 1179656 | tf_op jit(solution)/shard_map/ppermute | solution.py:69
  32.2 8.5 %collective-permute-start.11 = (f32[80,128]{1,0:T(8,128)S(1)}, f32[80,128]{1,0:T(8,128)S(1)}, u32[]{:S(2)}, u32[]{:S(2)}) collective-permute-start(f32[80,128]{1,0:T(8,128)S(1)} %add_add_fusion.3.mine), channel_id=1, source_target_pairs={{0,1},{1,0},{2,3},{3,2},{4,5},{5,4},{6,7},{7,6},{8,9},{9,8},{10,11... | collective-permute-start | bytes 122888 | tf_op jit(solution)/shard_map/ppermute | solution.py:69
  32.2 14.0 %collective-permute-start.17 = (f32[512,128]{1,0:T(8,128)S(1)}, f32[512,128]{1,0:T(8,128)S(1)}, u32[]{:S(2)}, u32[]{:S(2)}) collective-permute-start(f32[512,128]{1,0:T(8,128)S(1)} %get-tuple-element.77.piece.previous), channel_id=1, source_target_pairs={{0,4},{1,5},{2,6},{3,7},{4,0},{5,1},{6,2},{7,3},{8,12},{9,13},{10,... | collective-permute-start | bytes 786440 | tf_op jit(solution)/shard_map/ppermute | solution.py:69
  33.8 13.4 %collective-permute-start.15 = (f32[512,128]{1,0:T(8,128)S(1)}, f32[512,128]{1,0:T(8,128)S(1)}, u32[]{:S(2)}, u32[]{:S(2)}) collective-permute-start(f32[512,128]{1,0:T(8,128)S(1)} %get-tuple-element.77.piece.previous), channel_id=1, source_target_pairs={{0,2},{1,3},{2,0},{3,1},{4,6},{5,7},{6,4},{7,5},{8,10},{9,11},{10,... | collective-permute-start | bytes 786440 | tf_op jit(solution)/shard_map/ppermute | solution.py:69
  37.6 11.2 %collective-permute-start.19 = (f32[512,128]{1,0:T(8,128)S(1)}, f32[512,128]{1,0:T(8,128)S(1)}, u32[]{:S(2)}, u32[]{:S(2)}) collective-permute-start(f32[512,128]{1,0:T(8,128)S(1)} %get-tuple-element.77.piece.previous), channel_id=1, source_target_pairs={{0,6},{1,7},{2,4},{3,5},{4,2},{5,3},{6,0},{7,1},{8,14},{9,15},{10,... | collective-permute-start | bytes 786440 | tf_op jit(solution)/shard_map/ppermute | solution.py:69
  40.0 10.4 %collective-permute-start.12 = (bf16[1,1,4,128,128]{4,3,2,1,0:T(8,128)(2,1)S(1)}, bf16[1,1,4,128,128]{4,3,2,1,0:T(8,128)(2,1)S(1)}, u32[]{:S(2)}, u32[]{:S(2)}) collective-permute-start(bf16[1,1,4,128,128]{4,3,2,1,0:T(8,128)(2,1)S(1)} %collective-permute-done.4.refs_4_), channel_id=1, source_target_pairs={{0,8},{8,0},{16,24},{24,16},{1,9},{9,1},{17,25},{25,17},{2,10},{10... | collective-permute-start | bytes 393224 | tf_op jit(solution)/shard_map/ppermute | solution.py:69
  40.7 11.9 %collective-permute-start.13 = (bf16[1,1,12,128,128]{4,3,2,1,0:T(8,128)(2,1)S(1)}, bf16[1,1,12,128,128]{4,3,2,1,0:T(8,128)(2,1)S(1)}, u32[]{:S(2)}, u32[]{:S(2)}) collective-permute-start(bf16[1,1,12,128,128]{4,3,2,1,0:T(8,128)(2,1)S(1)} %collective-permute-done.10.refs_5_), channel_id=1, source_target_pairs={{0,8},{8,0},{16,24},{24,16},{1,9},{9,1},{17,25},{25,17},{2,10},{10... | collective-permute-start | bytes 1179656 | tf_op jit(solution)/shard_map/ppermute | solution.py:69
  56.7 5.7 %collective-permute-start.24 = (f32[128,128]{1,0:T(8,128)S(1)}, f32[128,128]{1,0:T(8,128)S(1)}, u32[]{:S(2)}, u32[]{:S(2)}) collective-permute-start(f32[128,128]{1,0:T(8,128)S(1)} %add.52), channel_id=1, source_target_pairs={{0,6},{1,7},{2,4},{3,5},{4,2},{5,3},{6,0},{7,1},{8,14},{9,15},{10,... | collective-permute-start | bytes 196616 | tf_op jit(solution)/shard_map/ppermute | solution.py:69
  57.9 5.5 %collective-permute-start.23 = (f32[128,128]{1,0:T(8,128)S(1)}, f32[128,128]{1,0:T(8,128)S(1)}, u32[]{:S(2)}, u32[]{:S(2)}) collective-permute-start(f32[128,128]{1,0:T(8,128)S(1)} %add.52), channel_id=1, source_target_pairs={{0,4},{1,5},{2,6},{3,7},{4,0},{5,1},{6,2},{7,3},{8,12},{9,13},{10,... | collective-permute-start | bytes 196616 | tf_op jit(solution)/shard_map/ppermute | solution.py:69
  60.3 9.0 %collective-permute-start.29 = (f32[512,128]{1,0:T(8,128)S(1)}, f32[512,128]{1,0:T(8,128)S(1)}, u32[]{:S(2)}, u32[]{:S(2)}) collective-permute-start(f32[512,128]{1,0:T(8,128)S(1)} %get-tuple-element.97.value), channel_id=1, source_target_pairs={{0,4},{1,5},{2,6},{3,7},{4,0},{5,1},{6,2},{7,3},{8,12},{9,13},{10,... | collective-permute-start | bytes 786440 | tf_op jit(solution)/shard_map/ppermute | solution.py:69
  60.8 10.9 %collective-permute-start.27 = (f32[512,128]{1,0:T(8,128)S(1)}, f32[512,128]{1,0:T(8,128)S(1)}, u32[]{:S(2)}, u32[]{:S(2)}) collective-permute-start(f32[512,128]{1,0:T(8,128)S(1)} %get-tuple-element.97.value), channel_id=1, source_target_pairs={{0,2},{1,3},{2,0},{3,1},{4,6},{5,7},{6,4},{7,5},{8,10},{9,11},{10,... | collective-permute-start | bytes 786440 | tf_op jit(solution)/shard_map/ppermute | solution.py:69
  69.7 5.6 %collective-permute-start.31 = (bf16[512,128]{1,0:T(8,128)(2,1)S(1)}, bf16[512,128]{1,0:T(8,128)(2,1)S(1)}, u32[]{:S(2)}, u32[]{:S(2)}) collective-permute-start(bf16[512,128]{1,0:T(8,128)(2,1)S(1)} %get-tuple-element.107.refs_12_), channel_id=1, source_target_pairs={{0,2},{1,3},{2,0},{3,1},{4,6},{5,7},{6,4},{7,5},{8,10},{9,11},{10,... | collective-permute-start | bytes 393224 | tf_op jit(solution)/shard_map/ppermute | solution.py:69
  80.7 5.5 %collective-permute-start.36 = (f32[128,128]{1,0:T(8,128)S(1)}, f32[128,128]{1,0:T(8,128)S(1)}, u32[]{:S(2)}, u32[]{:S(2)}) collective-permute-start(f32[128,128]{1,0:T(8,128)S(1)} %add.56), channel_id=1, source_target_pairs={{0,6},{1,7},{2,4},{3,5},{4,2},{5,3},{6,0},{7,1},{8,14},{9,15},{10,... | collective-permute-start | bytes 196616 | tf_op jit(solution)/shard_map/ppermute | solution.py:69
  81.7 5.6 %collective-permute-start.35 = (f32[128,128]{1,0:T(8,128)S(1)}, f32[128,128]{1,0:T(8,128)S(1)}, u32[]{:S(2)}, u32[]{:S(2)}) collective-permute-start(f32[128,128]{1,0:T(8,128)S(1)} %add.56), channel_id=1, source_target_pairs={{0,4},{1,5},{2,6},{3,7},{4,0},{5,1},{6,2},{7,3},{8,12},{9,13},{10,... | collective-permute-start | bytes 196616 | tf_op jit(solution)/shard_map/ppermute | solution.py:69
  84.2 9.6 %collective-permute-start.41 = (f32[512,128]{1,0:T(8,128)S(1)}, f32[512,128]{1,0:T(8,128)S(1)}, u32[]{:S(2)}, u32[]{:S(2)}) collective-permute-start(f32[512,128]{1,0:T(8,128)S(1)} %get-tuple-element.116.value), channel_id=1, source_target_pairs={{0,4},{1,5},{2,6},{3,7},{4,0},{5,1},{6,2},{7,3},{8,12},{9,13},{10,... | collective-permute-start | bytes 786440 | tf_op jit(solution)/shard_map/ppermute | solution.py:69
  84.4 11.3 %collective-permute-start.39 = (f32[512,128]{1,0:T(8,128)S(1)}, f32[512,128]{1,0:T(8,128)S(1)}, u32[]{:S(2)}, u32[]{:S(2)}) collective-permute-start(f32[512,128]{1,0:T(8,128)S(1)} %get-tuple-element.116.value), channel_id=1, source_target_pairs={{0,2},{1,3},{2,0},{3,1},{4,6},{5,7},{6,4},{7,5},{8,10},{9,11},{10,... | collective-permute-start | bytes 786440 | tf_op jit(solution)/shard_map/ppermute | solution.py:69
  94.2 5.6 %collective-permute-start.43 = (bf16[512,128]{1,0:T(8,128)(2,1)S(1)}, bf16[512,128]{1,0:T(8,128)(2,1)S(1)}, u32[]{:S(2)}, u32[]{:S(2)}) collective-permute-start(bf16[512,128]{1,0:T(8,128)(2,1)S(1)} %shard_map.75.refs_12_), channel_id=1, source_target_pairs={{0,2},{1,3},{2,0},{3,1},{4,6},{5,7},{6,4},{7,5},{8,10},{9,11},{10,... | collective-permute-start | bytes 393224 | tf_op jit(solution)/shard_map/ppermute | solution.py:69
  105.4 5.9 %collective-permute-start.48 = (f32[128,128]{1,0:T(8,128)S(1)}, f32[128,128]{1,0:T(8,128)S(1)}, u32[]{:S(2)}, u32[]{:S(2)}) collective-permute-start(f32[128,128]{1,0:T(8,128)S(1)} %add.60), channel_id=1, source_target_pairs={{0,6},{1,7},{2,4},{3,5},{4,2},{5,3},{6,0},{7,1},{8,14},{9,15},{10,... | collective-permute-start | bytes 196616 | tf_op jit(solution)/shard_map/ppermute | solution.py:69
  (30 other events, 98.8 us)

commit v5 on v4

--- a/solution.py
+++ b/solution.py
@@ -231,17 +231,18 @@
     high = jnp.concatenate([half[edge // 2 : edge, :], half[edge + part :, :]], axis=0)
     keep[...] = jnp.where(core == 0, low, high)
     send[...] = jnp.where(core == 0, high, low)
-    scale = inverse_fourth_root(row_energy)
-    for u in range(n_row):
-        row_scale[u * edge : (u + 1) * edge, :] = down_rows(scale[u : u + 1, :], edge)
+    down_rows(inverse_fourth_root(row_energy), row_scale)
 
 
 def inverse_fourth_root(energy):
     return 1.0 / jnp.sqrt(jnp.sqrt(energy + EPSILON))
 
 
-def down_rows(row, edge):
-    return jnp.transpose(jnp.broadcast_to(row, (edge, edge)))
+def down_rows(scales, out):
+    edge = scales.shape[1]
+    columns = jnp.transpose(scales)
+    for u in range(out.shape[0] // edge):
+        out[u * edge : (u + 1) * edge, :] = jnp.broadcast_to(columns[:, u : u + 1], (edge, edge))
 
 
 def halves(here, mine, other):
@@ -259,14 +260,15 @@
     inverse[...] = factor(gram)[1]
 
 
-def first_update_kernel(sizes, distance, here, inverse, energy, piece, new, scaled, col_scale):
+def first_update_kernel(sizes, distance, here, inverse, energy, piece, scaled, col_scale, *new):
     edge, n_row, n_col = sizes
-    for u in range(n_row):
-        row = energy[pl.ds(u * n_col + (here[1] ^ distance), 1), :]
-        col_scale[u * edge : (u + 1) * edge, :] = down_rows(inverse_fourth_root(row), edge)
+    rows = [energy[pl.ds(u * n_col + (here[1] ^ distance), 1), :] for u in range(n_row)]
+    rows += rows[:1] * (-n_row % SUB)
+    down_rows(inverse_fourth_root(jnp.concatenate(rows, axis=0)), col_scale)
     value = dot(piece[...], inverse[...], ((1,), (1,)))
-    new[...] = value
     scaled[...] = (col_scale[...] * value).astype(BF16)
+    if new:
+        new[0][...] = value
 
 
 def apply_kernel(sizes, first, meta, here, row_scale, current, previous, *refs):
@@ -418,16 +420,17 @@
         [square, ((n_row * n_col, columns), F32)],
         inputs=3,
     )(here, mine, other)
-    firsts = [
-        call(
-            functools.partial(first_update_kernel, (edge, n_row, n_col), distance),
-            [block, piece_rows, block],
+    firsts = {
+        k: call(
+            functools.partial(first_update_kernel, (edge, n_row, n_col), k),
+            [piece_rows, block, block] if k in near else [piece_rows],
+            [] if k in near else [pltpu.VMEM(*block)],
             inputs=4,
         )(here, inverse, energy, piece)
-        for distance, piece in zip(everywhere, pieces)
-    ]
-    scaled = {k: f[1] for k, f in zip(everywhere, firsts)}
-    currents, _, col_scales = zip(*[f for k, f in zip(everywhere, firsts) if k in near])
+        for k, piece in zip(everywhere, pieces)
+    }
+    scaled = {k: f[0] for k, f in firsts.items()}
+    col_scales, currents = zip(*[firsts[k][1:] for k in near])
     previous = basis
     for iteration in range(ITERS):
         first, final = iteration == 0, iteration == ITERS - 1

time: 119 us -> 119 us (level)
  starting transfers between devices: 42.9 us -> 44.1 us
    ppermute x50, starting transfers between devices: 42.9 us -> 44.1 us  [swap(): return lax.ppermute(value, axis, [(i, i ^ distance) for i in range(size)])]
  transfers between devices with their start and end apart: 50 -> 50, of which waited for: 29 -> 28; matrix products, arithmetic and copies ran while one was open for 0% -> 0% of each run, Pallas kernels for 16% -> 16%
where the time goes in v5:
time: 119 us
  starting transfers between devices  44.1 us (37%)
  waiting for transfers between devices  39.4 us (33%)
  Pallas kernels  31.4 us (26%)
  local copies, waits for them, and re-layouts  2.03 us (2%)
  between operations  1.62 us (1%)
    ppermute x50, starting transfers between devices, swap(): return lax.ppermute(value, axis, [(i, i ^ distance) for i in range(size)])  44.1 us
    ppermute x50, waiting for transfers between devices, swap(): return lax.ppermute(value, axis, [(i, i ^ distance) for i in range(size)])  39.4 us
    pallas_call x19, Pallas kernels, run(): pl.pallas_call(body, out_shape=[jax.ShapeDtypeStruct(shape, dtype) for sh...  31.4 us
  transfers between devices with their start and end apart: 50, of which 28 were waited for; matrix products, arithmetic and copies ran while one was open for 0% of the time, Pallas kernels for 16%

profile of v5, /device:TPU:0, one launch (start us, length us, event | category | flops | bytes accessed | tf_op | source)
XLA Modules:
  0.0 118.9 jit_solution(16193313092558231468)
XLA Ops:
  1.6 4.1 %collective-permute-start.4 = (bf16[1,1,4,128,128]{4,3,2,1,0:T(8,128)(2,1)S(1)}, bf16[1,1,4,128,128]{4,3,2,1,0:T(8,128)(2,1)S(1)}, u32[]{:S(2)}, u32[]{:S(2)}) collective-permute-start(bf16[1,1,4,128,128]{4,3,2,1,0:T(8,128)(2,1)S(1)} %slice.18.refs_0_), channel_id=1, source_target_pairs={{0,16},{8,24},{16,0},{24,8},{1,17},{9,25},{17,1},{25,9},{2,18},{10... | collective-permute-start | bytes 393224 | tf_op jit(solution)/shard_map/ppermute | solution.py:69
  5.7 1.6 %collective-permute-start.3 = (bf16[1,1,4,128,128]{4,3,2,1,0:T(8,128)(2,1)S(1)}, bf16[1,1,4,128,128]{4,3,2,1,0:T(8,128)(2,1)S(1)}, u32[]{:S(2)}, u32[]{:S(2)}) collective-permute-start(bf16[1,1,4,128,128]{4,3,2,1,0:T(8,128)(2,1)S(1)} %slice.18.refs_0_), channel_id=1, source_target_pairs={{0,8},{8,0},{16,24},{24,16},{1,9},{9,1},{17,25},{25,17},{2,10},{10... | collective-permute-start | bytes 393224 | tf_op jit(solution)/shard_map/ppermute | solution.py:69
  10.3 1.9 %collective-permute-start.1 = (f32[152,128]{1,0:T(8,128)S(1)}, f32[152,128]{1,0:T(8,128)S(1)}, u32[]{:S(2)}, u32[]{:S(2)}) collective-permute-start(f32[152,128]{1,0:T(8,128)S(1)} %shard_map.59.refs_0_), channel_id=1, source_target_pairs={{0,16},{8,24},{16,0},{24,8},{1,17},{9,25},{17,1},{25,9},{2,18},{10... | collective-permute-start | bytes 233480 | tf_op jit(solution)/shard_map/ppermute | solution.py:69
  12.2 2.1 %collective-permute-start = (f32[152,128]{1,0:T(8,128)S(1)}, f32[152,128]{1,0:T(8,128)S(1)}, u32[]{:S(2)}, u32[]{:S(2)}) collective-permute-start(f32[152,128]{1,0:T(8,128)S(1)} %shard_map.59.refs_0_), channel_id=1, source_target_pairs={{0,8},{8,0},{16,24},{24,16},{1,9},{9,1},{17,25},{25,17},{2,10},{10... | collective-permute-start | bytes 233480 | tf_op jit(solution)/shard_map/ppermute | solution.py:69
  14.4 2.6 %collective-permute-done.2.refs_3_ = f32[152,128]{1,0:T(8,128)S(1)} collective-permute-done((f32[152,128]{1,0:T(8,128)S(1)}, f32[152,128]{1,0:T(8,128)S(1)}, u32[]{:S(2)}, u32[]{:S(2)}) %collective-permute-start.2) | collective-permute-done | bytes 77856 | tf_op jit(solution)/shard_map/ppermute | solution.py:69
  17.0 2.6 %collective-permute-done.1.refs_2_ = f32[152,128]{1,0:T(8,128)S(1)} collective-permute-done((f32[152,128]{1,0:T(8,128)S(1)}, f32[152,128]{1,0:T(8,128)S(1)}, u32[]{:S(2)}, u32[]{:S(2)}) %collective-permute-start.1) | collective-permute-done | bytes 77856 | tf_op jit(solution)/shard_map/ppermute | solution.py:69
  20.0 2.9 %collective-permute-start.9 = (bf16[1,1,12,128,128]{4,3,2,1,0:T(8,128)(2,1)S(1)}, bf16[1,1,12,128,128]{4,3,2,1,0:T(8,128)(2,1)S(1)}, u32[]{:S(2)}, u32[]{:S(2)}) collective-permute-start(bf16[1,1,12,128,128]{4,3,2,1,0:T(8,128)(2,1)S(1)} %slice.19.refs_1_), channel_id=1, source_target_pairs={{0,8},{8,0},{16,24},{24,16},{1,9},{9,1},{17,25},{25,17},{2,10},{10... | collective-permute-start | bytes 1179656 | tf_op jit(solution)/shard_map/ppermute | solution.py:69
  25.2 2.4 %collective-permute-start.8 = (f32[80,128]{1,0:T(8,128)S(1)}, f32[80,128]{1,0:T(8,128)S(1)}, u32[]{:S(2)}, u32[]{:S(2)}) collective-permute-start(f32[80,128]{1,0:T(8,128)S(1)} %add.48), channel_id=1, source_target_pairs={{0,6},{1,7},{2,4},{3,5},{4,2},{5,3},{6,0},{7,1},{8,14},{9,15},{10,... | collective-permute-start | bytes 122888 | tf_op jit(solution)/shard_map/ppermute | solution.py:69
  30.1 1.5 %collective-permute-done.7 = f32[80,128]{1,0:T(8,128)S(1)} collective-permute-done((f32[80,128]{1,0:T(8,128)S(1)}, f32[80,128]{1,0:T(8,128)S(1)}, u32[]{:S(2)}, u32[]{:S(2)}) %collective-permute-start.7) | collective-permute-done | bytes 40992 | tf_op jit(solution)/shard_map/ppermute | solution.py:69
  32.3 1.6 %collective-permute-start.19 = (f32[512,128]{1,0:T(8,128)S(1)}, f32[512,128]{1,0:T(8,128)S(1)}, u32[]{:S(2)}, u32[]{:S(2)}) collective-permute-start(f32[512,128]{1,0:T(8,128)S(1)} %get-tuple-element.76.piece.previous), channel_id=1, source_target_pairs={{0,6},{1,7},{2,4},{3,5},{4,2},{5,3},{6,0},{7,1},{8,14},{9,15},{10,... | collective-permute-start | bytes 786440 | tf_op jit(solution)/shard_map/ppermute | solution.py:69
  34.4 4.7 %collective-permute-done.10.refs_5_ = bf16[1,1,12,128,128]{4,3,2,1,0:T(8,128)(2,1)S(1)} collective-permute-done((bf16[1,1,12,128,128]{4,3,2,1,0:T(8,128)(2,1)S(1)}, bf16[1,1,12,128,128]{4,3,2,1,0:T(8,128)(2,1)S(1)}, u32[]{:S(2)}, u32[]{:S(2)}) %collective-permute-start.10) | collective-permute-done | bytes 393248 | tf_op jit(solution)/shard_map/ppermute | solution.py:69
  41.1 3.2 %shard_map.61 = (f32[128,128]{1,0:T(8,128)S(1)}, f32[32,128]{1,0:T(8,128)S(1)}) custom-call(s32[2]{0:T(128)S(1)} %pad_add_fusion.here, f32[80,128]{1,0:T(8,128)S(1)} %add_add_fusion.3.mine, f32[80,128]{1,0:T(8,128)S(1)} %collective-permute-done.11.other), custom_call_target="tpu_custom_call" | custom-call | tf_op jit(solution)/shard_map/pallas_call | solution.py:34
  51.7 2.6 %shard_map.66 = (f32[512,128]{1,0:T(8,128)S(1)}, f32[128,128]{1,0:T(8,128)S(1)}, f32[128,128]{1,0:T(8,128)S(1)}) custom-call(s32[68]{0:T(128)S(1)} %maximum_convert_fusion.meta, s32[2]{0:T(128)S(1)} %pad_add_fusion.here, f32[512,128]{1,0:T(8,128)S(1)} %get-tuple-element.67.row_scale, f32[512,128]{1,0:T(8,128)S(1)} %get-tuple-element.77.current.refs_0_, ...), custom_call_target="tpu_custom_call" | custom-call | tf_op jit(solution)/shard_map/pallas_call | solution.py:34
  55.6 3.6 %collective-permute-start.24 = (f32[128,128]{1,0:T(8,128)S(1)}, f32[128,128]{1,0:T(8,128)S(1)}, u32[]{:S(2)}, u32[]{:S(2)}) collective-permute-start(f32[128,128]{1,0:T(8,128)S(1)} %add.52), channel_id=1, source_target_pairs={{0,6},{1,7},{2,4},{3,5},{4,2},{5,3},{6,0},{7,1},{8,14},{9,15},{10,... | collective-permute-start | bytes 196616 | tf_op jit(solution)/shard_map/ppermute | solution.py:69
  61.4 1.9 %collective-permute-start.27 = (f32[512,128]{1,0:T(8,128)S(1)}, f32[512,128]{1,0:T(8,128)S(1)}, u32[]{:S(2)}, u32[]{:S(2)}) collective-permute-start(f32[512,128]{1,0:T(8,128)S(1)} %get-tuple-element.95.value), channel_id=1, source_target_pairs={{0,2},{1,3},{2,0},{3,1},{4,6},{5,7},{6,4},{7,5},{8,10},{9,11},{10,... | collective-permute-start | bytes 786440 | tf_op jit(solution)/shard_map/ppermute | solution.py:69
  66.0 3.7 %shard_map.67 = (f32[128,128]{1,0:T(8,128)S(1)}, f32[512,128]{1,0:T(8,128)S(1)}, f32[512,128]{1,0:T(8,128)S(1)}, f32[512,128]{1,0:T(8,128)S(1)}) custom-call(s32[2]{0:T(128)S(1)} %pad_add_fusion.here, f32[128,128]{1,0:T(8,128)S(1)} %add_add_fusion.2.mine, f32[128,128]{1,0:T(8,128)S(1)} %collective-permute-done.25.other, ...), custom_call_target="tpu_custom_call" | custom-call | tf_op jit(solution)/shard_map/pallas_call | solution.py:34
  72.2 3.5 %collective-permute-done.31.refs_14_ = bf16[512,128]{1,0:T(8,128)(2,1)S(1)} collective-permute-done((bf16[512,128]{1,0:T(8,128)(2,1)S(1)}, bf16[512,128]{1,0:T(8,128)(2,1)S(1)}, u32[]{:S(2)}, u32[]{:S(2)}) %collective-permute-start.31) | collective-permute-done | bytes 131104 | tf_op jit(solution)/shard_map/ppermute | solution.py:69
  77.0 2.4 %shard_map.71 = (f32[512,128]{1,0:T(8,128)S(1)}, f32[128,128]{1,0:T(8,128)S(1)}, f32[128,128]{1,0:T(8,128)S(1)}) custom-call(s32[68]{0:T(128)S(1)} %maximum_convert_fusion.meta, s32[2]{0:T(128)S(1)} %pad_add_fusion.here, f32[512,128]{1,0:T(8,128)S(1)} %get-tuple-element.67.row_scale, f32[512,128]{1,0:T(8,128)S(1)} %get-tuple-element.97.current.refs_0_, ...), custom_call_target="tpu_custom_call" | custom-call | tf_op jit(solution)/shard_map/pallas_call | solution.py:34
  89.2 3.7 %shard_map.72 = (f32[128,128]{1,0:T(8,128)S(1)}, f32[512,128]{1,0:T(8,128)S(1)}, f32[512,128]{1,0:T(8,128)S(1)}, f32[512,128]{1,0:T(8,128)S(1)}, f32[128,128]{1,0:T(8,128)S(1)}) custom-call(s32[2]{0:T(128)S(1)} %pad_add_fusion.here, f32[128,128]{1,0:T(8,128)S(1)} %add_add_fusion.1.mine, f32[128,128]{1,0:T(8,128)S(1)} %collective-permute-done.37.other, ...), custom_call_target="tpu_custom_call" | custom-call | tf_op jit(solution)/shard_map/pallas_call | solution.py:34
  96.5 2.4 %collective-permute-done.43.refs_14_ = bf16[512,128]{1,0:T(8,128)(2,1)S(1)} collective-permute-done((bf16[512,128]{1,0:T(8,128)(2,1)S(1)}, bf16[512,128]{1,0:T(8,128)(2,1)S(1)}, u32[]{:S(2)}, u32[]{:S(2)}) %collective-permute-start.43) | collective-permute-done | bytes 131104 | tf_op jit(solution)/shard_map/ppermute | solution.py:69
  100.3 2.7 %shard_map.76 = (f32[512,128]{1,0:T(8,128)S(1)}, f32[128,128]{1,0:T(8,128)S(1)}, f32[128,128]{1,0:T(8,128)S(1)}) custom-call(s32[68]{0:T(128)S(1)} %maximum_convert_fusion.meta, s32[2]{0:T(128)S(1)} %pad_add_fusion.here, f32[512,128]{1,0:T(8,128)S(1)} %get-tuple-element.67.row_scale, f32[512,128]{1,0:T(8,128)S(1)} %get-tuple-element.115.current, ...), custom_call_target="tpu_custom_call" | custom-call | tf_op jit(solution)/shard_map/pallas_call | solution.py:34
  104.5 2.7 %collective-permute-start.48 = (f32[128,128]{1,0:T(8,128)S(1)}, f32[128,128]{1,0:T(8,128)S(1)}, u32[]{:S(2)}, u32[]{:S(2)}) collective-permute-start(f32[128,128]{1,0:T(8,128)S(1)} %add.60), channel_id=1, source_target_pairs={{0,6},{1,7},{2,4},{3,5},{4,2},{5,3},{6,0},{7,1},{8,14},{9,15},{10,... | collective-permute-start | bytes 196616 | tf_op jit(solution)/shard_map/ppermute | solution.py:69
  109.8 1.6 %collective-permute-done.47 = f32[128,128]{1,0:T(8,128)S(1)} collective-permute-done((f32[128,128]{1,0:T(8,128)S(1)}, f32[128,128]{1,0:T(8,128)S(1)}, u32[]{:S(2)}, u32[]{:S(2)}) %collective-permute-start.47) | collective-permute-done | bytes 65568 | tf_op jit(solution)/shard_map/ppermute | solution.py:69
  113.8 5.0 %shard_map.77 = (f32[128,128]{1,0:T(8,128)}, f32[128,128]{1,0:T(8,128)}) custom-call(s32[2]{0:T(128)S(1)} %pad_add_fusion.here, f32[128,128]{1,0:T(8,128)S(1)} %add_add_fusion.mine, f32[128,128]{1,0:T(8,128)S(1)} %collective-permute-done.49.other, f32[512,128]{1,0:T(8,128)S(1)} %get-tuple-element.115.current, f32[512,128]{1,0:T(8,128)S(1)} %get-tuple-element.122.value, ...), custom_call_target="tpu_custom_call" | custom-call | tf_op jit(solution)/shard_map/pallas_call | solution.py:34
  (117 shorter events, 50.1 us)
Async XLA Ops:
  1.6 18.0 %collective-permute-start.4 = (bf16[1,1,4,128,128]{4,3,2,1,0:T(8,128)(2,1)S(1)}, bf16[1,1,4,128,128]{4,3,2,1,0:T(8,128)(2,1)S(1)}, u32[]{:S(2)}, u32[]{:S(2)}) collective-permute-start(bf16[1,1,4,128,128]{4,3,2,1,0:T(8,128)(2,1)S(1)} %slice.18.refs_0_), channel_id=1, source_target_pairs={{0,16},{8,24},{16,0},{24,8},{1,17},{9,25},{17,1},{25,9},{2,18},{10... | collective-permute-start | bytes 393224 | tf_op jit(solution)/shard_map/ppermute | solution.py:69
  5.7 13.9 %collective-permute-start.3 = (bf16[1,1,4,128,128]{4,3,2,1,0:T(8,128)(2,1)S(1)}, bf16[1,1,4,128,128]{4,3,2,1,0:T(8,128)(2,1)S(1)}, u32[]{:S(2)}, u32[]{:S(2)}) collective-permute-start(bf16[1,1,4,128,128]{4,3,2,1,0:T(8,128)(2,1)S(1)} %slice.18.refs_0_), channel_id=1, source_target_pairs={{0,8},{8,0},{16,24},{24,16},{1,9},{9,1},{17,25},{25,17},{2,10},{10... | collective-permute-start | bytes 393224 | tf_op jit(solution)/shard_map/ppermute | solution.py:69
  9.9 7.1 %collective-permute-start.2 = (f32[152,128]{1,0:T(8,128)S(1)}, f32[152,128]{1,0:T(8,128)S(1)}, u32[]{:S(2)}, u32[]{:S(2)}) collective-permute-start(f32[152,128]{1,0:T(8,128)S(1)} %shard_map.59.refs_0_), channel_id=1, source_target_pairs={{0,24},{8,16},{16,8},{24,0},{1,25},{9,17},{17,9},{25,1},{2,26},{10... | collective-permute-start | bytes 233480 | tf_op jit(solution)/shard_map/ppermute | solution.py:69
  10.3 9.3 %collective-permute-start.1 = (f32[152,128]{1,0:T(8,128)S(1)}, f32[152,128]{1,0:T(8,128)S(1)}, u32[]{:S(2)}, u32[]{:S(2)}) collective-permute-start(f32[152,128]{1,0:T(8,128)S(1)} %shard_map.59.refs_0_), channel_id=1, source_target_pairs={{0,16},{8,24},{16,0},{24,8},{1,17},{9,25},{17,1},{25,9},{2,18},{10... | collective-permute-start | bytes 233480 | tf_op jit(solution)/shard_map/ppermute | solution.py:69
  12.2 7.3 %collective-permute-start = (f32[152,128]{1,0:T(8,128)S(1)}, f32[152,128]{1,0:T(8,128)S(1)}, u32[]{:S(2)}, u32[]{:S(2)}) collective-permute-start(f32[152,128]{1,0:T(8,128)S(1)} %shard_map.59.refs_0_), channel_id=1, source_target_pairs={{0,8},{8,0},{16,24},{24,16},{1,9},{9,1},{17,25},{25,17},{2,10},{10... | collective-permute-start | bytes 233480 | tf_op jit(solution)/shard_map/ppermute | solution.py:69
  19.6 19.5 %collective-permute-start.10 = (bf16[1,1,12,128,128]{4,3,2,1,0:T(8,128)(2,1)S(1)}, bf16[1,1,12,128,128]{4,3,2,1,0:T(8,128)(2,1)S(1)}, u32[]{:S(2)}, u32[]{:S(2)}) collective-permute-start(bf16[1,1,12,128,128]{4,3,2,1,0:T(8,128)(2,1)S(1)} %slice.19.refs_1_), channel_id=1, source_target_pairs={{0,16},{8,24},{16,0},{24,8},{1,17},{9,25},{17,1},{25,9},{2,18},{10... | collective-permute-start | bytes 1179656 | tf_op jit(solution)/shard_map/ppermute | solution.py:69
  20.0 19.2 %collective-permute-start.9 = (bf16[1,1,12,128,128]{4,3,2,1,0:T(8,128)(2,1)S(1)}, bf16[1,1,12,128,128]{4,3,2,1,0:T(8,128)(2,1)S(1)}, u32[]{:S(2)}, u32[]{:S(2)}) collective-permute-start(bf16[1,1,12,128,128]{4,3,2,1,0:T(8,128)(2,1)S(1)} %slice.19.refs_1_), channel_id=1, source_target_pairs={{0,8},{8,0},{16,24},{24,16},{1,9},{9,1},{17,25},{25,17},{2,10},{10... | collective-permute-start | bytes 1179656 | tf_op jit(solution)/shard_map/ppermute | solution.py:69
  32.2 7.5 %collective-permute-start.11 = (f32[80,128]{1,0:T(8,128)S(1)}, f32[80,128]{1,0:T(8,128)S(1)}, u32[]{:S(2)}, u32[]{:S(2)}) collective-permute-start(f32[80,128]{1,0:T(8,128)S(1)} %add_add_fusion.3.mine), channel_id=1, source_target_pairs={{0,1},{1,0},{2,3},{3,2},{4,5},{5,4},{6,7},{7,6},{8,9},{9,8},{10,11... | collective-permute-start | bytes 122888 | tf_op jit(solution)/shard_map/ppermute | solution.py:69
  32.3 13.0 %collective-permute-start.19 = (f32[512,128]{1,0:T(8,128)S(1)}, f32[512,128]{1,0:T(8,128)S(1)}, u32[]{:S(2)}, u32[]{:S(2)}) collective-permute-start(f32[512,128]{1,0:T(8,128)S(1)} %get-tuple-element.76.piece.previous), channel_id=1, source_target_pairs={{0,6},{1,7},{2,4},{3,5},{4,2},{5,3},{6,0},{7,1},{8,14},{9,15},{10,... | collective-permute-start | bytes 786440 | tf_op jit(solution)/shard_map/ppermute | solution.py:69
  33.8 13.7 %collective-permute-start.17 = (f32[512,128]{1,0:T(8,128)S(1)}, f32[512,128]{1,0:T(8,128)S(1)}, u32[]{:S(2)}, u32[]{:S(2)}) collective-permute-start(f32[512,128]{1,0:T(8,128)S(1)} %get-tuple-element.76.piece.previous), channel_id=1, source_target_pairs={{0,4},{1,5},{2,6},{3,7},{4,0},{5,1},{6,2},{7,3},{8,12},{9,13},{10,... | collective-permute-start | bytes 786440 | tf_op jit(solution)/shard_map/ppermute | solution.py:69
  39.0 9.5 %collective-permute-start.15 = (f32[512,128]{1,0:T(8,128)S(1)}, f32[512,128]{1,0:T(8,128)S(1)}, u32[]{:S(2)}, u32[]{:S(2)}) collective-permute-start(f32[512,128]{1,0:T(8,128)S(1)} %get-tuple-element.76.piece.previous), channel_id=1, source_target_pairs={{0,2},{1,3},{2,0},{3,1},{4,6},{5,7},{6,4},{7,5},{8,10},{9,11},{10,... | collective-permute-start | bytes 786440 | tf_op jit(solution)/shard_map/ppermute | solution.py:69
  39.1 11.0 %collective-permute-start.12 = (bf16[1,1,4,128,128]{4,3,2,1,0:T(8,128)(2,1)S(1)}, bf16[1,1,4,128,128]{4,3,2,1,0:T(8,128)(2,1)S(1)}, u32[]{:S(2)}, u32[]{:S(2)}) collective-permute-start(bf16[1,1,4,128,128]{4,3,2,1,0:T(8,128)(2,1)S(1)} %collective-permute-done.4.refs_4_), channel_id=1, source_target_pairs={{0,8},{8,0},{16,24},{24,16},{1,9},{9,1},{17,25},{25,17},{2,10},{10... | collective-permute-start | bytes 393224 | tf_op jit(solution)/shard_map/ppermute | solution.py:69
  39.7 11.9 %collective-permute-start.13 = (bf16[1,1,12,128,128]{4,3,2,1,0:T(8,128)(2,1)S(1)}, bf16[1,1,12,128,128]{4,3,2,1,0:T(8,128)(2,1)S(1)}, u32[]{:S(2)}, u32[]{:S(2)}) collective-permute-start(bf16[1,1,12,128,128]{4,3,2,1,0:T(8,128)(2,1)S(1)} %collective-permute-done.10.refs_5_), channel_id=1, source_target_pairs={{0,8},{8,0},{16,24},{24,16},{1,9},{9,1},{17,25},{25,17},{2,10},{10... | collective-permute-start | bytes 1179656 | tf_op jit(solution)/shard_map/ppermute | solution.py:69
  55.6 7.7 %collective-permute-start.24 = (f32[128,128]{1,0:T(8,128)S(1)}, f32[128,128]{1,0:T(8,128)S(1)}, u32[]{:S(2)}, u32[]{:S(2)}) collective-permute-start(f32[128,128]{1,0:T(8,128)S(1)} %add.52), channel_id=1, source_target_pairs={{0,6},{1,7},{2,4},{3,5},{4,2},{5,3},{6,0},{7,1},{8,14},{9,15},{10,... | collective-permute-start | bytes 196616 | tf_op jit(solution)/shard_map/ppermute | solution.py:69
  59.3 5.0 %collective-permute-start.23 = (f32[128,128]{1,0:T(8,128)S(1)}, f32[128,128]{1,0:T(8,128)S(1)}, u32[]{:S(2)}, u32[]{:S(2)}) collective-permute-start(f32[128,128]{1,0:T(8,128)S(1)} %add.52), channel_id=1, source_target_pairs={{0,4},{1,5},{2,6},{3,7},{4,0},{5,1},{6,2},{7,3},{8,12},{9,13},{10,... | collective-permute-start | bytes 196616 | tf_op jit(solution)/shard_map/ppermute | solution.py:69
  59.9 9.8 %collective-permute-start.29 = (f32[512,128]{1,0:T(8,128)S(1)}, f32[512,128]{1,0:T(8,128)S(1)}, u32[]{:S(2)}, u32[]{:S(2)}) collective-permute-start(f32[512,128]{1,0:T(8,128)S(1)} %get-tuple-element.95.value), channel_id=1, source_target_pairs={{0,4},{1,5},{2,6},{3,7},{4,0},{5,1},{6,2},{7,3},{8,12},{9,13},{10,... | collective-permute-start | bytes 786440 | tf_op jit(solution)/shard_map/ppermute | solution.py:69
  61.4 10.3 %collective-permute-start.27 = (f32[512,128]{1,0:T(8,128)S(1)}, f32[512,128]{1,0:T(8,128)S(1)}, u32[]{:S(2)}, u32[]{:S(2)}) collective-permute-start(f32[512,128]{1,0:T(8,128)S(1)} %get-tuple-element.95.value), channel_id=1, source_target_pairs={{0,2},{1,3},{2,0},{3,1},{4,6},{5,7},{6,4},{7,5},{8,10},{9,11},{10,... | collective-permute-start | bytes 786440 | tf_op jit(solution)/shard_map/ppermute | solution.py:69
  70.1 5.6 %collective-permute-start.31 = (bf16[512,128]{1,0:T(8,128)(2,1)S(1)}, bf16[512,128]{1,0:T(8,128)(2,1)S(1)}, u32[]{:S(2)}, u32[]{:S(2)}) collective-permute-start(bf16[512,128]{1,0:T(8,128)(2,1)S(1)} %get-tuple-element.105.refs_12_), channel_id=1, source_target_pairs={{0,2},{1,3},{2,0},{3,1},{4,6},{5,7},{6,4},{7,5},{8,10},{9,11},{10,... | collective-permute-start | bytes 393224 | tf_op jit(solution)/shard_map/ppermute | solution.py:69
  81.0 5.6 %collective-permute-start.36 = (f32[128,128]{1,0:T(8,128)S(1)}, f32[128,128]{1,0:T(8,128)S(1)}, u32[]{:S(2)}, u32[]{:S(2)}) collective-permute-start(f32[128,128]{1,0:T(8,128)S(1)} %add.56), channel_id=1, source_target_pairs={{0,6},{1,7},{2,4},{3,5},{4,2},{5,3},{6,0},{7,1},{8,14},{9,15},{10,... | collective-permute-start | bytes 196616 | tf_op jit(solution)/shard_map/ppermute | solution.py:69
  82.5 5.3 %collective-permute-start.35 = (f32[128,128]{1,0:T(8,128)S(1)}, f32[128,128]{1,0:T(8,128)S(1)}, u32[]{:S(2)}, u32[]{:S(2)}) collective-permute-start(f32[128,128]{1,0:T(8,128)S(1)} %add.56), channel_id=1, source_target_pairs={{0,4},{1,5},{2,6},{3,7},{4,0},{5,1},{6,2},{7,3},{8,12},{9,13},{10,... | collective-permute-start | bytes 196616 | tf_op jit(solution)/shard_map/ppermute | solution.py:69
  84.6 8.8 %collective-permute-start.41 = (f32[512,128]{1,0:T(8,128)S(1)}, f32[512,128]{1,0:T(8,128)S(1)}, u32[]{:S(2)}, u32[]{:S(2)}) collective-permute-start(f32[512,128]{1,0:T(8,128)S(1)} %get-tuple-element.114.value), channel_id=1, source_target_pairs={{0,4},{1,5},{2,6},{3,7},{4,0},{5,1},{6,2},{7,3},{8,12},{9,13},{10,... | collective-permute-start | bytes 786440 | tf_op jit(solution)/shard_map/ppermute | solution.py:69
  86.0 10.0 %collective-permute-start.39 = (f32[512,128]{1,0:T(8,128)S(1)}, f32[512,128]{1,0:T(8,128)S(1)}, u32[]{:S(2)}, u32[]{:S(2)}) collective-permute-start(f32[512,128]{1,0:T(8,128)S(1)} %get-tuple-element.114.value), channel_id=1, source_target_pairs={{0,2},{1,3},{2,0},{3,1},{4,6},{5,7},{6,4},{7,5},{8,10},{9,11},{10,... | collective-permute-start | bytes 786440 | tf_op jit(solution)/shard_map/ppermute | solution.py:69
  93.7 5.2 %collective-permute-start.43 = (bf16[512,128]{1,0:T(8,128)(2,1)S(1)}, bf16[512,128]{1,0:T(8,128)(2,1)S(1)}, u32[]{:S(2)}, u32[]{:S(2)}) collective-permute-start(bf16[512,128]{1,0:T(8,128)(2,1)S(1)} %shard_map.75.refs_12_), channel_id=1, source_target_pairs={{0,2},{1,3},{2,0},{3,1},{4,6},{5,7},{6,4},{7,5},{8,10},{9,11},{10,... | collective-permute-start | bytes 393224 | tf_op jit(solution)/shard_map/ppermute | solution.py:69
  104.5 5.3 %collective-permute-start.48 = (f32[128,128]{1,0:T(8,128)S(1)}, f32[128,128]{1,0:T(8,128)S(1)}, u32[]{:S(2)}, u32[]{:S(2)}) collective-permute-start(f32[128,128]{1,0:T(8,128)S(1)} %add.60), channel_id=1, source_target_pairs={{0,6},{1,7},{2,4},{3,5},{4,2},{5,3},{6,0},{7,1},{8,14},{9,15},{10,... | collective-permute-start | bytes 196616 | tf_op jit(solution)/shard_map/ppermute | solution.py:69
  (30 other events, 94.0 us)
